TPU v7x, 32 devices: a whole 2x2x4 slice. The times are simulated.
32 devices in a mesh: dp: 8 (over y, x, core), mp: 4 (over z).
Axes of the slice: x: 2, y: 2, z: 4, core: 2. Of those that a mesh axis runs over, the one named last changes fastest.
Arguments:
- tokens: bfloat16 [8, 2048, 2048], P('dp', 'mp'), may hold values from -6 to 6
- seq_lengths: int32 [8, 16], P('dp'), may hold values from 1 to 1537, 2048 in all within a row
- attn_gain: float32 [2048], replicated, may hold values from 0.5 to 1.5
- attn_shift: float32 [2048], replicated, may hold values from -3 to 3
- mlp_gain: float32 [2048], replicated, may hold values from 0.5 to 1.5
- mlp_shift: float32 [2048], replicated, may hold values from -3 to 3
- in_weight: bfloat16 [2048, 8, 768], P(None, 'mp'), may hold values from -0.125 to 0.125
- in_bias: float32 [8, 768], P('mp'), may hold values from -3 to 3
- out_weight: bfloat16 [2048, 2048], P('mp'), may hold values from -0.5 to 0.5
- out_bias: float32 [2048], replicated, may hold values from -3 to 3
- up_weight: bfloat16 [2048, 8192], P(None, 'mp'), may hold values from -0.125 to 0.125
- up_bias: float32 [8192], P('mp'), may hold values from -3 to 3
- down_weight: bfloat16 [8192, 2048], P('mp'), may hold values from -0.0625 to 0.0625
- down_bias: float32 [2048], replicated, may hold values from -3 to 3
- cotangent: bfloat16 [8, 2048, 2048], P('dp', 'mp'), may hold values from -6 to 6
Outputs:
- block_out: bfloat16 [8, 2048, 2048], P('dp', 'mp')
- tokens_grad: bfloat16 [8, 2048, 2048], P('dp', 'mp')
- grad_attn_gain: float32 [2048], replicated
- grad_attn_shift: float32 [2048], replicated
- grad_mlp_gain: float32 [2048], replicated
- grad_mlp_shift: float32 [2048], replicated
- grad_in_weight: float32 [2048, 8, 768], P(None, 'mp')
- grad_in_bias: float32 [8, 768], P('mp')
- grad_out_weight: float32 [2048, 2048], P('mp')
- grad_out_bias: float32 [2048], replicated
- grad_up_weight: float32 [2048, 8192], P(None, 'mp')
- grad_up_bias: float32 [8192], P('mp')
- grad_down_weight: float32 [8192, 2048], P('mp')
- grad_down_bias: float32 [2048], replicated
- branch_rms: float32 [2], replicated
Inputs may be any that keep to these rules, and one draw needn't show every extreme that they name: `seq_lengths`: each row's 16 lengths sum to 2048, and one of them is 1537.
All inputs are finite; a program needn't handle non-finite values.
Results may differ from a plain program's by a relative error of at most 0.012.
Values may be sent and summed in bfloat16 or wider, within the bound.
A program may use at most 384 MiB of HBM per device.

v0:
```python
import jax
import jax.numpy as jnp
from jax import lax
from jax.sharding import PartitionSpec as P

D = 2048
HD = 256
ROT = 64
LEN = 2048
QBLOCK = 512
NSEG = 16


NORM_EPS = 1e-05
NEG_FILL = -1000000000.0


def layer_norm(values, norm_gain, norm_shift):
    average = jnp.mean(values, axis=-1, keepdims=True)
    centred = values - average
    variance = jnp.mean(centred * centred, axis=-1, keepdims=True)
    return centred * lax.rsqrt(variance + NORM_EPS) * norm_gain + norm_shift


def gelu_exact(values):
    return jax.nn.gelu(values, approximate=False)


def segment_layout(row_lengths):
    seg_ends = jnp.cumsum(row_lengths)
    seg_starts = seg_ends - row_lengths
    places = jnp.arange(LEN, dtype=jnp.int32)
    segment = jnp.sum((places[:, None] >= seg_ends[None, :]).astype(jnp.int32), axis=1)
    matches = segment[:, None] == jnp.arange(NSEG, dtype=jnp.int32)[None, :]
    offset = jnp.sum(jnp.where(matches, seg_starts[None, :], 0), axis=1)
    return (segment, places - offset)


def rotary_tables(positions):
    inverse = 10000.0 ** (-jnp.arange(0, ROT, 2).astype(jnp.float32) / ROT)
    angles = positions.astype(jnp.float32)[:, None] * inverse[None, :]
    angles = jnp.concatenate([angles, angles], axis=-1)[:, None, :]
    return (jnp.cos(angles), jnp.sin(angles))


def rotate(values, cosine_table, sine_table):
    turned = values[..., :ROT]
    first_half = turned[..., : ROT // 2]
    second_half = turned[..., ROT // 2 :]
    swapped = jnp.concatenate([-second_half, first_half], axis=-1)
    return jnp.concatenate(
        [turned * cosine_table + swapped * sine_table, values[..., ROT:]], axis=-1
    )


def block_inputs(array):
    return array.reshape((LEN // QBLOCK, QBLOCK) + array.shape[1:])


def masked_scores(query_block, all_keys, block_segment, block_places, segment):
    scaling = HD ** (-0.5)
    places = jnp.arange(LEN, dtype=jnp.int32)
    scores = (
        jnp.einsum("qhc,khc->hqk", query_block, all_keys, preferred_element_type=jnp.float32)
        * scaling
    )
    allowed = (segment[None, :] == block_segment[:, None]) & (
        places[None, :] <= block_places[:, None]
    )
    return jnp.where(allowed[None], scores, NEG_FILL)


def attend_row(queries, all_keys, all_values, segment):
    places = jnp.arange(LEN, dtype=jnp.int32)

    def forward_step(carried, inputs):
        query_block, block_segment, block_places = inputs
        scores = masked_scores(query_block, all_keys, block_segment, block_places, segment)
        row_max = jnp.max(scores, axis=-1, keepdims=True)
        weights = jnp.exp(scores - row_max)
        totals = jnp.sum(weights, axis=-1, keepdims=True)
        shares = (weights / totals).astype(jnp.bfloat16)
        output = jnp.einsum("hqk,khc->qhc", shares, all_values, preferred_element_type=jnp.float32)
        return (carried, (output.astype(jnp.bfloat16), (row_max + jnp.log(totals))[..., 0]))

    unused, (outputs, log_totals) = lax.scan(
        forward_step,
        jnp.zeros((), jnp.float32),
        (block_inputs(queries), block_inputs(segment), block_inputs(places)),
    )
    return (outputs.reshape(queries.shape), log_totals)


def attend_back(queries, all_keys, all_values, heads_grad, log_totals, segment):
    scaling = HD ** (-0.5)
    places = jnp.arange(LEN, dtype=jnp.int32)

    def back_step(carried, inputs):
        key_grad, value_grad = carried
        query_block, grad_block, log_block, block_segment, block_places = inputs
        scores = masked_scores(query_block, all_keys, block_segment, block_places, segment)
        shares = jnp.exp(scores - log_block[..., None])
        value_grad = value_grad + jnp.einsum(
            "hqk,qhc->khc",
            shares.astype(jnp.bfloat16),
            grad_block,
            preferred_element_type=jnp.float32,
        )
        share_grad = jnp.einsum(
            "qhc,khc->hqk", grad_block, all_values, preferred_element_type=jnp.float32
        )
        inner_sum = jnp.sum(shares * share_grad, axis=-1, keepdims=True)
        score_grad = (shares * (share_grad - inner_sum)).astype(jnp.bfloat16)
        query_grad = (
            jnp.einsum("hqk,khc->qhc", score_grad, all_keys, preferred_element_type=jnp.float32)
            * scaling
        )
        key_grad = (
            key_grad
            + jnp.einsum(
                "hqk,qhc->khc", score_grad, query_block, preferred_element_type=jnp.float32
            )
            * scaling
        )
        return ((key_grad, value_grad), query_grad)

    zero_grad = jnp.zeros(all_keys.shape, jnp.float32)
    (key_grad, value_grad), query_grad = lax.scan(
        back_step,
        (zero_grad, zero_grad),
        (
            block_inputs(queries),
            block_inputs(heads_grad),
            log_totals,
            block_inputs(segment),
            block_inputs(places),
        ),
    )
    return (query_grad.reshape(queries.shape), key_grad, value_grad)


def per_device(
    tokens,
    seq_lengths,
    attn_gain,
    attn_shift,
    mlp_gain,
    mlp_shift,
    in_weight,
    in_bias,
    out_weight,
    out_bias,
    up_weight,
    up_bias,
    down_weight,
    down_bias,
    cotangent,
):
    row_count = tokens.shape[0]
    local_heads = in_weight.shape[1]
    tokens_wide = tokens.astype(jnp.float32)
    attn_in = layer_norm(tokens_wide, attn_gain, attn_shift).astype(jnp.bfloat16)
    mlp_in = layer_norm(tokens_wide, mlp_gain, mlp_shift).astype(jnp.bfloat16)
    attn_full, mlp_full = (
        lax.all_gather(attn_in, "mp", axis=1, tiled=True),
        lax.all_gather(mlp_in, "mp", axis=1, tiled=True),
    )
    attn_rows = attn_full.reshape(row_count * LEN, D)
    mlp_rows = mlp_full.reshape(row_count * LEN, D)
    projected = (
        jnp.einsum("td,dhc->thc", attn_rows, in_weight, preferred_element_type=jnp.float32)
        + in_bias
    )
    projected = projected.reshape(row_count, LEN, local_heads, 3 * HD)
    row_index = 0
    segment, positions = segment_layout(seq_lengths[row_index])
    cosine_table, sine_table = rotary_tables(positions)
    row_proj = projected[row_index]
    queries = rotate(row_proj[..., :HD], cosine_table, sine_table).astype(jnp.bfloat16)
    all_keys = rotate(row_proj[..., HD : 2 * HD], cosine_table, sine_table).astype(jnp.bfloat16)
    all_values = row_proj[..., 2 * HD :].astype(jnp.bfloat16)
    outputs, log_totals = attend_row(queries, all_keys, all_values, segment)
    kept_rows = [(queries, all_keys, all_values, log_totals, segment, cosine_table, sine_table)]
    head_rows = [outputs]
    heads_out = jnp.stack(head_rows).reshape(row_count * LEN, local_heads * HD)
    attn_part = jnp.dot(heads_out, out_weight, preferred_element_type=jnp.float32).reshape(
        row_count, LEN, D
    )
    up_values = jnp.dot(mlp_rows, up_weight, preferred_element_type=jnp.float32) + up_bias
    activated = gelu_exact(up_values).astype(jnp.bfloat16)
    down_part = jnp.dot(activated, down_weight, preferred_element_type=jnp.float32).reshape(
        row_count, LEN, D
    )
    attn_sum, mlp_sum = (
        lax.psum_scatter(attn_part, "mp", scatter_dimension=1, tiled=True),
        lax.psum_scatter(down_part, "mp", scatter_dimension=1, tiled=True),
    )
    attn_branch = attn_sum + out_bias
    mlp_branch = mlp_sum + down_bias
    block_out = (tokens_wide + attn_branch + mlp_branch).astype(jnp.bfloat16)
    squares = jnp.stack([jnp.sum(attn_branch * attn_branch), jnp.sum(mlp_branch * mlp_branch)])
    grad_full = lax.all_gather(cotangent, "mp", axis=1, tiled=True).reshape(row_count * LEN, D)
    grad_down_weight = jnp.dot(activated.T, grad_full, preferred_element_type=jnp.float32)
    act_grad = jnp.dot(grad_full, down_weight.T, preferred_element_type=jnp.float32)
    unused, gelu_back = jax.vjp(gelu_exact, up_values)
    up_grad = gelu_back(act_grad)[0].astype(jnp.bfloat16)
    grad_up_weight = jnp.dot(mlp_rows.T, up_grad, preferred_element_type=jnp.float32)
    grad_up_bias = jnp.sum(up_grad.astype(jnp.float32), axis=0)
    mlp_in_grad = jnp.dot(up_grad, up_weight.T, preferred_element_type=jnp.float32).reshape(
        row_count, LEN, D
    )
    grad_out_weight = jnp.dot(heads_out.T, grad_full, preferred_element_type=jnp.float32)
    heads_grad = jnp.dot(grad_full, out_weight.T, preferred_element_type=jnp.float32).astype(
        jnp.bfloat16
    )
    heads_grad = heads_grad.reshape(row_count, LEN, local_heads, HD)
    row_index = 0
    queries, all_keys, all_values, log_totals, segment, cosine_table, sine_table = kept_rows[
        row_index
    ]
    query_grad, key_grad, value_grad = attend_back(
        queries, all_keys, all_values, heads_grad[row_index], log_totals, segment
    )
    proj_rows = [
        jnp.concatenate(
            [
                rotate(query_grad, cosine_table, -sine_table),
                rotate(key_grad, cosine_table, -sine_table),
                value_grad,
            ],
            axis=-1,
        ).astype(jnp.bfloat16)
    ]
    proj_grad = jnp.stack(proj_rows).reshape(row_count * LEN, local_heads, 3 * HD)
    grad_in_weight = jnp.einsum(
        "td,thc->dhc", attn_rows, proj_grad, preferred_element_type=jnp.float32
    )
    grad_in_bias = jnp.sum(proj_grad.astype(jnp.float32), axis=0)
    attn_in_grad = jnp.einsum(
        "thc,dhc->td", proj_grad, in_weight, preferred_element_type=jnp.float32
    )
    attn_in_grad = attn_in_grad.reshape(row_count, LEN, D)
    attn_norm_grad, mlp_norm_grad = (
        lax.psum_scatter(attn_in_grad, "mp", scatter_dimension=1, tiled=True),
        lax.psum_scatter(mlp_in_grad, "mp", scatter_dimension=1, tiled=True),
    )
    unused, attn_norm_back = jax.vjp(layer_norm, tokens_wide, attn_gain, attn_shift)
    attn_token_term, attn_gain_grad, attn_shift_grad = attn_norm_back(attn_norm_grad)
    unused, mlp_norm_back = jax.vjp(layer_norm, tokens_wide, mlp_gain, mlp_shift)
    mlp_token_term, mlp_gain_grad, mlp_shift_grad = mlp_norm_back(mlp_norm_grad)
    tokens_grad = (cotangent.astype(jnp.float32) + attn_token_term + mlp_token_term).astype(
        jnp.bfloat16
    )
    bias_grad = jnp.sum(cotangent.astype(jnp.float32), axis=(0, 1))
    grad_attn_gain, grad_attn_shift, grad_mlp_gain, grad_mlp_shift, bias_total, square_sums = (
        lax.psum(
            (attn_gain_grad, attn_shift_grad, mlp_gain_grad, mlp_shift_grad, bias_grad, squares),
            ("dp", "mp"),
        )
    )
    (
        grad_in_weight,
        grad_in_bias,
        grad_out_weight,
        grad_up_weight,
        grad_up_bias,
        grad_down_weight,
    ) = lax.psum(
        (
            grad_in_weight,
            grad_in_bias,
            grad_out_weight,
            grad_up_weight,
            grad_up_bias,
            grad_down_weight,
        ),
        "dp",
    )
    element_count = float(
        lax.axis_size("dp") * lax.axis_size("mp") * row_count * tokens.shape[1] * D
    )
    branch_rms = jnp.sqrt(square_sums / element_count)
    return (
        block_out,
        tokens_grad,
        grad_attn_gain,
        grad_attn_shift,
        grad_mlp_gain,
        grad_mlp_shift,
        grad_in_weight,
        grad_in_bias,
        grad_out_weight,
        bias_total,
        grad_up_weight,
        grad_up_bias,
        grad_down_weight,
        bias_total,
        branch_rms,
    )


def solution(mesh):
    in_specs = (
        P("dp", "mp", None),
        P("dp", None),
        P(),
        P(),
        P(),
        P(),
        P(None, "mp", None),
        P("mp", None),
        P("mp", None),
        P(),
        P(None, "mp"),
        P("mp"),
        P("mp", None),
        P(),
        P("dp", "mp", None),
    )
    out_specs = (
        P("dp", "mp", None),
        P("dp", "mp", None),
        P(),
        P(),
        P(),
        P(),
        P(None, "mp", None),
        P("mp", None),
        P("mp", None),
        P(),
        P(None, "mp"),
        P("mp"),
        P("mp", None),
        P(),
        P(),
    )
    return jax.shard_map(
        per_device, mesh=mesh, in_specs=in_specs, out_specs=out_specs, check_vma=False
    )
```

profile of v0, /device:TPU:0, one launch (start us, length us, event | category | flops | bytes accessed | tf_op | source)
XLA Modules:
  0.0 2570.6 jit_solution(1546161304760454574)
XLA Ops:
  22.1 147.7 %all-gather.4.cloned.1.call-done = bf16[1,2048,2048]{2,1,0:T(8,128)(2,1)} async-done(((bf16[1,512,2048]{2,1,0:T(8,128)(2,1)}), bf16[1,2048,2048]{2,1,0:T(8,128)(2,1)}) %all-gather.4.cloned.1.call-update) | async-done | bytes 8388624 | tf_op jit(solution)/shard_map/all_gather | solution.py:165
  169.8 19.2 fusion.108
  224.1 46.6 %while.27 = (s32[]{:T(128)}, bf16[4,512,2,256]{3,2,1,0:T(2,128)(2,1)}, f32[4,2,512]{2,1,0:T(2,128)S(1)}, s32[2048]{0:T(1024)S(1)}, s32[4,512]{1,0:T(4,128)S(1)},...) while((s32[]{:T(128)}, ...), condition=%wide.region_8.9_spmd, body=%wide.region_5.0_spmd.sunk | while | flops 2176056320 | bytes 44093592 | solution.py:86
  270.8 48.5 %all-gather.8.cloned.1.call-done = bf16[1,2048,2048]{2,1,0:T(8,128)(2,1)} async-done(((bf16[1,512,2048]{2,1,0:T(8,128)(2,1)}), bf16[1,2048,2048]{2,1,0:T(8,128)(2,1)}) %all-gather.8.cloned.1.call-update) | async-done | bytes 8388624 | tf_op jit(solution)/shard_map/all_gather | solution.py:202
  332.5 215.4 %while.28 = (s32[]{:T(128)}, f32[2048,2,256]{0,2,1:T(8,128)}, f32[2048,2,256]{0,2,1:T(8,128)}, f32[4,512,2,256]{1,0,3,2:T(4,128)}, bf16[4,512,2,256]{3,1,2,0:T(8...) while((s32[]{:T(128)}, f32[2048,2,256]{0,2,1:T(8,128)}, ...), condition=%wide.region_13.14_spmd.clone, body=%wide.region_11.13_spmd.clone.sunk | while | flops 5408816128 | bytes 237027776 | solution.py:128
  364.8 21.1 dynamic_update_slice.20
  418.9 21.0 dynamic_update_slice.20
  472.9 21.0 dynamic_update_slice.20
  526.9 21.0 dynamic_update_slice.20
  626.6 59.3 %multiply_convert_fusion.1 = (bf16[2048,2048]{1,0:T(8,128)(2,1)}, f32[2048,2048]{1,0:T(8,128)}, f32[2048,2048]{1,0:T(8,128)}) fusion(f32[2048]{0:T(1024)S(1)} %copy-done.33, bf16[2048,2048]{1,0:T(8,128)(2,1)} %param.29, bf16[1,2048,2048]{2,1,0:T(8,128)(2,1)} %all-gather.6.cloned.1.call-done), kind=kOutput, calls=%fused_computation.54 | convolution fusion | flops 17456693248 | bytes 58728448 | tf_op jit(solution)/shard_map/dot_general | solution.py:189
  685.9 33.4 %convert_reduce_fusion = (f32[2048]{0:T(1024)}, bf16[2048,2048]{1,0:T(8,128)(2,1)}) fusion(f32[2048,2048]{1,0:T(8,128)} %get-tuple-element.344, bf16[2048,2048]{1,0:T(8,128)(2,1)S(1)} %copy-done.31, bf16[1,2048,2048]{2,1,0:T(8,128)(2,1)} %all-gather.8.cloned.1.call-done, f32[2048,2048]{1,0:T(8,128)} %get-tuple-element.383, f32[2048]{0:T(1024)S(1)} %copy-done.33), kind=kOutput, calls=%fused_computation.52 | convolution fusion | flops 17251170304 | bytes 58736640 | tf_op jit(solution)/shard_map/dot_general | solution.py:204
  719.3 24.5 fusion.49
  743.8 21.2 fusion.39
  765.1 24.5 convolution_bitcast_fusion
  789.6 19.7 convolution_bitcast_fusion.1
  819.8 24.2 convolution_bitcast_fusion.2
  847.9 26.9 %all-reduce.1 = (f32[2,768]{1,0:T(2,128)}, f32[2048]{0:T(1024)}) all-reduce(f32[2,768]{1,0:T(2,128)S(1)} %convert_reduce_fusion.1, f32[2048]{0:T(1024)S(1)} %copy-done.28), channel_id=1, replica_groups=mesh['dp'=8,'mp'=4] {'dp'}, use_global_device_ids=true, to_apply=%region_30.31 | all-reduce | flops 3584 | bytes 28672 | tf_op jit(solution)/shard_map/psum | solution.py:268
  874.8 471.9 %all-reduce.5.cloned.1.call-done = (f32[2048,2,768]{2,0,1:T(8,128)}, f32[512,2048]{1,0:T(8,128)}, f32[2048,2048]{1,0:T(8,128)}, f32[2048,2048]{1,0:T(8,128)}) async-done(((f32[2048,2,768]{2,0,1:T(8,128)}, f32[512,2048]{1,0:T(8,128)}, f32[2048,2048]{1,0:T(8,128)}, f32[2048,2048]{1,0:T(8,128)}), (f32[2048,2,768]{2,0,1:T(8,128)}, f32[512,2048]{1,0:T(8,128)}, f32[2048,2048]{1,0:T(8,128)}, ...) | async-done | bytes 50331664 | tf_op jit(solution)/shard_map/psum | solution.py:268
  1346.7 22.1 copy.91
  1368.7 260.5 %reduce-scatter.11.cloned.1.call-done = f32[1,512,2048]{2,1,0:T(8,128)} async-done(((f32[1,2048,2048]{2,1,0:T(8,128)}), f32[1,512,2048]{2,1,0:T(8,128)}) %reduce-scatter.11.cloned.1.call-update) | async-done | bytes 4194320 | tf_op jit(solution)/shard_map/reduce_scatter | solution.py:245
  1629.2 283.4 %reduce-scatter.9.cloned.1.call-done = f32[1,512,2048]{2,1,0:T(8,128)} async-done(((f32[1,2048,2048]{2,1,0:T(8,128)}), f32[1,512,2048]{2,1,0:T(8,128)}) %reduce-scatter.9.cloned.1.call-update) | async-done | bytes 4194320 | tf_op jit(solution)/shard_map/reduce_scatter | solution.py:244
  1923.3 273.3 %reduce-scatter.5.cloned.1.call-done = f32[1,512,2048]{2,1,0:T(8,128)} async-done(((f32[1,2048,2048]{2,1,0:T(8,128)}), f32[1,512,2048]{2,1,0:T(8,128)}) %reduce-scatter.5.cloned.1.call-update) | async-done | bytes 4194320 | tf_op jit(solution)/shard_map/reduce_scatter | solution.py:195
  2196.6 284.1 %reduce-scatter.7.cloned.1.call-done = f32[1,512,2048]{2,1,0:T(8,128)} async-done(((f32[1,2048,2048]{2,1,0:T(8,128)}), f32[1,512,2048]{2,1,0:T(8,128)}) %reduce-scatter.7.cloned.1.call-update) | async-done | bytes 4194320 | tf_op jit(solution)/shard_map/reduce_scatter | solution.py:196
  2493.7 42.2 %all-reduce = (f32[2048]{0:T(1024)}, f32[2048]{0:T(1024)}, f32[2048]{0:T(1024)}, f32[2048]{0:T(1024)}, f32[2048]{0:T(1024)S(1)}, /*index=5*/f32[2]{0:T(128)S(1)}) all-reduce(f32[2048]{0:T(1024)S(1)} %get-tuple-element.288, f32[2048]{0:T(1024)S(1)} %get-tuple-element.285, ...), channel_id=1, replica_groups=mesh['dp'=8,'mp'=4] {'dp','mp'}, use_global_device_ids=true, to_apply=%region_21.22 | all-reduce | flops 10242 | bytes 81936 | tf_op jit(solution)/shard_map/psum | solution.py:256
  (294 shorter events, 383.8 us)
Async XLA Ops:
  7.2 312.1 %copy-start = (bf16[512,2048]{1,0:T(8,128)(2,1)S(1)}, bf16[512,2048]{1,0:T(8,128)(2,1)}, u32[]{:S(2)}) copy-start(bf16[512,2048]{1,0:T(8,128)(2,1)} %param.27) | copy-start | bytes 6291460
  7.2 162.6 %all-gather.4.cloned.1.call-start = ((), (), s32[]{:S(2)}) async-start(), calls=%async_computation.4 | async-start | bytes 10485760 | tf_op jit(solution)/shard_map/all_gather | solution.py:165
  12.2 157.6 %copy-start.34 = (f32[2,768]{1,0:T(2,128)S(1)}, f32[2,768]{1,0:T(2,128)}, u32[]{:S(2)}) copy-start(f32[2,768]{1,0:T(2,128)} %param.26) | copy-start | bytes 18436
  17.3 302.0 %all-gather.8.cloned.1.call-start = ((), (), s32[]{:S(2)}) async-start(), calls=%async_computation.8 | async-start | bytes 10485760 | tf_op jit(solution)/shard_map/all_gather | solution.py:202
  18.1 608.5 %all-gather.6.cloned.1.call-start = ((), (), s32[]{:S(2)}) async-start(), calls=%async_computation.6 | async-start | bytes 10485760 | tf_op jit(solution)/shard_map/all_gather | solution.py:166
  18.8 1327.9 %all-reduce.5.cloned.1.call-start = ((), (), s32[]{:S(2)}) async-start(), calls=%async_computation.11 | async-start | bytes 100663296 | tf_op jit(solution)/shard_map/psum | solution.py:268
  22.1 180.2 %copy-start.11 = (f32[2048,64]{0,1:T(8,128)}, f32[2048,64]{0,1:T(8,128)S(1)}, u32[]{:S(2)}) copy-start(f32[2048,64]{0,1:T(8,128)S(1)} %get-tuple-element.378) | copy-start | bytes 1572868
  609.4 17.1 copy-start.33
  626.6 59.3 %copy-start.31 = (bf16[2048,2048]{1,0:T(8,128)(2,1)S(1)}, bf16[2048,2048]{1,0:T(8,128)(2,1)}, u32[]{:S(2)}) copy-start(bf16[2048,2048]{1,0:T(8,128)(2,1)} %param.31) | copy-start | bytes 25165828
  719.3 24.5 copy-start.32
  719.3 24.5 copy-start.35
  765.0 864.2 %reduce-scatter.11.cloned.1.call-start = ((), (), s32[]{:S(2)}) async-start(), calls=%async_computation.10 | async-start | bytes 20971520 | tf_op jit(solution)/shard_map/reduce_scatter | solution.py:245
  789.6 1123.0 %reduce-scatter.9.cloned.1.call-start = ((), (), s32[]{:S(2)}) async-start(), calls=%async_computation.9 | async-start | bytes 20971520 | tf_op jit(solution)/shard_map/reduce_scatter | solution.py:244
  809.3 1387.3 %reduce-scatter.5.cloned.1.call-start = ((), (), s32[]{:S(2)}) async-start(), calls=%async_computation.5 | async-start | bytes 20971520 | tf_op jit(solution)/shard_map/reduce_scatter | solution.py:195
  819.7 1661.0 %reduce-scatter.7.cloned.1.call-start = ((), (), s32[]{:S(2)}) async-start(), calls=%async_computation.7 | async-start | bytes 20971520 | tf_op jit(solution)/shard_map/reduce_scatter | solution.py:196
  1346.7 565.9 %copy-start.18 = (f32[2048]{0:T(1024)S(1)}, f32[2048]{0:T(1024)}, u32[]{:S(2)}) copy-start(f32[2048]{0:T(1024)} %param.21) | copy-start | bytes 24580
  1346.7 565.9 %copy-start.19 = (f32[2048]{0:T(1024)S(1)}, f32[2048]{0:T(1024)}, u32[]{:S(2)}) copy-start(f32[2048]{0:T(1024)} %param.23) | copy-start | bytes 24580
  1346.7 565.9 %copy-start.21 = (f32[512]{0:T(512)S(1)}, f32[512]{0:T(512)}, u32[]{:S(2)}) copy-start(f32[512]{0:T(512)} %copy-done.20) | copy-start | bytes 6148
  1368.7 549.0 %copy-start.25 = (f32[512]{0:T(512)S(1)}, f32[512]{0:T(512)}, u32[]{:S(2)}) copy-start(f32[512]{0:T(512)} %copy-done.24) | copy-start | bytes 6148
  1368.7 549.1 %copy-start.23 = (f32[512]{0:T(512)S(1)}, f32[512]{0:T(512)}, u32[]{:S(2)}) copy-start(f32[512]{0:T(512)} %copy-done.22) | copy-start | bytes 6148
  1917.7 563.0 %copy-start.26 = (f32[2048]{0:T(1024)S(1)}, f32[2048]{0:T(1024)}, u32[]{:S(2)}) copy-start(f32[2048]{0:T(1024)} %param.28) | copy-start | bytes 24580
  1917.8 563.0 %copy-start.27 = (f32[2048]{0:T(1024)S(1)}, f32[2048]{0:T(1024)}, u32[]{:S(2)}) copy-start(f32[2048]{0:T(1024)} %param.32) | copy-start | bytes 24580
  2535.9 19.5 copy-start.29
  2537.0 18.4 slice-start
  (54 other events, 330.7 us)
Sparse Core Ops, SparseCore 0:
  17.4 152.3 all-gather.3
  171.4 147.8 all-gather.7
  320.9 147.8 all-gather.5
  765.1 581.4 all-reduce.4
  1348.9 280.2 reduce-scatter.10
  1631.5 281.0 reduce-scatter.8
  1915.5 281.0 reduce-scatter.4
  2199.7 281.0 reduce-scatter.6
where the time goes:
time: 2580 us; the launch traced here: 2570 us
  waiting for transfers between devices  1770 us (69%)
  matrix products  378 us (15%)
  local copies, waits for them, and re-layouts  246 us (10%)
  other arithmetic  90.1 us (3%)
  blocking collectives  69.1 us (3%)
    psum x1, waiting for transfers between devices, per_device(): lax.psum((grad_in_weight, grad_in_bias, grad_out_weight, grad_up_weight,...  472 us
    reduce_scatter x1, waiting for transfers between devices, per_device(): lax.psum_scatter(down_part, 'mp', scatter_dimension=1, tiled=True)  284 us
    reduce_scatter x1, waiting for transfers between devices, per_device(): lax.psum_scatter(attn_in_grad, 'mp', scatter_dimension=1, tiled=True)  283 us
    reduce_scatter x1, waiting for transfers between devices, per_device(): lax.psum_scatter(attn_part, 'mp', scatter_dimension=1, tiled=True)  273 us
    reduce_scatter x1, waiting for transfers between devices, per_device(): lax.psum_scatter(mlp_in_grad, 'mp', scatter_dimension=1, tiled=True)  260 us
    all_gather x1, waiting for transfers between devices, per_device(): lax.all_gather(attn_in, 'mp', axis=1, tiled=True)  148 us
    dynamic_update_slice x8, local copies, waits for them, and re-layouts, attend_back(): lax.scan(back_step, (zero_grad, zero_grad), (block_inputs(queries), block...  93.7 us
    dot_general x1, matrix products, per_device(): jnp.dot(mlp_rows, up_weight, preferred_element_type=jnp.float32) + up_bias  59.3 us
  transfers between devices with their start and end apart: 8, of which 7 were waited for; matrix products, arithmetic and copies ran while one was open for 20% of the time, Pallas kernels for 0%

commit v1 on v0

v1 whole, which is shorter than its diff:
```python
import functools

import jax
import jax.numpy as jnp
import numpy as np
from jax import lax
from jax.experimental import pallas as pl
from jax.experimental.pallas import tpu as pltpu
from jax.sharding import PartitionSpec as P

HD = 256
ROT = 64
KBLOCK = 256
NORM_EPS = 1e-05
NEG_FILL = -1000000000.0
VMEM_LIMIT = 56 * 1024 * 1024
BF16 = jnp.bfloat16
F32 = jnp.float32

NT = (((1,), (1,)), ((), ()))
NN = (((1,), (0,)), ((), ()))
TN = (((0,), (0,)), ((), ()))


def dot(a, b, dims=NN):
    return lax.dot_general(a, b, dims, preferred_element_type=F32)


def params():
    return pltpu.CompilerParams(vmem_limit_bytes=VMEM_LIMIT)


def turn(part, cosine, sine):
    lane = lax.broadcasted_iota(jnp.int32, part.shape, 1)
    swapped = jnp.where(
        lane < ROT // 2,
        pltpu.roll(part, 128 - ROT // 2, 1),
        pltpu.roll(part, ROT // 2, 1),
    )
    return part * cosine + swapped * sine


def qkv_kernel(x_ref, w_ref, b_ref, cos_ref, sin_ref, *refs):
    out_ref = refs[-1]
    kind = lax.rem(pl.program_id(0), 3)
    acc = dot(x_ref[...], w_ref[...]) + b_ref[...]

    @pl.when(kind < 2)
    def _():
        scale = jnp.where(kind == 0, HD**-0.5, 1.0)
        out_ref[:, :128] = (turn(acc[:, :128], cos_ref[...], sin_ref[...]) * scale).astype(BF16)
        out_ref[:, 128:] = (acc[:, 128:] * scale).astype(BF16)

    @pl.when(kind == 2)
    def _():
        out_ref[...] = acc.astype(BF16)


def qkv_slot(slot, rows, x, weight, bias, cosine, sine, buffer):
    t, d = x.shape
    width = weight.shape[1]
    in_specs = [
        pl.BlockSpec((t, d), lambda j: (0, 0)),
        pl.BlockSpec((d, HD), lambda j: (0, j)),
        pl.BlockSpec((1, HD), lambda j: (0, j)),
        pl.BlockSpec((t, 128), lambda j: (slot, 0)),
        pl.BlockSpec((t, 128), lambda j: (slot, 0)),
    ]
    args = [x, weight, bias, cosine, sine]
    aliases = {}
    if buffer is not None:
        in_specs.append(pl.BlockSpec(memory_space=pl.ANY))
        args.append(buffer)
        aliases = {5: 0}
    return pl.pallas_call(
        qkv_kernel,
        grid=(width // HD,),
        in_specs=in_specs,
        out_specs=pl.BlockSpec((t, HD), lambda j: (slot, j)),
        out_shape=jax.ShapeDtypeStruct((rows, width), BF16),
        input_output_aliases=aliases,
        compiler_params=params(),
        cost_estimate=pl.CostEstimate(
            flops=2 * t * d * width, bytes_accessed=2 * (t * d + d * width + t * width), transcendentals=0
        ),
        name="qkv",
    )(*args)


def up_kernel(x_ref, w_ref, b_ref, *refs):
    act_ref, slope_ref = refs[-2:]
    u = dot(x_ref[...], w_ref[...]) + b_ref[...]
    below = 0.5 + 0.5 * lax.erf(u * (0.5**0.5))
    act_ref[...] = (u * below).astype(BF16)
    density = jnp.exp(u * u * -0.5) * ((2.0 * np.pi) ** -0.5)
    slope_ref[...] = (below + u * density).astype(BF16)


def up_slot(slot, rows, x, weight, bias, buffers):
    t, d = x.shape
    width = weight.shape[1]
    tile = 512
    in_specs = [
        pl.BlockSpec((t, d), lambda j: (0, 0)),
        pl.BlockSpec((d, tile), lambda j: (0, j)),
        pl.BlockSpec((1, tile), lambda j: (0, j)),
    ]
    args = [x, weight, bias]
    aliases = {}
    if buffers is not None:
        in_specs += [pl.BlockSpec(memory_space=pl.ANY)] * 2
        args += list(buffers)
        aliases = {3: 0, 4: 1}
    return pl.pallas_call(
        up_kernel,
        grid=(width // tile,),
        in_specs=in_specs,
        out_specs=[pl.BlockSpec((t, tile), lambda j: (slot, j))] * 2,
        out_shape=[jax.ShapeDtypeStruct((rows, width), BF16)] * 2,
        input_output_aliases=aliases,
        compiler_params=params(),
        cost_estimate=pl.CostEstimate(
            flops=2 * t * d * width,
            bytes_accessed=2 * (t * d + d * width + 2 * t * width),
            transcendentals=2 * t * width,
        ),
        name="up",
    )(*args)


def key_row(slot_ref, j, t):
    per = t // KBLOCK
    return pl.multiple_of(slot_ref[j // per] * t + lax.rem(j, per) * KBLOCK, KBLOCK)


def allowed(j, i, t, start):
    key = j * KBLOCK + lax.broadcasted_iota(jnp.int32, (KBLOCK, t), 0)
    query = i * t + lax.broadcasted_iota(jnp.int32, (1, t), 1)
    return (key >= start) & (key <= query)


def attend_kernel(t, heads, slot_ref, low_ref, qkv_ref, start_ref, out_ref, log_ref, vt_ref, acc_ref):
    blocks = qkv_ref.shape[0] // t
    per = t // KBLOCK

    for h in range(heads):
        for c in range(blocks):
            rows = pl.ds(c * t, t)
            vt_ref[h, :, rows] = qkv_ref[rows, (3 * h + 2) * HD : (3 * h + 3) * HD].T

    def query_block(i, unused):
        row = pl.multiple_of(slot_ref[i] * t, t)
        where = pl.ds(pl.multiple_of(i * t, t), t)
        start = start_ref[:, where]
        acc_ref[...] = jnp.zeros_like(acc_ref)

        def key_block(j, carried):
            place = key_row(slot_ref, j, t)
            mask = allowed(j, i, t, start)
            new = []
            for h in range(heads):
                top, total = carried[h]
                query = qkv_ref[pl.ds(row, t), 3 * h * HD : (3 * h + 1) * HD]
                key = qkv_ref[pl.ds(place, KBLOCK), (3 * h + 1) * HD : (3 * h + 2) * HD]
                s = jnp.where(mask, dot(key, query, NT), NEG_FILL)
                higher = jnp.maximum(top, jnp.max(s, axis=0, keepdims=True))
                p = jnp.exp(s - higher)
                shrink = jnp.exp(top - higher)
                total = total * shrink + jnp.sum(p, axis=0, keepdims=True)
                vt = vt_ref[h, :, pl.ds(place, KBLOCK)]
                acc_ref[h] = acc_ref[h] * shrink + dot(vt, p.astype(BF16))
                new.append((higher, total))
            return tuple(new)

        first = (jnp.full((1, t), 2 * NEG_FILL, F32), jnp.zeros((1, t), F32))
        carried = lax.fori_loop(low_ref[i], (i + 1) * per, key_block, (first,) * heads)
        for h in range(heads):
            top, total = carried[h]
            log_ref[h : h + 1, where] = top + jnp.log(total)
            out_ref[pl.ds(row, t), h * HD : (h + 1) * HD] = (acc_ref[h] / total).T.astype(BF16)
        return unused

    lax.fori_loop(0, blocks, query_block, 0)


def attend(t, slot_of, low, qkv, start):
    rows, width = qkv.shape
    heads = width // (3 * HD)
    return pl.pallas_call(
        functools.partial(attend_kernel, t, heads),
        in_specs=[pl.BlockSpec(memory_space=pltpu.SMEM)] * 2 + [pl.BlockSpec(memory_space=pltpu.VMEM)] * 2,
        out_specs=[pl.BlockSpec(memory_space=pltpu.VMEM)] * 2,
        out_shape=[
            jax.ShapeDtypeStruct((rows, heads * HD), BF16),
            jax.ShapeDtypeStruct((heads, rows), F32),
        ],
        scratch_shapes=[pltpu.VMEM((heads, HD, rows), BF16), pltpu.VMEM((heads, HD, t), F32)],
        compiler_params=params(),
        cost_estimate=pl.CostEstimate(
            flops=2 * rows * rows * HD * heads,
            bytes_accessed=2 * rows * width,
            transcendentals=rows * rows * heads // 2,
        ),
        name="attend",
    )(slot_of, low, qkv, start)


def attend_back_kernel(
    t, heads, slot_ref, high_ref, qkv_ref, grad_ref, out_ref, log_ref, start_ref, cos_ref, sin_ref,
    proj_ref, query_grad, delta, key_grad, value_grad,
):
    rows = qkv_ref.shape[0]
    blocks = rows // t
    per = t // KBLOCK
    query_grad[...] = jnp.zeros_like(query_grad)

    def prepare(i, unused):
        row = pl.multiple_of(slot_ref[i] * t, t)
        for h in range(heads):
            cols = slice(h * HD, (h + 1) * HD)
            both = grad_ref[pl.ds(row, t), cols].astype(F32) * out_ref[pl.ds(row, t), cols].astype(F32)
            delta[h : h + 1, pl.ds(pl.multiple_of(i * t, t), t)] = jnp.sum(both.T, axis=0, keepdims=True)
        return unused

    lax.fori_loop(0, blocks, prepare, 0)

    def turned_back(grad, place, count):
        cosine, sine = cos_ref[pl.ds(place, count), :], sin_ref[pl.ds(place, count), :]
        return turn(grad[:, :128], cosine, -sine)

    def key_block(j, unused):
        place = key_row(slot_ref, j, t)
        key_grad[...] = jnp.zeros_like(key_grad)
        value_grad[...] = jnp.zeros_like(value_grad)

        def query_block(i, unused):
            row = pl.multiple_of(slot_ref[i] * t, t)
            where = pl.ds(pl.multiple_of(i * t, t), t)
            mask = allowed(j, i, t, start_ref[:, where])
            for h in range(heads):
                query = qkv_ref[pl.ds(row, t), 3 * h * HD : (3 * h + 1) * HD]
                key = qkv_ref[pl.ds(place, KBLOCK), (3 * h + 1) * HD : (3 * h + 2) * HD]
                value = qkv_ref[pl.ds(place, KBLOCK), (3 * h + 2) * HD : (3 * h + 3) * HD]
                grad = grad_ref[pl.ds(row, t), h * HD : (h + 1) * HD]
                s = dot(key, query, NT) - log_ref[h : h + 1, where]
                p = jnp.exp(jnp.where(mask, s, NEG_FILL))
                p_grad = dot(value, grad, NT)
                value_grad[h] += dot(p.astype(BF16), grad)
                s_grad = (p * (p_grad - delta[h : h + 1, where])).astype(BF16)
                key_grad[h] += dot(s_grad, query)
                query_grad[pl.ds(row, t), h * HD : (h + 1) * HD] += dot(s_grad, key, TN)
            return unused

        lax.fori_loop(j // per, high_ref[j], query_block, 0)
        for h in range(heads):
            base = 3 * h * HD
            grad = key_grad[h]
            proj_ref[pl.ds(place, KBLOCK), base + HD : base + HD + 128] = turned_back(grad, place, KBLOCK).astype(BF16)
            proj_ref[pl.ds(place, KBLOCK), base + HD + 128 : base + 2 * HD] = grad[:, 128:].astype(BF16)
            proj_ref[pl.ds(place, KBLOCK), base + 2 * HD : base + 3 * HD] = value_grad[h].astype(BF16)
        return unused

    lax.fori_loop(0, rows // KBLOCK, key_block, 0)

    def finish(c, unused):
        place = pl.multiple_of(c * t, t)
        for h in range(heads):
            base = 3 * h * HD
            grad = query_grad[pl.ds(place, t), h * HD : (h + 1) * HD] * HD**-0.5
            proj_ref[pl.ds(place, t), base : base + 128] = turned_back(grad, place, t).astype(BF16)
            proj_ref[pl.ds(place, t), base + 128 : base + HD] = grad[:, 128:].astype(BF16)
        return unused

    lax.fori_loop(0, blocks, finish, 0)


def attend_back(t, slot_of, high, qkv, heads_grad, heads_out, logs, start, cosine, sine):
    rows, width = qkv.shape
    heads = width // (3 * HD)
    return pl.pallas_call(
        functools.partial(attend_back_kernel, t, heads),
        in_specs=[pl.BlockSpec(memory_space=pltpu.SMEM)] * 2 + [pl.BlockSpec(memory_space=pltpu.VMEM)] * 7,
        out_specs=pl.BlockSpec(memory_space=pltpu.VMEM),
        out_shape=jax.ShapeDtypeStruct((rows, width), BF16),
        scratch_shapes=[
            pltpu.VMEM((rows, heads * HD), F32),
            pltpu.VMEM((heads, rows), F32),
            pltpu.VMEM((heads, KBLOCK, HD), F32),
            pltpu.VMEM((heads, KBLOCK, HD), F32),
        ],
        compiler_params=params(),
        cost_estimate=pl.CostEstimate(
            flops=5 * rows * rows * HD * heads,
            bytes_accessed=4 * rows * width,
            transcendentals=rows * rows * heads // 2,
        ),
        name="attend_back",
    )(slot_of, high, qkv, heads_grad, heads_out, logs, start, cosine, sine)


def arrival_order(n):
    return [sorted(range(n), key=lambda p, z=z: (abs(p - z), p)) for z in range(n)]


def gather_slots(own, z, n):
    right = left = own
    came = {}
    for k in range(1, n):
        right = lax.ppermute(right, "mp", [(i, i + 1) for i in range(k - 1, n - 1)])
        left = lax.ppermute(left, "mp", [(i, i - 1) for i in range(1, n - k + 1)])
        came[k], came[-k] = right, left
    order = arrival_order(n)
    slots = [own]
    for s in range(1, n):
        chosen = came[n - 1 - order[n - 1][s]]
        for at in range(n - 1):
            source = came[at - order[at][s]]
            if at == 0 or source is not chosen:
                chosen = jnp.where(z == at, source, chosen)
        slots.append(chosen)
    return slots


def scatter_sum(part, own, z, n):
    right = left = None
    for k in range(n - 1, 0, -1):
        for_right, for_left = part(z + k), part(z - k)
        if right is not None:
            for_right = (for_right.astype(F32) + right.astype(F32)).astype(BF16)
            for_left = (for_left.astype(F32) + left.astype(F32)).astype(BF16)
        right = lax.ppermute(for_right, "mp", [(i, i + 1) for i in range(n - k)])
        left = lax.ppermute(for_left, "mp", [(i, i - 1) for i in range(k, n)])
    return own + right.astype(F32) + left.astype(F32)


def exchange(part, own, z, n):
    came = [None] * (2 * n - 1)
    came[n - 1] = own
    for k in range(1, n):
        came[n - 1 - k] = lax.ppermute(part(z + k), "mp", [(i, i + k) for i in range(n - k)])
        came[n - 1 + k] = lax.ppermute(part(z - k), "mp", [(i, i - k) for i in range(k, n)])
    return lax.dynamic_slice_in_dim(jnp.stack(came), n - 1 - z, n, axis=0)


def sum_over_dp(part):
    return lax.psum(part, "dp")


def document_starts(row_lengths, length):
    count = row_lengths.shape[0]
    before = np.tri(count, k=-1, dtype=np.int32)
    starts = jnp.sum(before * row_lengths[None, :], axis=1)
    places = jnp.arange(length, dtype=jnp.int32)
    return jnp.max(jnp.where(starts[None, :] <= places[:, None], starts[None, :], 0), axis=1)


def per_device(
    tokens, seq_lengths, attn_gain, attn_shift, mlp_gain, mlp_shift, in_weight, in_bias, out_weight, out_bias,
    up_weight, up_bias, down_weight, down_bias, cotangent,
):
    n, groups = lax.axis_size("mp"), lax.axis_size("dp")
    z, group = lax.axis_index("mp"), lax.axis_index("dp")
    t, d = tokens.shape[1:]
    length = n * t
    local_heads = in_weight.shape[1]
    in_width, hidden = local_heads * 3 * HD, up_weight.shape[1]
    order = np.array(arrival_order(n), np.int32)
    slot_table = np.argsort(order, axis=1).astype(np.int32)
    slot_of = jnp.asarray(slot_table)[z]
    position_of = jnp.asarray(order)[z]

    own_tokens = tokens[0].astype(F32)
    centred = own_tokens - jnp.mean(own_tokens, axis=-1, keepdims=True)
    spread = lax.rsqrt(jnp.mean(centred * centred, axis=-1, keepdims=True) + NORM_EPS)
    normed = centred * spread
    own_grad = cotangent[0]
    x_slots = gather_slots(normed.astype(BF16), z, n)

    flat_in = in_weight.reshape(d, in_width)
    in_scaled = (flat_in.astype(F32) * attn_gain[:, None]).astype(BF16)
    up_scaled = (up_weight.astype(F32) * mlp_gain[:, None]).astype(BF16)
    in_offset = jnp.sum(flat_in.astype(F32) * attn_shift[:, None], axis=0) + in_bias.reshape(in_width)
    up_offset = jnp.sum(up_weight.astype(F32) * mlp_shift[:, None], axis=0) + up_bias
    share = out_weight.shape[0] // groups
    out_full = lax.all_gather(
        lax.dynamic_slice_in_dim(out_weight, group * share, share, axis=0), ("mp", "dp"), axis=0, tiled=True
    )

    starts = document_starts(seq_lengths[0], length)
    first_of_block = starts[:: t]
    low = first_of_block // KBLOCK
    last_key = (jnp.arange(length // KBLOCK, dtype=jnp.int32) + 1) * KBLOCK - 1
    high = jnp.sum((first_of_block[None, :] <= last_key[:, None]).astype(jnp.int32), axis=1)
    places = jnp.arange(length, dtype=jnp.int32).reshape(n, t)
    offsets = (places - starts.reshape(n, t))[position_of].reshape(length)
    inverse = 10000.0 ** (-jnp.arange(0, ROT, 2).astype(F32) / ROT)
    angles = offsets.astype(F32)[:, None] * inverse[None, :]
    cosine, sine = jnp.cos(angles), jnp.sin(angles)
    cosine = jnp.concatenate([cosine, cosine, jnp.ones((length, 128 - ROT), F32)], axis=1)
    sine = jnp.concatenate([-sine, sine, jnp.zeros((length, 128 - ROT), F32)], axis=1)
    start_row = starts[None, :]

    qkv = hidden_pair = None
    for s, x in enumerate(x_slots):
        qkv = qkv_slot(s, length, x, in_scaled, in_offset[None, :], cosine, sine, qkv)
        hidden_pair = up_slot(s, length, x, up_scaled, up_offset[None, :], hidden_pair)
    activated, slope = hidden_pair
    x_rows = jnp.concatenate(x_slots, axis=0)
    own_grad, unused = lax.optimization_barrier((own_grad, x_slots[-1]))
    g_slots = gather_slots(own_grad, z, n)
    heads_out, logs = attend(t, slot_of, low, qkv, start_row)

    def rows_for(array):
        def part(position):
            slot = slot_of[jnp.clip(position, 0, n - 1)]
            return lax.dynamic_slice_in_dim(array, slot * t, t, axis=0)

        return part

    heads_mine = exchange(rows_for(heads_out), heads_out[:t], z, n)
    heads_mine = heads_mine.transpose(1, 0, 2).reshape(t, n * local_heads * HD)
    attn_branch = dot(heads_mine, out_full) + out_bias
    down_part = dot(activated, down_weight).astype(BF16)
    mlp_branch = scatter_sum(rows_for(down_part), dot(activated[:t], down_weight), z, n) + down_bias
    block_out = (own_tokens + attn_branch + mlp_branch).astype(BF16)
    squares = jnp.stack([jnp.sum(attn_branch * attn_branch), jnp.sum(mlp_branch * mlp_branch)])

    g_rows = jnp.concatenate(g_slots, axis=0)
    heads_grad = dot(g_rows, out_weight, NT).astype(BF16)
    up_grad = (dot(g_rows, down_weight, NT) * slope.astype(F32)).astype(BF16)
    proj_grad = attend_back(t, slot_of, high, qkv, heads_grad, heads_out, logs, start_row, cosine, sine)
    norm_part = dot(up_grad, up_scaled, NT) + dot(proj_grad, in_scaled, NT)
    norm_grad = scatter_sum(rows_for(norm_part.astype(BF16)), norm_part[:t], z, n)
    mean_grad = jnp.mean(norm_grad, axis=-1, keepdims=True)
    mean_normed = jnp.mean(norm_grad * normed, axis=-1, keepdims=True)
    tokens_grad = (own_grad.astype(F32) + spread * (norm_grad - mean_grad - normed * mean_normed)).astype(BF16)

    down_grad = dot(activated, g_rows, TN).astype(BF16)
    out_grad = dot(heads_out, g_rows, TN).astype(BF16)
    up_cross = dot(x_rows, up_grad, TN).astype(BF16)
    in_cross = dot(x_rows, proj_grad, TN).astype(BF16)
    up_total = jnp.sum(up_grad.astype(F32), axis=0)
    in_total = jnp.sum(proj_grad.astype(F32), axis=0)
    wide_in, wide_up = flat_in.astype(F32), up_weight.astype(F32)
    small = (
        jnp.sum(in_cross.astype(F32) * wide_in, axis=1),
        jnp.sum(wide_in * in_total[None, :], axis=1),
        jnp.sum(up_cross.astype(F32) * wide_up, axis=1),
        jnp.sum(wide_up * up_total[None, :], axis=1),
        jnp.sum(own_grad.astype(F32), axis=0),
        squares,
    )
    grad_attn_gain, grad_attn_shift, grad_mlp_gain, grad_mlp_shift, bias_total, square_sums = lax.psum(
        small, ("dp", "mp")
    )
    in_total, up_total = lax.psum((in_total, up_total), "dp")
    down_grad, out_grad, up_cross, in_cross = (sum_over_dp(a) for a in (down_grad, out_grad, up_cross, in_cross))
    grad_in_weight = in_cross.astype(F32) * attn_gain[:, None] + attn_shift[:, None] * in_total[None, :]
    grad_up_weight = up_cross.astype(F32) * mlp_gain[:, None] + mlp_shift[:, None] * up_total[None, :]
    element_count = float(groups * n * t * d)
    return (
        block_out[None],
        tokens_grad[None],
        grad_attn_gain,
        grad_attn_shift,
        grad_mlp_gain,
        grad_mlp_shift,
        grad_in_weight.reshape(d, local_heads, 3 * HD),
        in_total.reshape(local_heads, 3 * HD),
        out_grad.astype(F32),
        bias_total,
        grad_up_weight,
        up_total,
        down_grad.astype(F32),
        bias_total,
        jnp.sqrt(square_sums / element_count),
    )


def solution(mesh):
    rows, weights = P("dp", "mp", None), P(None, "mp", None)
    in_specs = (
        rows, P("dp", None), P(), P(), P(), P(), weights, P("mp", None), P("mp", None), P(),
        P(None, "mp"), P("mp"), P("mp", None), P(), rows,
    )
    out_specs = (
        rows, rows, P(), P(), P(), P(), weights, P("mp", None), P("mp", None), P(),
        P(None, "mp"), P("mp"), P("mp", None), P(), P(),
    )
    return jax.shard_map(per_device, mesh=mesh, in_specs=in_specs, out_specs=out_specs, check_vma=False)
```

time: 2580 us -> 1070 us (0.41)
  waiting for transfers between devices: 1770 us -> 250 us
  local copies, waits for them, and re-layouts: 246 us -> 44.6 us
  matrix products: 378 us -> 217 us
  Pallas kernels: 0 us -> 137 us
  other arithmetic: 90.1 us -> 225 us
  starting transfers between devices: 0.32 us -> 84.5 us
    reduce_scatter x4 -> x0, waiting for transfers between devices: 1100 us -> none  [the longest x1 284 us: per_device(): lax.psum_scatter(down_part, 'mp', scatter_dimension=1, tiled=True)]
    psum x1, waiting for transfers between devices: 472 us -> 0.01 us  [sum_over_dp(): return lax.psum(part, 'dp')]
    ppermute x0 -> x30, waiting for transfers between devices: none -> 250 us  [the longest x6 128 us: gather_slots(): left = lax.ppermute(left, 'mp', [(i, i - 1) for i in range(1, n - k + 1)])]
    all_gather x3 -> x1, waiting for transfers between devices: 196 us -> 0.02 us  [per_device(): lax.all_gather(lax.dynamic_slice_in_dim(out_weight, group * share, share,...]
    dot_general x40 -> x11, matrix products: 378 us -> 217 us  [dot(): return lax.dot_general(a, b, dims, preferred_element_type=F32)]
    pallas_call x0 -> x10, Pallas kernels: none -> 137 us  [the longest x4 40.5 us: up_slot(): pl.pallas_call(up_kernel, grid=(width // tile,), in_specs=in_specs, out_s...]
    dynamic_update_slice x12 -> x0, local copies, waits for them, and re-layouts: 99.1 us -> none  [the longest x8 93.7 us: attend_back(): lax.scan(back_step, (zero_grad, zero_grad), (block_inputs(queries), block...]
    reduce_sum x12 -> x9, other arithmetic: 38.8 us -> 124 us  [the longest x1 92.4 us: per_device(): jnp.sum(wide_in * in_total[None, :], axis=1)]
  transfers between devices with their start and end apart: 8 -> 32, of which waited for: 7 -> 6; matrix products, arithmetic and copies ran while one was open for 20% -> 40% of each run, Pallas kernels for 0% -> 13%
where the time goes in v1:
time: 1070 us
  waiting for transfers between devices  250 us (23%)
  other arithmetic  225 us (21%)
  matrix products  217 us (20%)
  Pallas kernels  137 us (13%)
  blocking collectives  88.9 us (8%)
  starting transfers between devices  84.5 us (8%)
  local copies, waits for them, and re-layouts  44.6 us (4%)
  between operations  20.4 us (2%)
    dot_general x11, matrix products, dot(): return lax.dot_general(a, b, dims, preferred_element_type=F32)  217 us
    ppermute x6, waiting for transfers between devices, gather_slots(): left = lax.ppermute(left, 'mp', [(i, i - 1) for i in range(1, n - k + 1)])  128 us
    reduce_sum x1, other arithmetic, per_device(): jnp.sum(wide_in * in_total[None, :], axis=1)  92.4 us
    ppermute x3, waiting for transfers between devices, exchange(): lax.ppermute(part(z - k), 'mp', [(i, i - k) for i in range(k, n)])  71.3 us
    psum x1, blocking collectives, per_device(): lax.psum(small, ('dp', 'mp'))  64.6 us
    ppermute x3, waiting for transfers between devices, exchange(): lax.ppermute(part(z + k), 'mp', [(i, i + k) for i in range(n - k)])  49.7 us
    pallas_call x4, Pallas kernels, up_slot(): pl.pallas_call(up_kernel, grid=(width // tile,), in_specs=in_specs, out_s...  40.5 us
    pallas_call x4, Pallas kernels, qkv_slot(): pl.pallas_call(qkv_kernel, grid=(width // HD,), in_specs=in_specs, out_sp...  36.9 us
  transfers between devices with their start and end apart: 32, of which 6 were waited for; matrix products, arithmetic and copies ran while one was open for 40% of the time, Pallas kernels for 13%

profile of v1, /device:TPU:0, one launch (start us, length us, event | category | flops | bytes accessed | tf_op | source)
XLA Modules:
  0.0 1066.4 jit_solution(4774093117698666359)
XLA Ops:
  25.2 57.0 %collective-permute-done.2 = bf16[512,2048]{1,0:T(8,128)(2,1)} collective-permute-done((bf16[512,2048]{1,0:T(8,128)(2,1)}, bf16[512,2048]{1,0:T(8,128)(2,1)}, u32[]{:S(2)}, u32[]{:S(2)}) %collective-permute-start.2) | collective-permute-done | bytes 2097184 | tf_op jit(solution)/shard_map/ppermute | solution.py:310
  103.3 50.5 %collective-permute-done.3 = bf16[512,2048]{1,0:T(8,128)(2,1)} collective-permute-done((bf16[512,2048]{1,0:T(8,128)(2,1)}, bf16[512,2048]{1,0:T(8,128)(2,1)}, u32[]{:S(2)}, u32[]{:S(2)}) %collective-permute-start.3) | collective-permute-done | bytes 2097184 | tf_op jit(solution)/shard_map/ppermute | solution.py:310
  182.7 20.5 %collective-permute-done.4 = bf16[512,2048]{1,0:T(8,128)(2,1)} collective-permute-done((bf16[512,2048]{1,0:T(8,128)(2,1)}, bf16[512,2048]{1,0:T(8,128)(2,1)}, u32[]{:S(2)}, u32[]{:S(2)}) %collective-permute-start.4) | collective-permute-done | bytes 2097184 | tf_op jit(solution)/shard_map/ppermute | solution.py:310
  217.4 10.2 up.4
  263.2 22.2 %convolution_convert_fusion.2 = bf16[2048,2048]{1,0:T(8,128)(2,1)S(1)} fusion(bf16[2048,2048]{1,0:T(8,128)(2,1)} %get-tuple-element.33, bf16[2048,2048]{1,0:T(8,128)(2,1)} %param.30), kind=kOutput, calls=%fused_computation.23 | convolution fusion | flops 17184063488 | bytes 25165824 | tf_op jit(solution)/shard_map/dot_general | solution.py:26
  345.0 25.5 %attend.1 = (bf16[2048,512]{1,0:T(8,128)(2,1)}, f32[2,2048]{1,0:T(2,128)}) custom-call(s32[4]{0:T(128)} %fusion.24.slot_ref, s32[4]{0:T(128)} %and_select_fusion.low_ref, bf16[2048,1536]{1,0:T(8,128)(2,1)} %qkv.7.qkv_ref, s32[1,2048]{1,0:T(1,128)} %bitcast.117), custom_call_target="tpu_custom_call" | custom-call | flops 4294967296 | bytes 6291456 | tf_op jit(solution)/shard_map/attend/pallas_call | solution.py:189
  389.2 28.9 %convert_reduce_fusion = (f32[2048]{0:T(1024)}, bf16[2048,2048]{1,0:T(8,128)(2,1)}) fusion(bf16[2048,2048]{1,0:T(8,128)(2,1)} %get-tuple-element.35, bf16[2048,2048]{1,0:T(8,128)(2,1)} %param.30, bf16[512,2048]{1,0:T(8,128)(2,1)} %get-tuple-element.67, bf16[512,2048]{1,0:T(8,128)(2,1)} %get-tuple-element.66, bf16[512,2048]{1,0:T(8,128)(2,1)} %get-tuple-element.72, ...), kind=kOutput, calls=%fused_computation.10 | convolution fusion | flops 17234393088 | bytes 33562624 | tf_op jit(solution)/shard_map/dot_general | solution.py:26
  418.1 24.5 %fusion.31 = f32[2048,2048]{1,0:T(8,128)} fusion(bf16[2048,2048]{1,0:T(8,128)(2,1)} %get-tuple-element.94, bf16[2048,2048]{1,0:T(8,128)(2,1)} %get-tuple-element.62.w_ref), kind=kOutput, calls=%fused_computation.122 | convolution fusion | flops 17179869184 | bytes 33554432 | tf_op jit(solution)/shard_map/dot_general | solution.py:26
  442.6 11.6 %convolution_convert_fusion.5.grad_ref = bf16[2048,512]{1,0:T(8,128)(2,1)} fusion(bf16[512,2048]{1,0:T(8,128)(2,1)S(1)} %copy-done, bf16[512,2048]{1,0:T(8,128)(2,1)S(1)} %copy-done.12, bf16[512,2048]{1,0:T(8,128)(2,1)S(1)} %copy-done.10, bf16[512,2048]{1,0:T(8,128)(2,1)S(1)} %copy-done.14, bf16[512,2048]{1,0:T(8,128)(2,1)S(1)} %bitcast.125), kind=kOutput, calls=%fused_computation.61 | convolution fusion | flops 4329570304 | bytes 12582912 | tf_op jit(solution)/shard_map/dot_general | solution.py:26
  454.1 33.8 %attend_back.1 = bf16[2048,1536]{1,0:T(8,128)(2,1)} custom-call(s32[4]{0:T(128)} %fusion.24.slot_ref, s32[8]{0:T(128)} %convert_reduce_fusion.4.high_ref, bf16[2048,1536]{1,0:T(8,128)(2,1)} %qkv.7.qkv_ref, bf16[2048,512]{1,0:T(8,128)(2,1)} %convolution_convert_fusion.5.grad_ref, bf16[2048,512]{1,0:T(8,128)(2,1)} %get-tuple-element.26.out_ref, ...), custom_call_target="tpu_custom_call" | custom-call | flops 10737418240 | bytes 12582912 | tf_op jit(solution)/shard_map/attend_back/pallas_call | solution.py:280
  487.9 24.4 %fusion.30 = (bf16[2048,2048]{1,0:T(8,128)(2,1)}, f32[2048,2048]{1,0:T(8,128)}) fusion(f32[2048,2048]{1,0:T(8,128)} %fusion.31, bf16[2048,1536]{1,0:T(8,128)(2,1)} %attend_back.1, bf16[2048,1536]{1,0:T(8,128)(2,1)} %multiply_convert_fusion.1.w_ref), kind=kOutput, calls=%fused_computation.121 | convolution fusion | flops 12893290496 | bytes 54525952 | tf_op jit(solution)/shard_map/dot_general | solution.py:26
  530.6 20.7 %convolution_convert_fusion = bf16[2048,2048]{1,0:T(8,128)(2,1)} fusion(bf16[2048,2048]{1,0:T(8,128)(2,1)S(1)} %bitcast.103, bf16[512,2048]{1,0:T(8,128)(2,1)S(1)} %copy-done.13, bf16[512,2048]{1,0:T(8,128)(2,1)S(1)} %copy-done.11, bf16[512,2048]{1,0:T(8,128)(2,1)S(1)} %copy-done.15, bf16[512,2048]{1,0:T(8,128)(2,1)S(1)} %bitcast.126), kind=kOutput, calls=%fused_computation.21 | convolution fusion | flops 17217617920 | bytes 25165824 | tf_op jit(solution)/shard_map/dot_general | solution.py:26
  551.4 26.6 %fusion.3 = (f32[2048]{0:T(1024)S(1)}, f32[2048]{0:T(1024)S(1)}, bf16[2048,2048]{1,0:T(8,128)(2,1)}) fusion(bf16[2048,2048]{1,0:T(8,128)(2,1)} %param.28, f32[2048]{0:T(1024)S(1)} %copy-done.32, bf16[2048,2048]{1,0:T(8,128)(2,1)} %get-tuple-element.94, bf16[512,2048]{1,0:T(8,128)(2,1)} %get-tuple-element.69.x_ref, bf16[512,2048]{1,0:T(8,128)(2,1)S(1)} %copy-done.5, ...), kind=kOutput, calls=%fused_computation.8 | convolution fusion | flops 17242779648 | bytes 33579008 | tf_op jit(solution)/shard_map/dot_general | solution.py:26
  577.9 21.3 %multiply_reduce_fusion.1 = (f32[2048]{0:T(1024)S(1)}, bf16[2048,1536]{1,0:T(8,128)(2,1)}) fusion(f32[2048,1536]{1,0:T(8,128)} %bitcast.106, bf16[2048,1536]{1,0:T(8,128)(2,1)} %attend_back.1, bf16[512,2048]{1,0:T(8,128)(2,1)} %get-tuple-element.69.x_ref, bf16[512,2048]{1,0:T(8,128)(2,1)S(1)} %copy-done.5, bf16[512,2048]{1,0:T(8,128)(2,1)} %get-tuple-element.79.x_ref, ...), kind=kOutput, calls=%fused_computation.15 | convolution fusion | flops 12931037184 | bytes 33562624 | tf_op jit(solution)/shard_map/dot_general | solution.py:26
  611.0 49.7 %collective-permute-done.6 = bf16[512,512]{1,0:T(8,128)(2,1)} collective-permute-done((bf16[512,512]{1,0:T(8,128)(2,1)}, bf16[512,512]{1,0:T(8,128)(2,1)}, u32[]{:S(2)}, u32[]{:S(2)}) %collective-permute-start.6) | collective-permute-done | bytes 524320 | tf_op jit(solution)/shard_map/ppermute | solution.py:340
  694.9 71.3 %collective-permute-done.10 = bf16[512,512]{1,0:T(8,128)(2,1)S(1)} collective-permute-done((bf16[512,512]{1,0:T(8,128)(2,1)S(1)}, bf16[512,512]{1,0:T(8,128)(2,1)S(1)}, u32[]{:S(2)}, u32[]{:S(2)}) %collective-permute-start.10) | collective-permute-done | bytes 524320 | tf_op jit(solution)/shard_map/ppermute | solution.py:341
  793.0 92.4 %multiply_reduce_fusion = f32[2048]{0:T(1024)S(1)} fusion(bf16[2048,2,768]{2,1,0:T(2,128)(2,1)} %param.24, f32[2,768]{1,0:T(2,128)S(1)} %mul.261), kind=kLoop, calls=%fused_computation.13 | loop fusion | flops 9435136 | bytes 6305792 | tf_op jit(solution)/shard_map/reduce_sum | solution.py:447
  885.5 24.2 %all-reduce.1 = (f32[1536]{0:T(1024)S(1)}, f32[2048]{0:T(1024)S(1)}) all-reduce(f32[1536]{0:T(1024)S(1)} %convert_reduce_fusion.1, f32[2048]{0:T(1024)S(1)} %copy-done.32), channel_id=1, replica_groups=mesh['dp'=8,'mp'=4] {'dp'}, use_global_device_ids=true, to_apply=%region_20.21 | all-reduce | flops 3584 | bytes 28672 | tf_op jit(solution)/shard_map/psum | solution.py:456
  910.3 12.0 %add_add_fusion = f32[512,2048]{1,0:T(8,128)} fusion(bf16[512,2048]{1,0:T(8,128)(2,1)} %collective-permute-done.17, bf16[512,2048]{1,0:T(8,128)(2,1)} %collective-permute-done.14, bf16[2048,2048]{1,0:T(8,128)(2,1)} %param.30, f32[2048]{0:T(1024)S(1)} %copy-done.40, bf16[2048,2048]{1,0:T(8,128)(2,1)} %get-tuple-element.33), kind=kOutput, calls=%fused_computation.51 | convolution fusion | flops 4300210176 | bytes 18882560 | tf_op jit(solution)/shard_map/dot_general | solution.py:26
  926.9 16.4 %multiply_reduce_fusion.4 = (f32[]{:T(128)}, bf16[1,512,2048]{2,1,0:T(8,128)(2,1)}, f32[]{:T(128)}, bf16[1,512,2048]{2,1,0:T(8,128)(2,1)}, f32[2048]{0:T(1024)S(1)}) fusion(f32[2048]{0:T(1024)S(1)} %copy-done.41, f32[512,2048]{1,0:T(8,128)} %add_add_fusion, bf16[1,512,2048]{2,1,0:T(8,128)(2,1)S(1)} %copy-done.3, f32[512]{0:T(512)S(1)} %broadcast_multiply_fusion, ...), kind=kOutput, calls=%fused_computation.46 | convolution fusion | flops 4319082496 | bytes 31481864 | tf_op jit(solution)/shard_map/dot_general | solution.py:26
  944.7 64.6 %all-reduce = (f32[2048]{0:T(1024)}, f32[2048]{0:T(1024)}, f32[2048]{0:T(1024)}, f32[2048]{0:T(1024)}, f32[2048]{0:T(1024)S(1)}, /*index=5*/f32[2]{0:T(128)S(1)}) all-reduce(f32[2048]{0:T(1024)S(1)} %get-tuple-element.91, f32[2048]{0:T(1024)S(1)} %multiply_reduce_fusion, ...), channel_id=1, replica_groups=mesh['dp'=8,'mp'=4] {'dp','mp'}, use_global_device_ids=true, to_apply=%region_10.11 | all-reduce | flops 10242 | bytes 81936 | tf_op jit(solution)/shard_map/psum | solution.py:453
  1017.9 15.5 %reshape.194 = f32[2048,2,768]{2,1,0:T(2,128)} reshape(f32[2048,1536]{1,0:T(8,128)} %multiply_add_fusion.1) | data formatting | bytes 25165824 | tf_op jit(solution)/shard_map/reshape | solution.py:468
  1035.9 11.7 %convert_element_type.257 = f32[2048,2048]{1,0:T(8,128)} convert(bf16[2048,2048]{1,0:T(8,128)(2,1)} %get-tuple-element.52) | non-fusion elementwise | flops 4194304 | bytes 25165824 | tf_op jit(solution)/shard_map/convert_element_type | solution.py:474
  1047.6 10.5 multiply_add_fusion
  (224 shorter events, 299.9 us)
Async XLA Ops:
  8.1 918.8 %all-gather.2.cloned.1.call-start = ((), (), s32[]{:S(2)}) async-start(), calls=%async_computation | async-start | bytes 8650752 | tf_op jit(solution)/shard_map/all_gather | solution.py:385
  14.4 67.8 %collective-permute-start.2 = (bf16[512,2048]{1,0:T(8,128)(2,1)}, bf16[512,2048]{1,0:T(8,128)(2,1)}, u32[]{:S(2)}, u32[]{:S(2)}) collective-permute-start(bf16[512,2048]{1,0:T(8,128)(2,1)} %fusion.10.x_ref), channel_id=1, source_target_pairs={{1,0},{2,1},{3,2},{5,4},{6,5},{7,6},{9,8},{10,9},{11,10},{13,12},{... | collective-permute-start | bytes 6291464 | tf_op jit(solution)/shard_map/ppermute | solution.py:310
  15.9 67.6 %collective-permute-start = (bf16[512,2048]{1,0:T(8,128)(2,1)}, bf16[512,2048]{1,0:T(8,128)(2,1)}, u32[]{:S(2)}, u32[]{:S(2)}) collective-permute-start(bf16[512,2048]{1,0:T(8,128)(2,1)} %fusion.10.x_ref), channel_id=1, source_target_pairs={{0,1},{1,2},{2,3},{4,5},{5,6},{6,7},{8,9},{9,10},{10,11},{12,13},{... | collective-permute-start | bytes 6291464 | tf_op jit(solution)/shard_map/ppermute | solution.py:309
  23.6 986.3 %all-reduce.5.cloned.1.call-start = ((), (), s32[]{:S(2)}) async-start(), calls=%async_computation.1 | async-start | bytes 50331648 | tf_op jit(solution)/shard_map/psum | solution.py:346
  82.2 71.5 %collective-permute-start.3 = (bf16[512,2048]{1,0:T(8,128)(2,1)}, bf16[512,2048]{1,0:T(8,128)(2,1)}, u32[]{:S(2)}, u32[]{:S(2)}) collective-permute-start(bf16[512,2048]{1,0:T(8,128)(2,1)} %collective-permute-done.2), channel_id=1, source_target_pairs={{1,0},{2,1},{5,4},{6,5},{9,8},{10,9},{13,12},{14,13},{17,16},{18,1... | collective-permute-start | bytes 6291464 | tf_op jit(solution)/shard_map/ppermute | solution.py:310
  83.5 71.5 %collective-permute-start.1 = (bf16[512,2048]{1,0:T(8,128)(2,1)}, bf16[512,2048]{1,0:T(8,128)(2,1)}, u32[]{:S(2)}, u32[]{:S(2)}) collective-permute-start(bf16[512,2048]{1,0:T(8,128)(2,1)} %collective-permute-done), channel_id=1, source_target_pairs={{1,2},{2,3},{5,6},{6,7},{9,10},{10,11},{13,14},{14,15},{17,18},{18... | collective-permute-start | bytes 6291464 | tf_op jit(solution)/shard_map/ppermute | solution.py:309
  210.0 49.9 %collective-permute-start.19 = (bf16[512,2048]{1,0:T(8,128)(2,1)S(1)}, bf16[512,2048]{1,0:T(8,128)(2,1)}, u32[]{:S(2)}, u32[]{:S(2)}) collective-permute-start(bf16[512,2048]{1,0:T(8,128)(2,1)S(1)} %bitcast.123), channel_id=1, source_target_pairs={{1,0},{2,1},{3,2},{5,4},{6,5},{7,6},{9,8},{10,9},{11,10},{13,12},{... | collective-permute-start | bytes 6291464 | tf_op jit(solution)/shard_map/ppermute | solution.py:310
  289.9 80.6 %collective-permute-start.12 = (bf16[512,2048]{1,0:T(8,128)(2,1)}, bf16[512,2048]{1,0:T(8,128)(2,1)}, u32[]{:S(2)}, u32[]{:S(2)}) collective-permute-start(bf16[512,2048]{1,0:T(8,128)(2,1)} %get-tuple-element.59), channel_id=1, source_target_pairs={{0,1},{4,5},{8,9},{12,13},{16,17},{20,21},{24,25},{28,29}} | collective-permute-start | bytes 6291464 | tf_op jit(solution)/shard_map/ppermute | solution.py:331
  307.9 74.4 %collective-permute-start.22 = (bf16[512,2048]{1,0:T(8,128)(2,1)}, bf16[512,2048]{1,0:T(8,128)(2,1)}, u32[]{:S(2)}, u32[]{:S(2)}) collective-permute-start(bf16[512,2048]{1,0:T(8,128)(2,1)} %collective-permute-done.20), channel_id=1, source_target_pairs={{1,0},{5,4},{9,8},{13,12},{17,16},{21,20},{25,24},{29,28}} | collective-permute-start | bytes 6291464 | tf_op jit(solution)/shard_map/ppermute | solution.py:310
  309.2 73.1 %collective-permute-start.23 = (bf16[512,2048]{1,0:T(8,128)(2,1)}, bf16[512,2048]{1,0:T(8,128)(2,1)}, u32[]{:S(2)}, u32[]{:S(2)}) collective-permute-start(bf16[512,2048]{1,0:T(8,128)(2,1)} %collective-permute-done.21), channel_id=1, source_target_pairs={{2,3},{6,7},{10,11},{14,15},{18,19},{22,23},{26,27},{30,31}} | collective-permute-start | bytes 6291464 | tf_op jit(solution)/shard_map/ppermute | solution.py:309
  314.9 348.3 %collective-permute-start.15 = (bf16[512,2048]{1,0:T(8,128)(2,1)}, bf16[512,2048]{1,0:T(8,128)(2,1)}, u32[]{:S(2)}, u32[]{:S(2)}) collective-permute-start(bf16[512,2048]{1,0:T(8,128)(2,1)} %get-tuple-element.60), channel_id=1, source_target_pairs={{3,2},{7,6},{11,10},{15,14},{19,18},{23,22},{27,26},{31,30}} | collective-permute-start | bytes 6291464 | tf_op jit(solution)/shard_map/ppermute | solution.py:332
  375.0 295.6 %collective-permute-start.13 = (bf16[512,2048]{1,0:T(8,128)(2,1)}, bf16[512,2048]{1,0:T(8,128)(2,1)}, u32[]{:S(2)}, u32[]{:S(2)}) collective-permute-start(bf16[512,2048]{1,0:T(8,128)(2,1)} %add_convert_fusion.7), channel_id=1, source_target_pairs={{0,1},{1,2},{4,5},{5,6},{8,9},{9,10},{12,13},{13,14},{16,17},{17,1... | collective-permute-start | bytes 6291464 | tf_op jit(solution)/shard_map/ppermute | solution.py:331
  517.5 81.8 %collective-permute-start.24 = (bf16[512,2048]{1,0:T(8,128)(2,1)}, bf16[512,2048]{1,0:T(8,128)(2,1)}, u32[]{:S(2)}, u32[]{:S(2)}) collective-permute-start(bf16[512,2048]{1,0:T(8,128)(2,1)} %get-tuple-element.55), channel_id=1, source_target_pairs={{0,1},{4,5},{8,9},{12,13},{16,17},{20,21},{24,25},{28,29}} | collective-permute-start | bytes 6291464 | tf_op jit(solution)/shard_map/ppermute | solution.py:331
  520.3 163.0 %collective-permute-start.27 = (bf16[512,2048]{1,0:T(8,128)(2,1)}, bf16[512,2048]{1,0:T(8,128)(2,1)}, u32[]{:S(2)}, u32[]{:S(2)}) collective-permute-start(bf16[512,2048]{1,0:T(8,128)(2,1)} %get-tuple-element.56), channel_id=1, source_target_pairs={{3,2},{7,6},{11,10},{15,14},{19,18},{23,22},{27,26},{31,30}} | collective-permute-start | bytes 6291464 | tf_op jit(solution)/shard_map/ppermute | solution.py:332
  604.0 80.8 %collective-permute-start.25 = (bf16[512,2048]{1,0:T(8,128)(2,1)}, bf16[512,2048]{1,0:T(8,128)(2,1)}, u32[]{:S(2)}, u32[]{:S(2)}) collective-permute-start(bf16[512,2048]{1,0:T(8,128)(2,1)} %add_convert_fusion.3), channel_id=1, source_target_pairs={{0,1},{1,2},{4,5},{5,6},{8,9},{9,10},{12,13},{13,14},{16,17},{17,1... | collective-permute-start | bytes 6291464 | tf_op jit(solution)/shard_map/ppermute | solution.py:331
  608.0 52.8 %collective-permute-start.6 = (bf16[512,512]{1,0:T(8,128)(2,1)}, bf16[512,512]{1,0:T(8,128)(2,1)}, u32[]{:S(2)}, u32[]{:S(2)}) collective-permute-start(bf16[512,512]{1,0:T(8,128)(2,1)} %get-tuple-element.78), channel_id=1, source_target_pairs={{0,3},{4,7},{8,11},{12,15},{16,19},{20,23},{24,27},{28,31}} | collective-permute-start | bytes 1572872 | tf_op jit(solution)/shard_map/ppermute | solution.py:340
  679.9 91.7 %collective-permute-start.16 = (bf16[512,2048]{1,0:T(8,128)(2,1)}, bf16[512,2048]{1,0:T(8,128)(2,1)}, u32[]{:S(2)}, u32[]{:S(2)}) collective-permute-start(bf16[512,2048]{1,0:T(8,128)(2,1)} %get-tuple-element.58), channel_id=1, source_target_pairs={{2,1},{3,2},{6,5},{7,6},{10,9},{11,10},{14,13},{15,14},{18,17},{19... | collective-permute-start | bytes 6291464 | tf_op jit(solution)/shard_map/ppermute | solution.py:332
  681.9 84.3 %collective-permute-start.10 = (bf16[512,512]{1,0:T(8,128)(2,1)S(1)}, bf16[512,512]{1,0:T(8,128)(2,1)S(1)}, u32[]{:S(2)}, u32[]{:S(2)}) collective-permute-start(bf16[512,512]{1,0:T(8,128)(2,1)S(1)} %get-tuple-element.74), channel_id=1, source_target_pairs={{2,0},{3,1},{6,4},{7,5},{10,8},{11,9},{14,12},{15,13},{18,16},{19,... | collective-permute-start | bytes 1572872 | tf_op jit(solution)/shard_map/ppermute | solution.py:341
  683.3 83.0 %collective-permute-start.11 = (bf16[512,512]{1,0:T(8,128)(2,1)S(1)}, bf16[512,512]{1,0:T(8,128)(2,1)S(1)}, u32[]{:S(2)}, u32[]{:S(2)}) collective-permute-start(bf16[512,512]{1,0:T(8,128)(2,1)S(1)} %get-tuple-element.73), channel_id=1, source_target_pairs={{3,0},{7,4},{11,8},{15,12},{19,16},{23,20},{27,24},{31,28}} | collective-permute-start | bytes 1572872 | tf_op jit(solution)/shard_map/ppermute | solution.py:341
  692.8 94.3 %collective-permute-start.28 = (bf16[512,2048]{1,0:T(8,128)(2,1)}, bf16[512,2048]{1,0:T(8,128)(2,1)}, u32[]{:S(2)}, u32[]{:S(2)}) collective-permute-start(bf16[512,2048]{1,0:T(8,128)(2,1)} %get-tuple-element.54), channel_id=1, source_target_pairs={{2,1},{3,2},{6,5},{7,6},{10,9},{11,10},{14,13},{15,14},{18,17},{19... | collective-permute-start | bytes 6291464 | tf_op jit(solution)/shard_map/ppermute | solution.py:332
  768.9 141.4 %collective-permute-start.14 = (bf16[512,2048]{1,0:T(8,128)(2,1)}, bf16[512,2048]{1,0:T(8,128)(2,1)}, u32[]{:S(2)}, u32[]{:S(2)}) collective-permute-start(bf16[512,2048]{1,0:T(8,128)(2,1)} %get-tuple-element.57), channel_id=1, source_target_pairs={{0,1},{1,2},{2,3},{4,5},{5,6},{6,7},{8,9},{9,10},{10,11},{12,13},{... | collective-permute-start | bytes 6291464 | tf_op jit(solution)/shard_map/ppermute | solution.py:331
  776.0 134.3 %collective-permute-start.17 = (bf16[512,2048]{1,0:T(8,128)(2,1)}, bf16[512,2048]{1,0:T(8,128)(2,1)}, u32[]{:S(2)}, u32[]{:S(2)}) collective-permute-start(bf16[512,2048]{1,0:T(8,128)(2,1)} %add_convert_fusion.4), channel_id=1, source_target_pairs={{1,0},{2,1},{3,2},{5,4},{6,5},{7,6},{9,8},{10,9},{11,10},{13,12},{... | collective-permute-start | bytes 6291464 | tf_op jit(solution)/shard_map/ppermute | solution.py:332
  781.2 141.2 %collective-permute-start.26 = (bf16[512,2048]{1,0:T(8,128)(2,1)}, bf16[512,2048]{1,0:T(8,128)(2,1)}, u32[]{:S(2)}, u32[]{:S(2)}) collective-permute-start(bf16[512,2048]{1,0:T(8,128)(2,1)} %get-tuple-element.53), channel_id=1, source_target_pairs={{0,1},{1,2},{2,3},{4,5},{5,6},{6,7},{8,9},{9,10},{10,11},{12,13},{... | collective-permute-start | bytes 6291464 | tf_op jit(solution)/shard_map/ppermute | solution.py:331
  791.6 130.8 %collective-permute-start.29 = (bf16[512,2048]{1,0:T(8,128)(2,1)}, bf16[512,2048]{1,0:T(8,128)(2,1)}, u32[]{:S(2)}, u32[]{:S(2)}) collective-permute-start(bf16[512,2048]{1,0:T(8,128)(2,1)} %add_convert_fusion), channel_id=1, source_target_pairs={{1,0},{2,1},{3,2},{5,4},{6,5},{7,6},{9,8},{10,9},{11,10},{13,12},{... | collective-permute-start | bytes 6291464 | tf_op jit(solution)/shard_map/ppermute | solution.py:332
  (52 other events, 1864.6 us)
Sparse Core Ops, SparseCore 0:
  23.7 98.9 all-gather.1
Sparse Core Ops, SparseCore 1:
  599.3 307.6 all-reduce.4

commit v2 on v1

v2 whole, which is shorter than its diff:
```python
import functools

import jax
import jax.numpy as jnp
import numpy as np
from jax import lax
from jax.experimental import pallas as pl
from jax.experimental.pallas import tpu as pltpu
from jax.sharding import PartitionSpec as P

HD = 256
ROT = 64
KBLOCK = 256
NORM_EPS = 1e-05
NEG_FILL = -1000000000.0
VMEM_LIMIT = 56 * 1024 * 1024
BF16 = jnp.bfloat16
F32 = jnp.float32

NT = (((1,), (1,)), ((), ()))
NN = (((1,), (0,)), ((), ()))
TN = (((0,), (0,)), ((), ()))


def dot(a, b, dims=NN):
    return lax.dot_general(a, b, dims, preferred_element_type=F32)


def arrival_order(n):
    return [sorted(range(n), key=lambda p, z=z: (abs(p - z), p)) for z in range(n)]


def params():
    return pltpu.CompilerParams(vmem_limit_bytes=VMEM_LIMIT)


def turn(part, cosine, sine):
    lane = lax.broadcasted_iota(jnp.int32, part.shape, 1)
    swapped = jnp.where(
        lane < ROT // 2,
        pltpu.roll(part, 128 - ROT // 2, 1),
        pltpu.roll(part, ROT // 2, 1),
    )
    return part * cosine + swapped * sine


def after(array, *others):
    anywhere = pl.BlockSpec(memory_space=pl.ANY)
    return pl.pallas_call(
        lambda *refs: None,
        in_specs=[anywhere] * (1 + len(others)),
        out_specs=anywhere,
        out_shape=jax.ShapeDtypeStruct(array.shape, array.dtype),
        input_output_aliases={0: 0},
        name="after",
    )(array, *others)


def across(z, n, values):
    picked = jnp.int32(0)
    for at in range(n):
        picked = picked + jnp.where(z == at, values[at], 0)
    return picked


def opening_kernel(n, heads, *refs):
    x_ref, in_ref, up_ref, down_ref, vec_ref, in_bias_ref, up_bias_ref, cos_ref, sin_ref = refs[:9]
    x_rows, qkv_ref, joint_ref, slope_ref, part_ref = refs[9:14]
    w_in, w_up, w_down, chunk, attn_in, mlp_in, qkv_out, act_out, slope_out, part_out = refs[14:24]
    send, recv, load, store = refs[24:]
    z = lax.axis_index("mp")
    t, d = x_ref.shape
    in_width, hidden = in_ref.shape[1], up_ref.shape[1]
    ids = pl.DeviceIdType.MESH

    barrier = pltpu.get_barrier_semaphore()
    for way in (1, -1):

        @pl.when((z + way >= 0) & (z + way < n))
        def _():
            pl.semaphore_signal(barrier, inc=1, device_id={"mp": z + way}, device_id_type=ids)

    pl.semaphore_wait(barrier, 2 - jnp.where(z == 0, 1, 0) - jnp.where(z == n - 1, 1, 0))

    def rows_of(position):
        return pl.ds(pl.multiple_of(position * t, t), t)

    own = pltpu.make_async_copy(x_ref, x_rows.at[rows_of(z)], load.at[0])
    own.start()
    hops = {}
    for k in range(1, n):
        for way in (1, -1):
            origin = z - way * (k - 1)
            there = z + way
            goes = (origin >= 0) & (origin < n) & (there >= 0) & (there < n)
            rows = rows_of(jnp.clip(origin, 0, n - 1))
            at = 2 * (k - 1) + (way < 0)
            copy = pltpu.make_async_remote_copy(
                x_ref if k == 1 else x_rows.at[rows], x_rows.at[rows], send.at[at], recv.at[at], {"mp": there}, ids
            )
            arrives = (z - way * k >= 0) & (z - way * k < n)
            hops[k, way] = (copy, goes, arrives)

    def start_step(k):
        for way in (1, -1):
            copy, goes, _ = hops[k, way]
            pl.when(goes)(copy.start)

    start_step(1)
    weights = [
        pltpu.make_async_copy(source, target, load.at[1 + i])
        for i, (source, target) in enumerate(((in_ref, w_in), (up_ref, w_up), (down_ref, w_down)))
    ]
    for copy in weights:
        copy.start()
    order = arrival_order(n)
    positions = [across(z, n, [order[zz][s] for zz in range(n)]) for s in range(n)]

    def slot(s, unused):
        position = jnp.int32(0)
        for at in range(n):
            position = position + jnp.where(s == at, positions[at], 0)
        rows = rows_of(position)
        for k in range(1, n):

            @pl.when(s == k)
            def _():
                for way in (1, -1):
                    copy, _, arrives = hops[k, way]
                    pl.when(arrives)(copy.wait_recv)
                if k < n - 1:
                    start_step(k + 1)

        @pl.when(s == 0)
        def _():
            pltpu.make_async_copy(x_ref, chunk, load.at[4]).start()

        @pl.when(s > 0)
        def _():
            pltpu.make_async_copy(x_rows.at[rows], chunk, load.at[4]).start()

        pltpu.make_async_copy(x_ref, chunk, load.at[4]).wait()

        def norm_rows(i, unused):
            block = pl.ds(pl.multiple_of(i * 32, 32), 32)
            x = chunk[block, :].astype(F32)
            attn_in[block, :] = (x * vec_ref[0:1, :] + vec_ref[1:2, :]).astype(BF16)
            mlp_in[block, :] = (x * vec_ref[2:3, :] + vec_ref[3:4, :]).astype(BF16)
            return unused

        lax.fori_loop(0, t // 32, norm_rows, 0)
        outs = [
            pltpu.make_async_copy(qkv_out, qkv_ref.at[rows], store.at[0]),
            pltpu.make_async_copy(act_out, joint_ref.at[rows, pl.ds(heads * HD, hidden)], store.at[1]),
            pltpu.make_async_copy(slope_out, slope_ref.at[rows], store.at[2]),
            pltpu.make_async_copy(part_out, part_ref.at[rows], store.at[3]),
        ]

        @pl.when(s == 0)
        def _():
            weights[0].wait()

        @pl.when(s > 0)
        def _():
            outs[0].wait()

        cosine, sine = cos_ref[rows, :], sin_ref[rows, :]
        for j in range(3 * heads):
            cols = slice(j * HD, (j + 1) * HD)
            acc = dot(attn_in[...], w_in[:, cols]) + in_bias_ref[:, cols]
            if j % 3 < 2:
                scale = HD**-0.5 if j % 3 == 0 else 1.0
                qkv_out[:, cols] = jnp.concatenate(
                    [turn(acc[:, :128], cosine, sine) * scale, acc[:, 128:] * scale], axis=1
                ).astype(BF16)
            else:
                qkv_out[:, cols] = acc.astype(BF16)
        outs[0].start()

        @pl.when(s == 0)
        def _():
            weights[1].wait()
            weights[2].wait()

        @pl.when(s > 0)
        def _():
            for copy in outs[1:]:
                copy.wait()

        tile = min(512, hidden)
        for first in range(0, hidden, tile):
            cols = slice(first, first + tile)
            u = dot(mlp_in[...], w_up[:, cols]) + up_bias_ref[:, cols]
            below = 0.5 + 0.5 * lax.erf(u * (0.5**0.5))
            act_out[:, cols] = (u * below).astype(BF16)
            density = jnp.exp(u * u * -0.5) * ((2.0 * np.pi) ** -0.5)
            slope_out[:, cols] = (below + u * density).astype(BF16)
        outs[1].start()
        outs[2].start()
        for first in range(0, d, 512):
            cols = slice(first, first + 512)
            part_out[:, cols] = dot(act_out[...], w_down[:, cols]).astype(BF16)
        outs[3].start()

        @pl.when(s == n - 1)
        def _():
            for copy in outs:
                copy.wait()

        return unused

    lax.fori_loop(0, n, slot, 0)
    own.wait()
    for copy, goes, _ in hops.values():
        pl.when(goes)(copy.wait_send)


def opening(n, x, flat_in, up_weight, down_weight, vectors, in_bias, up_bias, cosine, sine):
    t, d = x.shape
    in_width, hidden = flat_in.shape[1], up_weight.shape[1]
    heads, rows = in_width // (3 * HD), n * t
    anywhere, whole = pl.BlockSpec(memory_space=pl.ANY), pl.BlockSpec(memory_space=pltpu.VMEM)
    return pl.pallas_call(
        functools.partial(opening_kernel, n, heads),
        in_specs=[anywhere] * 4 + [whole] * 5,
        out_specs=[anywhere] * 5,
        out_shape=[
            jax.ShapeDtypeStruct(shape, BF16)
            for shape in (
                (rows, d), (rows, in_width), (rows, heads * HD + hidden), (rows, hidden), (rows, d),
            )
        ],
        scratch_shapes=[
            pltpu.VMEM(shape, BF16)
            for shape in (
                (d, in_width), (d, hidden), (hidden, d), (t, d), (t, d), (t, d),
                (t, in_width), (t, hidden), (t, hidden), (t, d),
            )
        ]
        + [pltpu.SemaphoreType.DMA((2 * (n - 1),))] * 2
        + [pltpu.SemaphoreType.DMA((5,)), pltpu.SemaphoreType.DMA((4,))],
        compiler_params=pltpu.CompilerParams(
            vmem_limit_bytes=VMEM_LIMIT, collective_id=1, has_side_effects=True
        ),
        cost_estimate=pl.CostEstimate(
            flops=16 * 2 * rows * d * (in_width + 2 * hidden), bytes_accessed=200 * 2**20, transcendentals=0
        ),
        name="opening",
    )(x, flat_in, up_weight, down_weight, vectors, in_bias, up_bias, cosine, sine)


def up_back_kernel(g_ref, w_ref, slope_ref, out_ref):
    out_ref[...] = (dot(g_ref[...], w_ref[...], NT) * slope_ref[...].astype(F32)).astype(BF16)


def up_back(in_width, tile, g, down_weight, slope):
    rows, d = g.shape
    width = down_weight.shape[0]
    first = in_width // tile
    block = min(rows, 1024)
    return pl.pallas_call(
        up_back_kernel,
        grid=(rows // block, width // tile),
        in_specs=[
            pl.BlockSpec((block, d), lambda i, j: (i, 0)),
            pl.BlockSpec((tile, d), lambda i, j: (j, 0)),
            pl.BlockSpec((block, tile), lambda i, j: (i, j)),
        ],
        out_specs=pl.BlockSpec((block, tile), lambda i, j: (i, first + j)),
        out_shape=jax.ShapeDtypeStruct((rows, in_width + width), BF16),
        compiler_params=params(),
        cost_estimate=pl.CostEstimate(
            flops=2 * rows * d * width, bytes_accessed=2 * (rows * d + d * width + 2 * rows * width), transcendentals=0
        ),
        name="up_back",
    )(g, down_weight, slope)


def cross_kernel(heads_tile, x_ref, back_ref, in_ref, up_ref, cross_ref, sums_ref, total_ref, xt_ref):
    width, in_width = back_ref.shape[1], in_ref.shape[1]
    tile = heads_tile

    @pl.when(pl.program_id(0) == 0)
    def _():
        total_ref[...] = jnp.zeros_like(total_ref)
        step = 64

        def body(i, unused):
            rows = back_ref[pl.ds(pl.multiple_of(i * step, step), step), :].astype(F32)
            for r in range(0, step, 8):
                total_ref[...] += rows[r : r + 8]
            return unused

        lax.fori_loop(0, back_ref.shape[0] // step, body, 0)
        total_ref[...] = jnp.broadcast_to(jnp.sum(total_ref[...], axis=0, keepdims=True), total_ref.shape)

    xt_ref[...] = x_ref[...].T
    sums = [jnp.zeros((xt_ref.shape[0], 128), F32) for _ in range(4)]
    for first in range(0, width, tile):
        cols = slice(first, first + tile)
        product = dot(xt_ref[...], back_ref[:, cols])
        cross_ref[:, cols] = product.astype(BF16)
        inside = first < in_width
        wide = (in_ref[:, cols] if inside else up_ref[:, first - in_width : first - in_width + tile]).astype(F32)
        kind = 0 if inside else 2
        for at, term in ((kind, product * wide), (kind + 1, total_ref[0:1, cols] * wide)):
            for lane in range(0, tile, 128):
                sums[at] = sums[at] + term[:, lane : lane + 128]
    lane = lax.broadcasted_iota(jnp.int32, sums[0].shape, 1)
    out = jnp.zeros_like(sums[0])
    for at in range(4):
        out = out + jnp.where(lane == at, jnp.sum(sums[at], axis=1, keepdims=True), 0.0)
    sums_ref[...] = out


def cross_products(heads_tile, x_rows, back, flat_in, up_weight):
    rows, d = x_rows.shape
    width = back.shape[1]
    tile = 512
    once = pl.Buffered(1)
    return pl.pallas_call(
        functools.partial(cross_kernel, heads_tile),
        grid=(d // tile,),
        in_specs=[
            pl.BlockSpec((rows, tile), lambda i: (0, i)),
            pl.BlockSpec((rows, width), lambda i: (0, 0), pipeline_mode=once),
            pl.BlockSpec((tile, flat_in.shape[1]), lambda i: (i, 0)),
            pl.BlockSpec((tile, up_weight.shape[1]), lambda i: (i, 0)),
        ],
        out_specs=[
            pl.BlockSpec((tile, width), lambda i: (i, 0)),
            pl.BlockSpec((tile, 128), lambda i: (i, 0)),
            pl.BlockSpec((8, width), lambda i: (0, 0)),
        ],
        out_shape=[
            jax.ShapeDtypeStruct((d, width), BF16),
            jax.ShapeDtypeStruct((d, 128), F32),
            jax.ShapeDtypeStruct((8, width), F32),
        ],
        scratch_shapes=[pltpu.VMEM((tile, rows), BF16)],
        compiler_params=params(),
        cost_estimate=pl.CostEstimate(
            flops=2 * rows * d * width, bytes_accessed=2 * (rows * d + rows * width + 2 * d * width), transcendentals=0
        ),
        name="cross",
    )(x_rows, back, flat_in, up_weight)


def allowed(j, i, t, start):
    key = j * KBLOCK + lax.broadcasted_iota(jnp.int32, (KBLOCK, t), 0)
    query = i * t + lax.broadcasted_iota(jnp.int32, (1, t), 1)
    return (key >= start) & (key <= query)


def attend_kernel(t, heads, low_ref, qkv_ref, start_ref, held_ref, out_ref, log_ref, vt_ref, acc_ref):
    blocks = qkv_ref.shape[0] // t
    per = t // KBLOCK

    for h in range(heads):
        for c in range(blocks):
            rows = pl.ds(c * t, t)
            vt_ref[h, :, rows] = qkv_ref[rows, (3 * h + 2) * HD : (3 * h + 3) * HD].T

    def query_block(i, unused):
        row = pl.multiple_of(i * t, t)
        where = pl.ds(pl.multiple_of(i * t, t), t)
        start = start_ref[:, where]
        acc_ref[...] = jnp.zeros_like(acc_ref)

        def key_block(j, carried):
            place = pl.multiple_of(j * KBLOCK, KBLOCK)
            mask = allowed(j, i, t, start)
            new = []
            for h in range(heads):
                top, total = carried[h]
                query = qkv_ref[pl.ds(row, t), 3 * h * HD : (3 * h + 1) * HD]
                key = qkv_ref[pl.ds(place, KBLOCK), (3 * h + 1) * HD : (3 * h + 2) * HD]
                s = jnp.where(mask, dot(key, query, NT), NEG_FILL)
                higher = jnp.maximum(top, jnp.max(s, axis=0, keepdims=True))
                p = jnp.exp(s - higher)
                shrink = jnp.exp(top - higher)
                total = total * shrink + jnp.sum(p, axis=0, keepdims=True)
                vt = vt_ref[h, :, pl.ds(place, KBLOCK)]
                acc_ref[h] = acc_ref[h] * shrink + dot(vt, p.astype(BF16))
                new.append((higher, total))
            return tuple(new)

        first = (jnp.full((1, t), 2 * NEG_FILL, F32), jnp.zeros((1, t), F32))
        carried = lax.fori_loop(low_ref[i], (i + 1) * per, key_block, (first,) * heads)
        for h in range(heads):
            top, total = carried[h]
            log_ref[h : h + 1, where] = top + jnp.log(total)
            out_ref[pl.ds(row, t), h * HD : (h + 1) * HD] = (acc_ref[h] / total).T.astype(BF16)
        return unused

    lax.fori_loop(0, blocks, query_block, 0)


def attend(t, low, qkv, start, hidden):
    rows, width = qkv.shape
    heads = width // (3 * HD)
    whole = pl.BlockSpec(memory_space=pltpu.VMEM)
    return pl.pallas_call(
        functools.partial(attend_kernel, t, heads),
        grid=(1,),
        in_specs=[pl.BlockSpec(memory_space=pltpu.SMEM)] + [whole] * 2 + [pl.BlockSpec(memory_space=pl.ANY)],
        out_specs=[pl.BlockSpec((rows, heads * HD), lambda i: (0, 0)), whole],
        out_shape=[
            jax.ShapeDtypeStruct(hidden.shape, BF16),
            jax.ShapeDtypeStruct((heads, rows), F32),
        ],
        scratch_shapes=[pltpu.VMEM((heads, HD, rows), BF16), pltpu.VMEM((heads, HD, t), F32)],
        input_output_aliases={3: 0},
        compiler_params=params(),
        cost_estimate=pl.CostEstimate(
            flops=2 * rows * rows * HD * heads,
            bytes_accessed=2 * rows * width,
            transcendentals=rows * rows * heads // 2,
        ),
        name="attend",
    )(low, qkv, start, hidden)


def attend_back_kernel(
    t, heads, high_ref, qkv_ref, grad_ref, out_ref, log_ref, start_ref, cos_ref, sin_ref, held_ref, after_ref,
    proj_ref, query_grad, delta, key_grad, value_grad,
):
    rows = qkv_ref.shape[0]
    blocks = rows // t
    per = t // KBLOCK
    query_grad[...] = jnp.zeros_like(query_grad)

    def prepare(i, unused):
        row = pl.multiple_of(i * t, t)
        for h in range(heads):
            cols = slice(h * HD, (h + 1) * HD)
            both = grad_ref[pl.ds(row, t), cols].astype(F32) * out_ref[pl.ds(row, t), cols].astype(F32)
            delta[h : h + 1, pl.ds(pl.multiple_of(i * t, t), t)] = jnp.sum(both.T, axis=0, keepdims=True)
        return unused

    lax.fori_loop(0, blocks, prepare, 0)

    def turned_back(grad, place, count):
        cosine, sine = cos_ref[pl.ds(place, count), :], sin_ref[pl.ds(place, count), :]
        return turn(grad[:, :128], cosine, -sine)

    def key_block(j, unused):
        place = pl.multiple_of(j * KBLOCK, KBLOCK)
        key_grad[...] = jnp.zeros_like(key_grad)
        value_grad[...] = jnp.zeros_like(value_grad)

        def query_block(i, unused):
            row = pl.multiple_of(i * t, t)
            where = pl.ds(pl.multiple_of(i * t, t), t)
            mask = allowed(j, i, t, start_ref[:, where])
            for h in range(heads):
                query = qkv_ref[pl.ds(row, t), 3 * h * HD : (3 * h + 1) * HD]
                key = qkv_ref[pl.ds(place, KBLOCK), (3 * h + 1) * HD : (3 * h + 2) * HD]
                value = qkv_ref[pl.ds(place, KBLOCK), (3 * h + 2) * HD : (3 * h + 3) * HD]
                grad = grad_ref[pl.ds(row, t), h * HD : (h + 1) * HD]
                s = dot(key, query, NT) - log_ref[h : h + 1, where]
                p = jnp.exp(jnp.where(mask, s, NEG_FILL))
                p_grad = dot(value, grad, NT)
                value_grad[h] += dot(p.astype(BF16), grad)
                s_grad = (p * (p_grad - delta[h : h + 1, where])).astype(BF16)
                key_grad[h] += dot(s_grad, query)
                query_grad[pl.ds(row, t), h * HD : (h + 1) * HD] += dot(s_grad, key, TN)
            return unused

        lax.fori_loop(j // per, high_ref[j], query_block, 0)
        for h in range(heads):
            base = 3 * h * HD
            grad = key_grad[h]
            proj_ref[pl.ds(place, KBLOCK), base + HD : base + HD + 128] = turned_back(grad, place, KBLOCK).astype(BF16)
            proj_ref[pl.ds(place, KBLOCK), base + HD + 128 : base + 2 * HD] = grad[:, 128:].astype(BF16)
            proj_ref[pl.ds(place, KBLOCK), base + 2 * HD : base + 3 * HD] = value_grad[h].astype(BF16)
        return unused

    lax.fori_loop(0, rows // KBLOCK, key_block, 0)

    def finish(c, unused):
        place = pl.multiple_of(c * t, t)
        for h in range(heads):
            base = 3 * h * HD
            grad = query_grad[pl.ds(place, t), h * HD : (h + 1) * HD] * HD**-0.5
            proj_ref[pl.ds(place, t), base : base + 128] = turned_back(grad, place, t).astype(BF16)
            proj_ref[pl.ds(place, t), base + 128 : base + HD] = grad[:, 128:].astype(BF16)
        return unused

    lax.fori_loop(0, blocks, finish, 0)


def attend_back(t, high, qkv, heads_grad, hidden, logs, start, cosine, sine, buffer, after):
    rows, width = qkv.shape
    heads = width // (3 * HD)
    whole = pl.BlockSpec(memory_space=pltpu.VMEM)
    left = pl.BlockSpec((rows, heads * HD), lambda i: (0, 0))
    return pl.pallas_call(
        functools.partial(attend_back_kernel, t, heads),
        grid=(1,),
        in_specs=[pl.BlockSpec(memory_space=pltpu.SMEM)]
        + [whole, whole, left, whole, whole, whole, whole]
        + [pl.BlockSpec(memory_space=pl.ANY)] * 2,
        out_specs=pl.BlockSpec((rows, width), lambda i: (0, 0)),
        out_shape=jax.ShapeDtypeStruct(buffer.shape, BF16),
        scratch_shapes=[
            pltpu.VMEM((rows, heads * HD), F32),
            pltpu.VMEM((heads, rows), F32),
            pltpu.VMEM((heads, KBLOCK, HD), F32),
            pltpu.VMEM((heads, KBLOCK, HD), F32),
        ],
        input_output_aliases={8: 0},
        compiler_params=params(),
        cost_estimate=pl.CostEstimate(
            flops=5 * rows * rows * HD * heads,
            bytes_accessed=4 * rows * width,
            transcendentals=rows * rows * heads // 2,
        ),
        name="attend_back",
    )(high, qkv, heads_grad, hidden, logs, start, cosine, sine, buffer, after)


def add_rows(into, at, terms, terms_at, count):
    step = 32

    def body(i, unused):
        rows = pl.ds(pl.multiple_of(at + i * step, step), step)
        more = pl.ds(pl.multiple_of(terms_at + i * step, step), step)
        into[rows, :] = (into[rows, :].astype(F32) + terms[more, :].astype(F32)).astype(BF16)
        return unused

    lax.fori_loop(0, count // step, body, 0)


def closing_kernel(n, groups, *refs):
    bits, mp_bits = groups.bit_length() - 1, n.bit_length() - 1
    part_ref, cross_ref, small_ref, norm_ref, summed_ref, small_out = refs[:6]
    come = {1: refs[6], -1: refs[7]}
    keep, core_in = refs[8:10]
    stage_in = [refs[10 : 9 + bits], refs[9 + bits : 8 + 2 * bits]]
    small_in, small_sum, send, recv, load = refs[8 + 2 * bits :]
    z, group = lax.axis_index("mp"), lax.axis_index("dp")
    t = norm_ref.shape[0]
    half = keep.shape[0]
    quarter = half // 2
    ids = pl.DeviceIdType.MESH
    sems = iter(range(send.shape[0]))

    def bit_of(b):
        return lax.rem(group // 2**b, 2)

    def dp_peer(b):
        return {"dp": group + (1 - 2 * bit_of(b)) * 2**b}

    def mp_peer(b):
        return {"mp": z + (1 - 2 * lax.rem(z // 2**b, 2)) * 2**b}

    def remote(source, target, device):
        k = next(sems)
        return pltpu.make_async_remote_copy(source, target, send.at[k], recv.at[k], device, ids)

    barrier = pltpu.get_barrier_semaphore()
    for peer in [dp_peer(b) for b in range(bits)] + [mp_peer(b) for b in range(mp_bits)]:
        pl.semaphore_signal(barrier, inc=1, device_id=peer, device_id_type=ids)

    @pl.when(z + 1 < n)
    def _():
        pl.semaphore_signal(barrier, inc=1, device_id={"mp": z + 1}, device_id_type=ids)

    @pl.when(z >= 1)
    def _():
        pl.semaphore_signal(barrier, inc=1, device_id={"mp": z - 1}, device_id_type=ids)

    ends = jnp.where(z == 0, 1, 0) + jnp.where(z == n - 1, 1, 0)
    pl.semaphore_wait(barrier, bits + mp_bits + 2 - ends)

    small_peers = [dp_peer(b) for b in range(bits)] + [mp_peer(b) for b in range(mp_bits)]
    small_copies = []

    def small_step(i):
        if i == 0:
            small_sum[0] = small_ref[...]
        else:
            small_copies[i - 1].wait_recv()
            if i - 1 < bits:
                total = small_sum[i - 1] + small_in[i - 1]
            else:
                total = small_sum[i - 1]
                small_sum[i, 8:, :] = total[8:]
                total = total[:8] + small_in[i - 1, :8, :]
            small_sum[i, : total.shape[0], :] = total
        if i < len(small_peers):
            small_copies.append(remote(small_sum.at[i], small_in.at[i], small_peers[i]))
            small_copies[i].start()
        else:
            small_out[...] = small_sum[i]

    hops = {}

    def rows_at(distance):
        return pl.multiple_of(jnp.clip(z + distance, 0, n - 1) * t, t)

    def line_step(k):
        for way in (1, -1):
            buffer = come[way].at[k]
            here = (z + k < n) if way == 1 else (z >= k)
            first = (z == 0) if way == 1 else (z == n - 1)
            if k < n - 1:

                @pl.when(here & jnp.logical_not(first))
                def _():
                    hops[k + 1, way][0].wait_recv()
                    add_rows(buffer, 0, part_ref, rows_at(way * k), t) if k > 0 else None

            if k > 0:

                @pl.when(here & first)
                def _():
                    buffer[...] = part_ref[pl.ds(rows_at(way * k), t), :]

                hops[k, way] = (remote(buffer, come[way].at[k - 1], {"mp": z + way}), here)

                @pl.when(here)
                def _():
                    hops[k, way][0].start()

        if k == 0:
            step = 32

            def body(i, unused):
                rows = pl.ds(pl.multiple_of(i * step, step), step)
                total = part_ref[pl.ds(pl.multiple_of(z * t + i * step, step), step), :].astype(F32)
                for way in (1, -1):
                    first = (z == 0) if way == 1 else (z == n - 1)
                    total = total + jnp.where(first, 0.0, come[way][0, rows, :].astype(F32))
                norm_ref[rows, :] = total
                return unused

            lax.fori_loop(0, t // step, body, 0)

    mine, other = bit_of(0) * half, (1 - bit_of(0)) * half
    path = [list(range(1, bits)), list(range(bits - 1, 0, -1))]
    base = [0, quarter]
    size = quarter
    regions = [[], []]
    current = [None, None]

    def first_halving():
        own.wait()
        for p in (0, 1):
            core[p].wait_recv()
            add_rows(keep, p * quarter, core_in, p * quarter, quarter)
            halve(p, 0)

    def halve(p, s):
        b = path[p][s]
        part = quarter // 2 ** (s + 1)
        regions[p].append((base[p], 2 * part))
        away = pl.multiple_of(base[p] + (1 - bit_of(b)) * part, 32)
        current[p] = remote(keep.at[pl.ds(away, part)], stage_in[p][s], dp_peer(b))
        current[p].start()
        started.append(current[p])
        base[p] = base[p] + bit_of(b) * part

    def next_halving(s):
        for p in (0, 1):
            current[p].wait_recv()
            add_rows(keep, base[p], stage_in[p][s - 1], 0, quarter // 2**s)
            if s < bits - 1:
                halve(p, s)
            else:
                count = quarter // 2**s
                place = pl.ds(pl.multiple_of(base[p], 32), count)
                target = summed_ref.at[pl.ds(pl.multiple_of(mine + base[p], 32), count)]
                local = pltpu.make_async_copy(keep.at[place], target, load.at[1 + p])
                local.start()
                current[p] = remote(keep.at[place], target, dp_peer(path[p][s - 1]))
                current[p].start()
                started.append(current[p])
                locals_.append(local)

    def doubling(s):
        for p in (0, 1):
            current[p].wait_recv()
            if s == bits - 2:
                locals_[p].wait()
            at, count = regions[p][s]
            rows = summed_ref.at[pl.ds(pl.multiple_of(mine + at, 32), count)]
            current[p] = remote(rows, rows, dp_peer(path[p][s - 1] if s > 0 else 0))
            current[p].start()
            started.append(current[p])

    started, locals_ = [], []
    core = [
        remote(
            cross_ref.at[pl.ds(pl.multiple_of(other + p * quarter, 32), quarter)],
            core_in.at[pl.ds(p * quarter, quarter)],
            dp_peer(0),
        )
        for p in (0, 1)
    ]
    own = pltpu.make_async_copy(cross_ref.at[pl.ds(pl.multiple_of(mine, 32), half)], keep, load.at[0])
    for copy in core:
        copy.start()
    own.start()
    line_step(n - 1)
    small_step(0)

    sums = [first_halving]
    sums += [functools.partial(next_halving, s) for s in range(1, bits)]
    sums += [functools.partial(doubling, s) for s in range(bits - 2, -1, -1)]
    lines = list(range(n - 2, -1, -1))
    smalls = list(range(1, bits + mp_bits + 1))
    for at, step in enumerate(sums):
        step()
        if at in (0, bits - 1) or at >= bits:
            if lines:
                line_step(lines.pop(0))
        if smalls:
            small_step(smalls.pop(0))
    for k in lines:
        line_step(k)
    for i in smalls:
        small_step(i)
    for p in (0, 1):
        current[p].wait_recv()
    for copy in core + started + small_copies:
        copy.wait_send()
    for copy, here in hops.values():

        @pl.when(here)
        def _():
            copy.wait_send()


def closing_sums(n, groups, part, cross, small):
    rows, d = part.shape
    width = cross.shape[1]
    t, half = rows // n, d // 2
    bits, mp_bits = groups.bit_length() - 1, n.bit_length() - 1
    stages = [pltpu.VMEM((half // 2 // 2**s, width), BF16) for s in range(1, bits)]
    copies = 2 + 2 * (bits - 1) + 2 + 2 * (bits - 1) + 2 * (n - 1) + bits + mp_bits
    whole = pl.BlockSpec(memory_space=pltpu.VMEM)
    return pl.pallas_call(
        functools.partial(closing_kernel, n, groups),
        in_specs=[whole, pl.BlockSpec(memory_space=pl.ANY), whole],
        out_specs=[whole, pl.BlockSpec(memory_space=pl.ANY), whole],
        out_shape=[
            jax.ShapeDtypeStruct((t, d), F32),
            jax.ShapeDtypeStruct((d, width), BF16),
            jax.ShapeDtypeStruct(small.shape, F32),
        ],
        scratch_shapes=[pltpu.VMEM((n, t, d), BF16)] * 2
        + [pltpu.VMEM((half, width), BF16)] * 2
        + stages * 2
        + [pltpu.VMEM((bits + mp_bits,) + small.shape, F32), pltpu.VMEM((bits + mp_bits + 1,) + small.shape, F32)]
        + [pltpu.SemaphoreType.DMA((copies,))] * 2
        + [pltpu.SemaphoreType.DMA((3,))],
        compiler_params=pltpu.CompilerParams(
            vmem_limit_bytes=VMEM_LIMIT, collective_id=0, has_side_effects=True
        ),
        name="closing_sums",
    )(part, cross, small)


def scatter_sum(part, own, z, n):
    right = left = None
    for k in range(n - 1, 0, -1):
        for_right, for_left = part(z + k), part(z - k)
        if right is not None:
            for_right = (for_right.astype(F32) + right.astype(F32)).astype(BF16)
            for_left = (for_left.astype(F32) + left.astype(F32)).astype(BF16)
        right = lax.ppermute(for_right, "mp", [(i, i + 1) for i in range(n - k)])
        left = lax.ppermute(for_left, "mp", [(i, i - 1) for i in range(k, n)])
    return own + right.astype(F32) + left.astype(F32)


def exchange(part, own, z, n):
    came = [None] * (2 * n - 1)
    came[n - 1] = own
    for k in range(1, n):
        came[n - 1 - k] = lax.ppermute(part(z + k), "mp", [(i, i + k) for i in range(n - k)])
        came[n - 1 + k] = lax.ppermute(part(z - k), "mp", [(i, i - k) for i in range(k, n)])
    return lax.dynamic_slice_in_dim(jnp.stack(came), n - 1 - z, n, axis=0)


def document_starts(row_lengths, length):
    count = row_lengths.shape[0]
    before = np.tri(count, k=-1, dtype=np.int32)
    starts = jnp.sum(before * row_lengths[None, :], axis=1)
    places = jnp.arange(length, dtype=jnp.int32)
    return jnp.max(jnp.where(starts[None, :] <= places[:, None], starts[None, :], 0), axis=1)


def per_device(
    tokens, seq_lengths, attn_gain, attn_shift, mlp_gain, mlp_shift, in_weight, in_bias, out_weight, out_bias,
    up_weight, up_bias, down_weight, down_bias, cotangent,
):
    n, groups = lax.axis_size("mp"), lax.axis_size("dp")
    z, group = lax.axis_index("mp"), lax.axis_index("dp")
    t, d = tokens.shape[1:]
    length = n * t
    local_heads = in_weight.shape[1]
    in_width, heads_width, hidden = local_heads * 3 * HD, local_heads * HD, up_weight.shape[1]

    own_tokens = tokens[0].astype(F32)
    centred = own_tokens - jnp.mean(own_tokens, axis=-1, keepdims=True)
    spread = lax.rsqrt(jnp.mean(centred * centred, axis=-1, keepdims=True) + NORM_EPS)
    normed = centred * spread
    own_grad = cotangent[0]

    flat_in = lax.optimization_barrier(in_weight.reshape(d, in_width))
    share = out_weight.shape[0] // groups
    out_full = lax.all_gather(
        lax.dynamic_slice_in_dim(out_weight, group * share, share, axis=0), ("mp", "dp"), axis=0, tiled=True
    )

    starts = document_starts(seq_lengths[0], length)
    first_of_block = starts[::t]
    low = first_of_block // KBLOCK
    last_key = (jnp.arange(length // KBLOCK, dtype=jnp.int32) + 1) * KBLOCK - 1
    high = jnp.sum((first_of_block[None, :] <= last_key[:, None]).astype(jnp.int32), axis=1)
    offsets = jnp.arange(length, dtype=jnp.int32) - starts
    inverse = 10000.0 ** (-jnp.arange(0, ROT, 2).astype(F32) / ROT)
    angles = offsets.astype(F32)[:, None] * inverse[None, :]
    cosine, sine = jnp.cos(angles), jnp.sin(angles)
    cosine = jnp.concatenate([cosine, cosine, jnp.ones((length, 128 - ROT), F32)], axis=1)
    sine = jnp.concatenate([-sine, sine, jnp.zeros((length, 128 - ROT), F32)], axis=1)
    start_row = starts[None, :]

    vectors = jnp.stack([attn_gain, attn_shift, mlp_gain, mlp_shift] * 2)
    x_rows, qkv, joint, slope, down_part = opening(
        n, normed.astype(BF16), flat_in, up_weight, down_weight, vectors, in_bias.reshape(1, in_width),
        up_bias[None, :], cosine, sine,
    )
    g_rows = lax.all_gather(after(own_grad, slope, out_full), "mp", axis=0, tiled=True)
    joint, logs = attend(t, low, qkv, start_row, joint)

    def rows_for(array):
        def part(position):
            return lax.dynamic_slice_in_dim(array, jnp.clip(position, 0, n - 1) * t, t, axis=0)

        return part

    heads_out = joint[:, :heads_width]
    heads_mine = exchange(rows_for(heads_out), rows_for(heads_out)(z), z, n)
    heads_mine = heads_mine.transpose(1, 0, 2).reshape(t, n * heads_width)
    attn_branch = dot(heads_mine, out_full) + out_bias
    mlp_branch = scatter_sum(rows_for(down_part), rows_for(down_part)(z).astype(F32), z, n) + down_bias
    block_out = (own_tokens + attn_branch + mlp_branch).astype(BF16)
    squares = jnp.stack([jnp.sum(attn_branch * attn_branch), jnp.sum(mlp_branch * mlp_branch)])

    back = up_back(in_width, heads_width, g_rows, down_weight, slope)
    heads_grad = dot(g_rows, out_weight, NT).astype(BF16)
    out_down_grad = dot(joint, g_rows, TN).astype(BF16)
    back = attend_back(
        t, high, qkv, heads_grad, joint, logs, start_row, cosine, sine, back, out_down_grad
    )
    out_down_grad = lax.psum(out_down_grad, "dp")
    norm_part = (
        dot(back[:, :in_width], flat_in, NT) * attn_gain + dot(back[:, in_width:], up_weight, NT) * mlp_gain
    ).astype(BF16)
    cross, row_sums, total = cross_products(heads_width, x_rows, back, flat_in, up_weight)
    total = total[0]
    attn_sums = row_sums[:, 0:2].T
    mlp_sums = row_sums[:, 2:4].T
    bias_sum = jnp.sum(own_grad.astype(F32), axis=0)
    small = jnp.concatenate(
        [
            attn_sums,
            mlp_sums,
            bias_sum[None],
            jnp.pad(squares, (0, d - 2))[None],
            jnp.zeros((2, d), F32),
            jnp.pad(total[:in_width], (0, d - in_width))[None],
            jnp.pad(total[in_width:], (0, d - hidden))[None],
            jnp.zeros((6, d), F32),
        ]
    )
    norm_grad, cross, small = closing_sums(n, groups, norm_part, cross, small)
    mean_grad = jnp.mean(norm_grad, axis=-1, keepdims=True)
    mean_normed = jnp.mean(norm_grad * normed, axis=-1, keepdims=True)
    tokens_grad = (own_grad.astype(F32) + spread * (norm_grad - mean_grad - normed * mean_normed)).astype(BF16)
    in_total, up_total = small[8, :in_width], small[9, :hidden]
    in_cross = lax.optimization_barrier(cross[:, :in_width].reshape(d, local_heads, 3 * HD))
    grad_in_weight = (
        in_cross.astype(F32) * attn_gain[:, None, None]
        + attn_shift[:, None, None] * in_total.reshape(local_heads, 3 * HD)[None]
    )
    grad_up_weight = cross[:, in_width:].astype(F32) * mlp_gain[:, None] + mlp_shift[:, None] * up_total[None, :]
    element_count = float(groups * n * t * d)
    return (
        block_out[None],
        tokens_grad[None],
        small[0],
        small[1],
        small[2],
        small[3],
        grad_in_weight,
        in_total.reshape(local_heads, 3 * HD),
        out_down_grad[:heads_width].astype(F32),
        small[4],
        grad_up_weight,
        up_total,
        out_down_grad[heads_width:].astype(F32),
        small[4],
        jnp.sqrt(small[5, :2] / element_count),
    )


def solution(mesh):
    rows, weights = P("dp", "mp", None), P(None, "mp", None)
    in_specs = (
        rows, P("dp", None), P(), P(), P(), P(), weights, P("mp", None), P("mp", None), P(),
        P(None, "mp"), P("mp"), P("mp", None), P(), rows,
    )
    out_specs = (
        rows, rows, P(), P(), P(), P(), weights, P("mp", None), P("mp", None), P(),
        P(None, "mp"), P("mp"), P("mp", None), P(), P(),
    )
    return jax.shard_map(per_device, mesh=mesh, in_specs=in_specs, out_specs=out_specs, check_vma=False)
```

time: 1070 us -> 1060 us (level)
  Pallas kernels: 137 us -> 546 us
  other arithmetic: 225 us -> 88.1 us
  matrix products: 217 us -> 91.4 us
  blocking collectives: 88.9 us -> 0 us
  starting transfers between devices: 84.5 us -> 43.2 us
  waiting for transfers between devices: 250 us -> 212 us
  local copies, waits for them, and re-layouts: 44.6 us -> 60.8 us
    pallas_call x10 -> x7, Pallas kernels: 137 us -> 546 us  [the longest x1 227 us: closing_sums(): pl.pallas_call(functools.partial(closing_kernel, n, groups), in_specs=[wh...]
    ppermute x6 -> x3, waiting for transfers between devices: 0.02 us -> 183 us  [scatter_sum(): right = lax.ppermute(for_right, 'mp', [(i, i + 1) for i in range(n - k)])]
    ppermute x12 -> x0, waiting for transfers between devices: 128 us -> none  [the longest x6 128 us: gather_slots(): left = lax.ppermute(left, 'mp', [(i, i - 1) for i in range(1, n - k + 1)])]
    dot_general x11 -> x5, matrix products: 217 us -> 91.4 us  [dot(): return lax.dot_general(a, b, dims, preferred_element_type=F32)]
    reduce_sum x4 -> x2, other arithmetic: 114 us -> 6.44 us  [the longest x1 5.47 us: per_device(): jnp.sum(mlp_branch * mlp_branch)]
    psum x2 -> x0, blocking collectives: 88.9 us -> none  [the longest x1 64.6 us: per_device(): lax.psum(small, ('dp', 'mp'))]
    ppermute x3, waiting for transfers between devices: 71.3 us -> 0.01 us  [exchange(): lax.ppermute(part(z - k), 'mp', [(i, i - k) for i in range(k, n)])]
    ppermute x3, waiting for transfers between devices: 49.7 us -> 17.9 us  [exchange(): lax.ppermute(part(z + k), 'mp', [(i, i + k) for i in range(n - k)])]
  transfers between devices with their start and end apart: 32 -> 15, of which waited for: 6 -> 7; matrix products, arithmetic and copies ran while one was open for 40% -> 15% of each run, Pallas kernels for 13% -> 42%
where the time goes in v2:
time: 1060 us
  Pallas kernels  546 us (52%)
  waiting for transfers between devices  212 us (20%)
  matrix products  91.4 us (9%)
  other arithmetic  88.1 us (8%)
  local copies, waits for them, and re-layouts  60.8 us (6%)
  starting transfers between devices  43.2 us (4%)
  between operations  14.5 us (1%)
    pallas_call x1, Pallas kernels, closing_sums(): pl.pallas_call(functools.partial(closing_kernel, n, groups), in_specs=[wh...  227 us
    pallas_call x1, Pallas kernels, opening(): pl.pallas_call(functools.partial(opening_kernel, n, heads), in_specs=[any...  195 us
    ppermute x3, waiting for transfers between devices, scatter_sum(): right = lax.ppermute(for_right, 'mp', [(i, i + 1) for i in range(n - k)])  183 us
    dot_general x5, matrix products, dot(): return lax.dot_general(a, b, dims, preferred_element_type=F32)  91.4 us
    pallas_call x1, Pallas kernels, cross_products(): pl.pallas_call(functools.partial(cross_kernel, heads_tile), grid=(d // ti...  45.8 us
    pallas_call x1, Pallas kernels, attend_back(): pl.pallas_call(functools.partial(attend_back_kernel, t, heads), grid=(1,)...  30.8 us
    pallas_call x1, Pallas kernels, up_back(): pl.pallas_call(up_back_kernel, grid=(rows // block, width // tile), in_sp...  24.6 us
    ppermute x3, starting transfers between devices, scatter_sum(): right = lax.ppermute(for_right, 'mp', [(i, i + 1) for i in range(n - k)])  23.9 us
  transfers between devices with their start and end apart: 15, of which 7 were waited for; matrix products, arithmetic and copies ran while one was open for 15% of the time, Pallas kernels for 42%

profile of v2, /device:TPU:0, one launch (start us, length us, event | category | flops | bytes accessed | tf_op | source)
XLA Modules:
  0.0 1056.3 jit_solution(11385842928328772651)
XLA Ops:
  32.5 195.3 %opening.1 = (bf16[2048,2048]{1,0:T(8,128)(2,1)}, bf16[2048,1536]{1,0:T(8,128)(2,1)}, bf16[2048,2560]{1,0:T(8,128)(2,1)}, bf16[2048,2048]{1,0:T(8,128)(2,1)}, bf16[2048,2048]{1,0:T(8,128)(2,1)}) custom-call(bf16[512,2048]{1,0:T(8,128)(2,1)} %fusion.9.refs_0_, bf16[2048,1536]{1,0:T(8,128)(2,1)} %bitcast.101, bf16[2048,2048]{1,0:T(8,128)(2,1)} %up_ref.1, ...), custom_call_target="tpu_custom_call" | custom-call | flops 755914244096 | bytes 209715200 | tf_op jit(solution)/shard_map/opening/pallas_call | solution.py:223
  238.6 82.2 %collective-permute-done.6 = bf16[512,2048]{1,0:T(8,128)(2,1)} collective-permute-done((bf16[512,2048]{1,0:T(8,128)(2,1)}, bf16[512,2048]{1,0:T(8,128)(2,1)}, u32[]{:S(2)}, u32[]{:S(2)}) %collective-permute-start.6) | collective-permute-done | bytes 2097184 | tf_op jit(solution)/shard_map/ppermute | solution.py:773
  325.2 6.1 collective-permute-start.7
  332.7 84.9 %collective-permute-done.7 = bf16[512,2048]{1,0:T(8,128)(2,1)} collective-permute-done((bf16[512,2048]{1,0:T(8,128)(2,1)}, bf16[512,2048]{1,0:T(8,128)(2,1)}, u32[]{:S(2)}, u32[]{:S(2)}) %collective-permute-start.7) | collective-permute-done | bytes 2097184 | tf_op jit(solution)/shard_map/ppermute | solution.py:773
  417.6 7.8 add_convert_fusion.3
  427.4 22.7 %attend.1 = (bf16[2048,2560]{1,0:T(8,128)(2,1)}, f32[2,2048]{1,0:T(2,128)}) custom-call(s32[4]{0:T(128)} %and_select_fusion.low_ref, bf16[2048,1536]{1,0:T(8,128)(2,1)} %get-tuple-element.28.qkv_ref, s32[1,2048]{1,0:T(1,128)} %bitcast.105, bf16[2048,2560]{1,0:T(8,128)(2,1)} %get-tuple-element.29.held_ref), custom_call_target="tpu_custom_call", output_to_operand_aliasing={{0}: (3, {})} | custom-call | flops 4294967296 | bytes 6291456 | tf_op jit(solution)/shard_map/attend/pallas_call | solution.py:403
  474.6 8.9 collective-permute-done.1
  485.8 6.4 collective-permute-done.2
  495.4 15.2 %collective-permute-start.8 = (bf16[512,2048]{1,0:T(8,128)(2,1)}, bf16[512,2048]{1,0:T(8,128)(2,1)}, u32[]{:S(2)}, u32[]{:S(2)}) collective-permute-start(bf16[512,2048]{1,0:T(8,128)(2,1)} %get-tuple-element.45), channel_id=1, source_target_pairs={{0,1},{1,2},{2,3},{4,5},{5,6},{6,7},{8,9},{9,10},{10,11},{12,13},{... | collective-permute-start | bytes 6291464 | tf_op jit(solution)/shard_map/ppermute | solution.py:773
  522.1 7.7 fusion.22
  529.8 15.5 %collective-permute-done.8 = bf16[512,2048]{1,0:T(8,128)(2,1)} collective-permute-done((bf16[512,2048]{1,0:T(8,128)(2,1)}, bf16[512,2048]{1,0:T(8,128)(2,1)}, u32[]{:S(2)}, u32[]{:S(2)}) %collective-permute-start.8) | collective-permute-done | bytes 2097184 | tf_op jit(solution)/shard_map/ppermute | solution.py:773
  545.3 11.9 %collective-permute-done.11 = bf16[512,2048]{1,0:T(8,128)(2,1)} collective-permute-done((bf16[512,2048]{1,0:T(8,128)(2,1)}, bf16[512,2048]{1,0:T(8,128)(2,1)}, u32[]{:S(2)}, u32[]{:S(2)}) %collective-permute-start.11) | collective-permute-done | bytes 2097184 | tf_op jit(solution)/shard_map/ppermute | solution.py:774
  564.6 9.1 convolution_convert_fusion.1.grad_ref
  573.8 24.6 %up_back.1.held_ref = bf16[2048,3584]{1,0:T(8,128)(2,1)} custom-call(bf16[2048,2048]{1,0:T(8,128)(2,1)} %all-gather.5.cloned.1.call-done.g_ref, bf16[2048,2048]{1,0:T(8,128)(2,1)} %w_ref.1, bf16[2048,2048]{1,0:T(8,128)(2,1)} %get-tuple-element.32.refs_1_.slope_ref), custom_call_target="tpu_custom_call" | custom-call | flops 17179869184 | bytes 33554432 | tf_op jit(solution)/shard_map/up_back/pallas_call | solution.py:261
  598.3 28.2 %convolution_convert_fusion.after_ref = bf16[2560,2048]{1,0:T(8,128)(2,1)} fusion(bf16[2048,2560]{1,0:T(8,128)(2,1)} %get-tuple-element.30.out_ref, bf16[2048,2048]{1,0:T(8,128)(2,1)} %all-gather.5.cloned.1.call-done.g_ref), kind=kOutput, calls=%fused_computation.3 | convolution fusion | flops 21480079360 | bytes 29360128 | tf_op jit(solution)/shard_map/dot_general | solution.py:26
  626.6 30.8 %attend_back.1.back_ref = bf16[2048,3584]{1,0:T(8,128)(2,1)} custom-call(s32[8]{0:T(128)} %convert_reduce_fusion.2.high_ref, bf16[2048,1536]{1,0:T(8,128)(2,1)} %get-tuple-element.28.qkv_ref, bf16[2048,512]{1,0:T(8,128)(2,1)} %convolution_convert_fusion.1.grad_ref, bf16[2048,2560]{1,0:T(8,128)(2,1)} %get-tuple-element.30.out_ref, ...), custom_call_target="tpu_custom_call", output_to_operand_aliasing={{}: (8, {})} | custom-call | flops 10737418240 | bytes 12582912 | tf_op jit(solution)/shard_map/attend_back/pallas_call | solution.py:498
  657.4 19.6 %fusion.1 = f32[2048,2048]{1,0:T(8,128)} fusion(bf16[2048,1536]{1,0:T(8,128)(2,1)} %bitcast.102, bf16[2048,3584]{1,0:T(8,128)(2,1)} %attend_back.1.back_ref), kind=kOutput, calls=%fused_computation.6 | convolution fusion | flops 12884901888 | bytes 29360128 | tf_op jit(solution)/shard_map/dot_general | solution.py:26
  677.0 45.8 %cross.1 = (bf16[2048,3584]{1,0:T(8,128)(2,1)}, f32[2048,128]{1,0:T(8,128)}, f32[8,3584]{1,0:T(8,128)}) custom-call(bf16[2048,2048]{1,0:T(8,128)(2,1)} %get-tuple-element.34.x_ref, bf16[2048,3584]{1,0:T(8,128)(2,1)} %attend_back.1.back_ref, bf16[2048,1536]{1,0:T(8,128)(2,1)} %bitcast.103, bf16[2048,2048]{1,0:T(8,128)(2,1)} %up_ref.1), custom_call_target="tpu_custom_call" | custom-call | flops 30064771072 | bytes 52428800 | tf_op jit(solution)/shard_map/cross/pallas_call | solution.py:321
  725.1 26.7 %add_convert_fusion.refs_0_ = bf16[2048,2048]{1,0:T(8,128)(2,1)} fusion(f32[2048,2048]{1,0:T(8,128)} %fusion.1, bf16[2048,2048]{1,0:T(8,128)(2,1)} %up_ref.1, bf16[2048,3584]{1,0:T(8,128)(2,1)} %attend_back.1.back_ref, f32[2048]{0:T(1024)S(1)} %copy-done.10, f32[2048]{0:T(1024)S(1)} %copy-done.14), kind=kOutput, calls=%fused_computation.1 | convolution fusion | flops 17196646400 | bytes 41959424 | tf_op jit(solution)/shard_map/dot_general | solution.py:26
  754.8 226.6 %closing_sums.1 = (f32[512,2048]{1,0:T(8,128)}, bf16[2048,3584]{1,0:T(8,128)(2,1)}, f32[16,2048]{1,0:T(8,128)}) custom-call(bf16[2048,2048]{1,0:T(8,128)(2,1)} %add_convert_fusion.refs_0_, bf16[2048,3584]{1,0:T(8,128)(2,1)} %get-tuple-element.35.refs_1_, f32[16,2048]{1,0:T(8,128)} %concatenate.11.refs_2_), custom_call_target="tpu_custom_call" | custom-call | tf_op jit(solution)/shard_map/closing_sums/pallas_call | solution.py:744
  987.3 13.5 %reshape.104 = bf16[2048,2,768]{2,1,0:T(2,128)(2,1)} reshape(bf16[2048,1536]{1,0:T(8,128)(2,1)} %slice.81) | data formatting | bytes 12582912 | tf_op jit(solution)/shard_map/reshape | solution.py:885
  1013.3 9.5 multiply_add_fusion.1
  1022.8 10.3 multiply_add_fusion
  1037.2 11.7 %slice_convert_fusion = f32[2048,2048]{1,0:T(8,128)} fusion(bf16[2560,2048]{1,0:T(8,128)(2,1)} %all-reduce.4.cloned.1.call-done), kind=kLoop, calls=%fused_computation.4 | loop fusion | flops 4194304 | bytes 25165824 | tf_op jit(solution)/shard_map/convert_element_type | solution.py:905
  (153 shorter events, 120.8 us)
Async XLA Ops:
  7.2 221.9 %all-gather.3.cloned.1.call-start = ((), (), s32[]{:S(2)}) async-start(), calls=%async_computation | async-start | bytes 8650752 | tf_op jit(solution)/shard_map/all_gather | solution.py:814
  9.5 555.1 %all-gather.5.cloned.1.call-start = ((), (), s32[]{:S(2)}) async-start(), calls=%async_computation.1 | async-start | bytes 10485760 | tf_op jit(solution)/shard_map/all_gather | solution.py:836
  32.5 195.3 %copy-start.4 = (bf16[1,512,2048]{2,1,0:T(8,128)(2,1)S(1)}, bf16[1,512,2048]{2,1,0:T(8,128)(2,1)}, u32[]{:S(2)}) copy-start(bf16[1,512,2048]{2,1,0:T(8,128)(2,1)} %param.30) | copy-start | bytes 6291460
  234.0 86.8 %collective-permute-start.6 = (bf16[512,2048]{1,0:T(8,128)(2,1)}, bf16[512,2048]{1,0:T(8,128)(2,1)}, u32[]{:S(2)}, u32[]{:S(2)}) collective-permute-start(bf16[512,2048]{1,0:T(8,128)(2,1)} %get-tuple-element.47), channel_id=1, source_target_pairs={{0,1},{4,5},{8,9},{12,13},{16,17},{20,21},{24,25},{28,29}} | collective-permute-start | bytes 6291464 | tf_op jit(solution)/shard_map/ppermute | solution.py:773
  236.6 96.1 %collective-permute-start.9 = (bf16[512,2048]{1,0:T(8,128)(2,1)}, bf16[512,2048]{1,0:T(8,128)(2,1)}, u32[]{:S(2)}, u32[]{:S(2)}) collective-permute-start(bf16[512,2048]{1,0:T(8,128)(2,1)} %get-tuple-element.48), channel_id=1, source_target_pairs={{3,2},{7,6},{11,10},{15,14},{19,18},{23,22},{27,26},{31,30}} | collective-permute-start | bytes 6291464 | tf_op jit(solution)/shard_map/ppermute | solution.py:774
  325.2 92.4 %collective-permute-start.7 = (bf16[512,2048]{1,0:T(8,128)(2,1)}, bf16[512,2048]{1,0:T(8,128)(2,1)}, u32[]{:S(2)}, u32[]{:S(2)}) collective-permute-start(bf16[512,2048]{1,0:T(8,128)(2,1)} %add_convert_fusion.4), channel_id=1, source_target_pairs={{0,1},{1,2},{4,5},{5,6},{8,9},{9,10},{12,13},{13,14},{16,17},{17,1... | collective-permute-start | bytes 6291464 | tf_op jit(solution)/shard_map/ppermute | solution.py:773
  425.3 85.3 %collective-permute-start.10 = (bf16[512,2048]{1,0:T(8,128)(2,1)}, bf16[512,2048]{1,0:T(8,128)(2,1)}, u32[]{:S(2)}, u32[]{:S(2)}) collective-permute-start(bf16[512,2048]{1,0:T(8,128)(2,1)} %get-tuple-element.46), channel_id=1, source_target_pairs={{2,1},{3,2},{6,5},{7,6},{10,9},{11,10},{14,13},{15,14},{18,17},{19... | collective-permute-start | bytes 6291464 | tf_op jit(solution)/shard_map/ppermute | solution.py:774
  456.5 15.7 %collective-permute-start = (bf16[512,512]{1,0:T(8,128)(2,1)}, bf16[512,512]{1,0:T(8,128)(2,1)}, u32[]{:S(2)}, u32[]{:S(2)}) collective-permute-start(bf16[512,512]{1,0:T(8,128)(2,1)} %get-tuple-element.55), channel_id=1, source_target_pairs={{0,3},{4,7},{8,11},{12,15},{16,19},{20,23},{24,27},{28,31}} | collective-permute-start | bytes 1572872 | tf_op jit(solution)/shard_map/ppermute | solution.py:782
  458.6 24.8 %collective-permute-start.1 = (bf16[512,512]{1,0:T(8,128)(2,1)}, bf16[512,512]{1,0:T(8,128)(2,1)}, u32[]{:S(2)}, u32[]{:S(2)}) collective-permute-start(bf16[512,512]{1,0:T(8,128)(2,1)} %get-tuple-element.54), channel_id=1, source_target_pairs={{0,2},{1,3},{4,6},{5,7},{8,10},{9,11},{12,14},{13,15},{16,18},{17,... | collective-permute-start | bytes 1572872 | tf_op jit(solution)/shard_map/ppermute | solution.py:782
  464.5 27.7 %collective-permute-start.2 = (bf16[512,512]{1,0:T(8,128)(2,1)}, bf16[512,512]{1,0:T(8,128)(2,1)}, u32[]{:S(2)}, u32[]{:S(2)}) collective-permute-start(bf16[512,512]{1,0:T(8,128)(2,1)} %get-tuple-element.53), channel_id=1, source_target_pairs={{0,1},{1,2},{2,3},{4,5},{5,6},{6,7},{8,9},{9,10},{10,11},{12,13},{... | collective-permute-start | bytes 1572872 | tf_op jit(solution)/shard_map/ppermute | solution.py:782
  466.6 27.7 %collective-permute-start.3 = (bf16[512,512]{1,0:T(8,128)(2,1)}, bf16[512,512]{1,0:T(8,128)(2,1)}, u32[]{:S(2)}, u32[]{:S(2)}) collective-permute-start(bf16[512,512]{1,0:T(8,128)(2,1)} %get-tuple-element.52), channel_id=1, source_target_pairs={{1,0},{2,1},{3,2},{5,4},{6,5},{7,6},{9,8},{10,9},{11,10},{13,12},{... | collective-permute-start | bytes 1572872 | tf_op jit(solution)/shard_map/ppermute | solution.py:783
  472.2 44.2 %collective-permute-start.4 = (bf16[512,512]{1,0:T(8,128)(2,1)S(1)}, bf16[512,512]{1,0:T(8,128)(2,1)S(1)}, u32[]{:S(2)}, u32[]{:S(2)}) collective-permute-start(bf16[512,512]{1,0:T(8,128)(2,1)S(1)} %get-tuple-element.51), channel_id=1, source_target_pairs={{2,0},{3,1},{6,4},{7,5},{10,8},{11,9},{14,12},{15,13},{18,16},{19,... | collective-permute-start | bytes 1572872 | tf_op jit(solution)/shard_map/ppermute | solution.py:783
  483.4 33.0 %collective-permute-start.5 = (bf16[512,512]{1,0:T(8,128)(2,1)S(1)}, bf16[512,512]{1,0:T(8,128)(2,1)S(1)}, u32[]{:S(2)}, u32[]{:S(2)}) collective-permute-start(bf16[512,512]{1,0:T(8,128)(2,1)S(1)} %get-tuple-element.50), channel_id=1, source_target_pairs={{3,0},{7,4},{11,8},{15,12},{19,16},{23,20},{27,24},{31,28}} | collective-permute-start | bytes 1572872 | tf_op jit(solution)/shard_map/ppermute | solution.py:783
  495.4 49.8 %collective-permute-start.8 = (bf16[512,2048]{1,0:T(8,128)(2,1)}, bf16[512,2048]{1,0:T(8,128)(2,1)}, u32[]{:S(2)}, u32[]{:S(2)}) collective-permute-start(bf16[512,2048]{1,0:T(8,128)(2,1)} %get-tuple-element.45), channel_id=1, source_target_pairs={{0,1},{1,2},{2,3},{4,5},{5,6},{6,7},{8,9},{9,10},{10,11},{12,13},{... | collective-permute-start | bytes 6291464 | tf_op jit(solution)/shard_map/ppermute | solution.py:773
  515.1 42.1 %collective-permute-start.11 = (bf16[512,2048]{1,0:T(8,128)(2,1)}, bf16[512,2048]{1,0:T(8,128)(2,1)}, u32[]{:S(2)}, u32[]{:S(2)}) collective-permute-start(bf16[512,2048]{1,0:T(8,128)(2,1)} %add_convert_fusion.1), channel_id=1, source_target_pairs={{1,0},{2,1},{3,2},{5,4},{6,5},{7,6},{9,8},{10,9},{11,10},{13,12},{... | collective-permute-start | bytes 6291464 | tf_op jit(solution)/shard_map/ppermute | solution.py:774
  522.1 35.1 %copy-start.2 = (bf16[1,512,2048]{2,1,0:T(8,128)(2,1)S(1)}, bf16[1,512,2048]{2,1,0:T(8,128)(2,1)}, u32[]{:S(2)}) copy-start(bf16[1,512,2048]{2,1,0:T(8,128)(2,1)} %param.16) | copy-start | bytes 6291460
  522.1 35.1 %copy-start.26 = (f32[2048]{0:T(1024)S(1)}, f32[2048]{0:T(1024)}, u32[]{:S(2)}) copy-start(f32[2048]{0:T(1024)} %param.29) | copy-start | bytes 24580
  522.1 35.1 %copy-start.27 = (f32[2048]{0:T(1024)S(1)}, f32[2048]{0:T(1024)}, u32[]{:S(2)}) copy-start(f32[2048]{0:T(1024)} %param.25) | copy-start | bytes 24580
  657.4 375.7 %all-reduce.4.cloned.1.call-start = ((), (), s32[]{:S(2)}) async-start(), calls=%async_computation.2 | async-start | bytes 20971520 | tf_op jit(solution)/shard_map/psum | solution.py:859
  725.1 28.3 %copy-start.22 = (f32[2048]{0:T(1024)S(1)}, f32[2048]{0:T(1024)}, u32[]{:S(2)}) copy-start(f32[2048]{0:T(1024)} %convert_reduce_fusion) | copy-start | bytes 24580
  725.1 28.3 %copy-start.23 = (f32[2048]{0:T(1024)S(1)}, f32[2048]{0:T(1024)}, u32[]{:S(2)}) copy-start(f32[2048]{0:T(1024)} %select_maximum_fusion) | copy-start | bytes 24580
  987.3 16.2 %copy-start.21 = (f32[512]{0:T(512)S(1)}, f32[512]{0:T(512)}, u32[]{:S(2)}) copy-start(f32[512]{0:T(512)} %copy-done.20) | copy-start | bytes 6148
  1003.5 19.3 %copy-start.19 = (f32[1,2048]{1,0:T(1,128)}, f32[1,2048]{1,0:T(1,128)S(1)}, u32[]{:S(2)}) copy-start(f32[1,2048]{1,0:T(1,128)S(1)} %get-tuple-element.58) | copy-start | bytes 24580
  1003.5 45.4 %copy-start.24 = (f32[1,2048]{1,0:T(1,128)}, f32[1,2048]{1,0:T(1,128)S(1)}, u32[]{:S(2)}) copy-start(f32[1,2048]{1,0:T(1,128)S(1)} %get-tuple-element.59) | copy-start | bytes 24580
  (24 other events, 165.7 us)
Sparse Core Ops, SparseCore 0:
  11.5 104.4 all-gather.2
  229.3 233.4 all-gather.4
  724.6 224.8 all-reduce.3

commit v3 on v2

--- a/solution.py
+++ b/solution.py
@@ -63,6 +63,55 @@
     return picked
 
 
+def greet_line(z, n):
+    barrier = pltpu.get_barrier_semaphore()
+    for way in (1, -1):
+
+        @pl.when((z + way >= 0) & (z + way < n))
+        def _():
+            pl.semaphore_signal(barrier, inc=1, device_id={"mp": z + way}, device_id_type=pl.DeviceIdType.MESH)
+
+    pl.semaphore_wait(barrier, 2 - jnp.where(z == 0, 1, 0) - jnp.where(z == n - 1, 1, 0))
+
+
+def line_gather(z, n, t, own, rows_ref, send, recv):
+    hops = {}
+    for k in range(1, n):
+        for way in (1, -1):
+            origin, there = z - way * (k - 1), z + way
+            goes = (origin >= 0) & (origin < n) & (there >= 0) & (there < n)
+            rows = rows_ref.at[pl.ds(pl.multiple_of(jnp.clip(origin, 0, n - 1) * t, t), t)]
+            at = 2 * (k - 1) + (way < 0)
+            copy = pltpu.make_async_remote_copy(
+                own if k == 1 else rows, rows, send.at[at], recv.at[at], {"mp": there}, pl.DeviceIdType.MESH
+            )
+            arrives = (z - way * k >= 0) & (z - way * k < n)
+            hops[k, way] = (copy, goes, arrives)
+    return hops
+
+
+def gather_step(hops, k):
+    for way in (1, -1):
+        copy, goes, _ = hops[k, way]
+        pl.when(goes)(copy.start)
+
+
+def gather_wait(hops, k):
+    for way in (1, -1):
+        copy, _, arrives = hops[k, way]
+        pl.when(arrives)(copy.wait_recv)
+
+
+def gather_end(hops):
+    for copy, goes, _ in hops.values():
+        pl.when(goes)(copy.wait_send)
+
+
+def slot_positions(z, n):
+    order = arrival_order(n)
+    return [across(z, n, [order[zz][s] for zz in range(n)]) for s in range(n)]
+
+
 def opening_kernel(n, heads, *refs):
     x_ref, in_ref, up_ref, down_ref, vec_ref, in_bias_ref, up_bias_ref, cos_ref, sin_ref = refs[:9]
     x_rows, qkv_ref, joint_ref, slope_ref, part_ref = refs[9:14]
@@ -71,50 +120,21 @@
     z = lax.axis_index("mp")
     t, d = x_ref.shape
     in_width, hidden = in_ref.shape[1], up_ref.shape[1]
-    ids = pl.DeviceIdType.MESH
-
-    barrier = pltpu.get_barrier_semaphore()
-    for way in (1, -1):
-
-        @pl.when((z + way >= 0) & (z + way < n))
-        def _():
-            pl.semaphore_signal(barrier, inc=1, device_id={"mp": z + way}, device_id_type=ids)
-
-    pl.semaphore_wait(barrier, 2 - jnp.where(z == 0, 1, 0) - jnp.where(z == n - 1, 1, 0))
+    greet_line(z, n)
 
     def rows_of(position):
         return pl.ds(pl.multiple_of(position * t, t), t)
 
-    own = pltpu.make_async_copy(x_ref, x_rows.at[rows_of(z)], load.at[0])
-    own.start()
-    hops = {}
-    for k in range(1, n):
-        for way in (1, -1):
-            origin = z - way * (k - 1)
-            there = z + way
-            goes = (origin >= 0) & (origin < n) & (there >= 0) & (there < n)
-            rows = rows_of(jnp.clip(origin, 0, n - 1))
-            at = 2 * (k - 1) + (way < 0)
-            copy = pltpu.make_async_remote_copy(
-                x_ref if k == 1 else x_rows.at[rows], x_rows.at[rows], send.at[at], recv.at[at], {"mp": there}, ids
-            )
-            arrives = (z - way * k >= 0) & (z - way * k < n)
-            hops[k, way] = (copy, goes, arrives)
-
-    def start_step(k):
-        for way in (1, -1):
-            copy, goes, _ = hops[k, way]
-            pl.when(goes)(copy.start)
-
-    start_step(1)
+    own = pltpu.make_async_copy(chunk, x_rows.at[rows_of(z)], load.at[0])
+    gather = line_gather(z, n, t, x_ref, x_rows, send, recv)
+    gather_step(gather, 1)
     weights = [
         pltpu.make_async_copy(source, target, load.at[1 + i])
         for i, (source, target) in enumerate(((in_ref, w_in), (up_ref, w_up), (down_ref, w_down)))
     ]
     for copy in weights:
         copy.start()
-    order = arrival_order(n)
-    positions = [across(z, n, [order[zz][s] for zz in range(n)]) for s in range(n)]
+    positions = slot_positions(z, n)
 
     def slot(s, unused):
         position = jnp.int32(0)
@@ -125,11 +145,9 @@
 
             @pl.when(s == k)
             def _():
-                for way in (1, -1):
-                    copy, _, arrives = hops[k, way]
-                    pl.when(arrives)(copy.wait_recv)
+                gather_wait(gather, k)
                 if k < n - 1:
-                    start_step(k + 1)
+                    gather_step(gather, k + 1)
 
         @pl.when(s == 0)
         def _():
@@ -140,6 +158,7 @@
             pltpu.make_async_copy(x_rows.at[rows], chunk, load.at[4]).start()
 
         pltpu.make_async_copy(x_ref, chunk, load.at[4]).wait()
+        pl.when(s == 0)(own.start)
 
         def norm_rows(i, unused):
             block = pl.ds(pl.multiple_of(i * 32, 32), 32)
@@ -179,6 +198,7 @@
 
         @pl.when(s == 0)
         def _():
+            own.wait()
             weights[1].wait()
             weights[2].wait()
 
@@ -210,9 +230,7 @@
         return unused
 
     lax.fori_loop(0, n, slot, 0)
-    own.wait()
-    for copy, goes, _ in hops.values():
-        pl.when(goes)(copy.wait_send)
+    gather_end(gather)
 
 
 def opening(n, x, flat_in, up_weight, down_weight, vectors, in_bias, up_bias, cosine, sine):
@@ -249,31 +267,218 @@
     )(x, flat_in, up_weight, down_weight, vectors, in_bias, up_bias, cosine, sine)
 
 
-def up_back_kernel(g_ref, w_ref, slope_ref, out_ref):
-    out_ref[...] = (dot(g_ref[...], w_ref[...], NT) * slope_ref[...].astype(F32)).astype(BF16)
-
-
-def up_back(in_width, tile, g, down_weight, slope):
-    rows, d = g.shape
-    width = down_weight.shape[0]
-    first = in_width // tile
-    block = min(rows, 1024)
+def middle_kernel(n, in_width, *refs):
+    g_ref, part_ref, joint_ref, slope_ref, out_ref, down_ref = refs[:6]
+    g_rows, heads_grad, back, grads, to_right, to_left = refs[7:13]
+    w_out, w_down, acc, chunk, hidden_in, slope_in, up_out, heads_out, stage, terms = refs[13:23]
+    come = {1: refs[23], -1: refs[24]}
+    send, recv, load, store = refs[25:]
+    z = lax.axis_index("mp")
+    t, d = g_ref.shape
+    heads_width, hidden = out_ref.shape[0], down_ref.shape[0]
+    ids = pl.DeviceIdType.MESH
+    greet_line(z, n)
+
+    def rows_of(position):
+        return pl.ds(pl.multiple_of(position * t, t), t)
+
+    gather = line_gather(z, n, t, g_ref, g_rows, send, recv)
+    gather_step(gather, 1)
+    weights = [
+        pltpu.make_async_copy(out_ref, w_out, load.at[1]),
+        pltpu.make_async_copy(down_ref, w_down, load.at[2]),
+    ]
+    for copy in weights:
+        copy.start()
+    positions = slot_positions(z, n)
+    hops = {}
+    for k in range(1, n):
+        for way, target in ((1, to_right), (-1, to_left)):
+            here = (z + k < n) if way == 1 else (z >= k)
+            first = (z == 0) if way == 1 else (z == n - 1)
+            source = part_ref.at[rows_of(jnp.clip(z + way * k, 0, n - 1))]
+            buffer = come[way].at[k - 1] if k < n - 1 else None
+            if k > 1:
+                at = 2 * (n - 1) + 2 * (k - 2) + (way < 0)
+                bare, passed = (
+                    from_ref
+                    and pltpu.make_async_remote_copy(
+                        from_ref, come[way].at[k - 2], send.at[at], recv.at[at], {"mp": z + way}, ids
+                    )
+                    for from_ref in (source, buffer)
+                )
+            else:
+                bare, passed = (pltpu.make_async_copy(from_ref, target, load.at[0]) for from_ref in (terms, buffer))
+            terms_copy = pltpu.make_async_copy(source, terms, load.at[3])
+            hops[k, way] = (here & first, here & jnp.logical_not(first), here, bare, passed, terms_copy, buffer)
+
+    def line_step(k):
+        for way in (1, -1):
+            first, later, _, bare, passed, terms_copy, buffer = hops[k, way]
+
+            @pl.when(first)
+            def _():
+                if k == 1:
+                    terms_copy.start()
+                    terms_copy.wait()
+                bare.start()
+                if k == 1:
+                    bare.wait()
+
+            if k < n - 1:
+
+                @pl.when(later)
+                def _():
+                    hops[k + 1, way][3].wait_recv()
+                    terms_copy.start()
+                    terms_copy.wait()
+                    add_rows(buffer, 0, terms, 0, t)
+                    passed.start()
+                    if k == 1:
+                        passed.wait()
+
+    def slot(s, unused):
+        position = jnp.int32(0)
+        for at in range(n):
+            position = position + jnp.where(s == at, positions[at], 0)
+        rows = rows_of(position)
+        inputs = [
+            pltpu.make_async_copy(joint_ref.at[rows], hidden_in, load.at[5]),
+            pltpu.make_async_copy(slope_ref.at[rows], slope_in, load.at[6]),
+        ]
+        for copy in inputs:
+            copy.start()
+        for k in range(1, n):
+
+            @pl.when(s == k)
+            def _():
+                gather_wait(gather, k)
+                if k < n - 1:
+                    gather_step(gather, k + 1)
+                    line_step(n - k)
+
+        @pl.when(s == 0)
+        def _():
+            pltpu.make_async_copy(g_ref, chunk, load.at[4]).start()
+            weights[0].wait()
+            weights[1].wait()
+
+        @pl.when(s > 0)
+        def _():
+            pltpu.make_async_copy(g_rows.at[rows], chunk, load.at[4]).start()
+
+        pltpu.make_async_copy(g_ref, chunk, load.at[4]).wait()
+        for copy in inputs:
+            copy.wait()
+        outs = [
+            pltpu.make_async_copy(heads_out, heads_grad.at[rows], store.at[0]),
+            pltpu.make_async_copy(up_out, back.at[rows, pl.ds(in_width, hidden)], store.at[1]),
+        ]
+
+        @pl.when(s > 0)
+        def _():
+            for copy in outs:
+                copy.wait()
+
+        heads_out[...] = dot(chunk[...], w_out[...], NT).astype(BF16)
+        outs[0].start()
+        tile = min(512, hidden)
+        for first in range(0, hidden, tile):
+            cols = slice(first, first + tile)
+            up_grad = dot(chunk[...], w_down[cols, :], NT) * slope_in[:, cols].astype(F32)
+            up_out[:, cols] = up_grad.astype(BF16)
+        outs[1].start()
+
+        def grad_tile(j, unused):
+            low = pl.multiple_of(j * heads_width, heads_width)
+            turned = hidden_in[:, pl.ds(low, heads_width)].T
+            into = pl.ds(low, heads_width)
+            for first in range(0, d, 512):
+                cols = slice(first, first + 512)
+                product = dot(turned, chunk[:, cols])
+
+                @pl.when(s == 0)
+                def _():
+                    acc[into, cols] = product
+
+                @pl.when((s > 0) & (s < n - 1))
+                def _():
+                    acc[into, cols] += product
+
+                @pl.when(s == n - 1)
+                def _():
+                    if first == 0:
+
+                        @pl.when(j > 0)
+                        def _():
+                            pltpu.make_async_copy(stage, grads.at[into], store.at[2]).wait()
+
+                    stage[:, cols] = (acc[into, cols] + product).astype(BF16)
+
+            @pl.when(s == n - 1)
+            def _():
+                pltpu.make_async_copy(stage, grads.at[into], store.at[2]).start()
+
+            return unused
+
+        lax.fori_loop(0, (heads_width + hidden) // heads_width, grad_tile, 0)
+
+        @pl.when(s == n - 1)
+        def _():
+            line_step(1)
+            for copy in outs:
+                copy.wait()
+            pltpu.make_async_copy(stage, grads.at[pl.ds(0, heads_width)], store.at[2]).wait()
+
+        return unused
+
+    lax.fori_loop(0, n, slot, 0)
+    gather_end(gather)
+    for (k, _), (_, _, here, bare, _, _, _) in hops.items():
+        if k > 1:
+            pl.when(here)(bare.wait_send)
+
+
+def middle(n, in_width, g, down_part, joint, slope, out_weight, down_weight, earlier):
+    t, d = g.shape
+    rows = n * t
+    heads_width, hidden = out_weight.shape[0], down_weight.shape[0]
+    anywhere = pl.BlockSpec(memory_space=pl.ANY)
+    copies = 2 * (n - 1) + 2 * (n - 2)
     return pl.pallas_call(
-        up_back_kernel,
-        grid=(rows // block, width // tile),
-        in_specs=[
-            pl.BlockSpec((block, d), lambda i, j: (i, 0)),
-            pl.BlockSpec((tile, d), lambda i, j: (j, 0)),
-            pl.BlockSpec((block, tile), lambda i, j: (i, j)),
+        functools.partial(middle_kernel, n, in_width),
+        in_specs=[anywhere] * 7,
+        out_specs=[anywhere] * 6,
+        out_shape=[
+            jax.ShapeDtypeStruct(shape, BF16)
+            for shape in (
+                (rows, d), (rows, heads_width), (rows, in_width + hidden), (heads_width + hidden, d), (t, d), (t, d),
+            )
         ],
-        out_specs=pl.BlockSpec((block, tile), lambda i, j: (i, first + j)),
-        out_shape=jax.ShapeDtypeStruct((rows, in_width + width), BF16),
-        compiler_params=params(),
+        scratch_shapes=[
+            pltpu.VMEM((heads_width, d), BF16),
+            pltpu.VMEM((hidden, d), BF16),
+            pltpu.VMEM((heads_width + hidden, d), F32),
+            pltpu.VMEM((t, d), BF16),
+            pltpu.VMEM((t, heads_width + hidden), BF16),
+            pltpu.VMEM((t, hidden), BF16),
+            pltpu.VMEM((t, hidden), BF16),
+            pltpu.VMEM((t, heads_width), BF16),
+            pltpu.VMEM((heads_width, d), BF16),
+            pltpu.VMEM((t, d), BF16),
+            pltpu.VMEM((n - 2, t, d), BF16),
+            pltpu.VMEM((n - 2, t, d), BF16),
+        ]
+        + [pltpu.SemaphoreType.DMA((copies,))] * 2
+        + [pltpu.SemaphoreType.DMA((7,)), pltpu.SemaphoreType.DMA((3,))],
+        compiler_params=pltpu.CompilerParams(
+            vmem_limit_bytes=60 * 1024 * 1024, collective_id=2, has_side_effects=True
+        ),
         cost_estimate=pl.CostEstimate(
-            flops=2 * rows * d * width, bytes_accessed=2 * (rows * d + d * width + 2 * rows * width), transcendentals=0
+            flops=16 * 4 * rows * d * (heads_width + hidden), bytes_accessed=200 * 2**20, transcendentals=0
         ),
-        name="up_back",
-    )(g, down_weight, slope)
+        name="middle",
+    )(g, down_part, joint, slope, out_weight, down_weight, earlier)
 
 
 def cross_kernel(heads_tile, x_ref, back_ref, in_ref, up_ref, cross_ref, sums_ref, total_ref, xt_ref):
@@ -763,16 +968,10 @@
     )(part, cross, small)
 
 
-def scatter_sum(part, own, z, n):
-    right = left = None
-    for k in range(n - 1, 0, -1):
-        for_right, for_left = part(z + k), part(z - k)
-        if right is not None:
-            for_right = (for_right.astype(F32) + right.astype(F32)).astype(BF16)
-            for_left = (for_left.astype(F32) + left.astype(F32)).astype(BF16)
-        right = lax.ppermute(for_right, "mp", [(i, i + 1) for i in range(n - k)])
-        left = lax.ppermute(for_left, "mp", [(i, i - 1) for i in range(k, n)])
-    return own + right.astype(F32) + left.astype(F32)
+def last_hop(to_right, to_left, n):
+    right = lax.ppermute(to_right, "mp", [(i, i + 1) for i in range(n - 1)])
+    left = lax.ppermute(to_left, "mp", [(i, i - 1) for i in range(1, n)])
+    return right.astype(F32) + left.astype(F32)
 
 
 def exchange(part, own, z, n):
@@ -833,8 +1032,10 @@
         n, normed.astype(BF16), flat_in, up_weight, down_weight, vectors, in_bias.reshape(1, in_width),
         up_bias[None, :], cosine, sine,
     )
-    g_rows = lax.all_gather(after(own_grad, slope, out_full), "mp", axis=0, tiled=True)
     joint, logs = attend(t, low, qkv, start_row, joint)
+    unused, heads_grad, back, out_down_grad, to_right, to_left = middle(
+        n, in_width, own_grad, down_part, joint, slope, out_weight, down_weight, out_full
+    )
 
     def rows_for(array):
         def part(position):
@@ -842,17 +1043,14 @@
 
         return part
 
-    heads_out = joint[:, :heads_width]
+    heads_out = after(joint[:, :heads_width], to_right)
     heads_mine = exchange(rows_for(heads_out), rows_for(heads_out)(z), z, n)
     heads_mine = heads_mine.transpose(1, 0, 2).reshape(t, n * heads_width)
     attn_branch = dot(heads_mine, out_full) + out_bias
-    mlp_branch = scatter_sum(rows_for(down_part), rows_for(down_part)(z).astype(F32), z, n) + down_bias
+    mlp_branch = last_hop(to_right, to_left, n) + rows_for(down_part)(z).astype(F32) + down_bias
     block_out = (own_tokens + attn_branch + mlp_branch).astype(BF16)
     squares = jnp.stack([jnp.sum(attn_branch * attn_branch), jnp.sum(mlp_branch * mlp_branch)])
 
-    back = up_back(in_width, heads_width, g_rows, down_weight, slope)
-    heads_grad = dot(g_rows, out_weight, NT).astype(BF16)
-    out_down_grad = dot(joint, g_rows, TN).astype(BF16)
     back = attend_back(
         t, high, qkv, heads_grad, joint, logs, start_row, cosine, sine, back, out_down_grad
     )

time: 1060 us -> 878 us (0.83); the launches traced: 1060 us -> 863 us
  waiting for transfers between devices: 212 us -> 36.5 us
  Pallas kernels: 546 us -> 627 us
  matrix products: 91.4 us -> 59.7 us
  other arithmetic: 88.1 us -> 57.7 us
  starting transfers between devices: 43.2 us -> 14.5 us
    ppermute x6 -> x2, waiting for transfers between devices: 194 us -> 0.01 us  [the longest x1 0.01 us: last_hop(): right = lax.ppermute(to_right, 'mp', [(i, i + 1) for i in range(n - 1)])]
    pallas_call x1, Pallas kernels: 24.6 us -> 159 us  [middle(): pl.pallas_call(functools.partial(middle_kernel, n, in_width), in_specs=[a...]
    pallas_call x1, Pallas kernels: 227 us -> 164 us  [closing_sums(): pl.pallas_call(functools.partial(closing_kernel, n, groups), in_specs=[wh...]
    ppermute x3, waiting for transfers between devices: 0.01 us -> 36.4 us  [exchange(): lax.ppermute(part(z - k), 'mp', [(i, i - k) for i in range(k, n)])]
    dot_general x5 -> x3, matrix products: 91.4 us -> 59.7 us  [dot(): return lax.dot_general(a, b, dims, preferred_element_type=F32)]
    ppermute x6 -> x2, starting transfers between devices: 29.2 us -> 3.9 us  [the longest x1 2.62 us: last_hop(): right = lax.ppermute(to_right, 'mp', [(i, i + 1) for i in range(n - 1)])]
    ppermute x3, waiting for transfers between devices: 17.9 us -> 0.01 us  [exchange(): lax.ppermute(part(z + k), 'mp', [(i, i + k) for i in range(n - k)])]
    convert_element_type x3 -> x0, other arithmetic: 16.7 us -> none  [the longest x2 12.2 us: scatter_sum(): for_right = (for_right.astype(F32) + right.astype(F32)).astype(BF16)]
  transfers between devices with their start and end apart: 15 -> 10, of which waited for: 7 -> 2; matrix products, arithmetic and copies ran while one was open for 15% -> 15% of each run, Pallas kernels for 42% -> 50%
where the time goes in v3:
time: 878 us; the launch traced here: 863 us
  Pallas kernels  627 us (71%)
  matrix products  59.7 us (7%)
  other arithmetic  57.7 us (7%)
  local copies, waits for them, and re-layouts  52.9 us (6%)
  waiting for transfers between devices  36.5 us (4%)
  between operations  14.7 us (2%)
  starting transfers between devices  14.5 us (2%)
    pallas_call x1, Pallas kernels, opening(): pl.pallas_call(functools.partial(opening_kernel, n, heads), in_specs=[any...  198 us
    pallas_call x1, Pallas kernels, closing_sums(): pl.pallas_call(functools.partial(closing_kernel, n, groups), in_specs=[wh...  164 us
    pallas_call x1, Pallas kernels, middle(): pl.pallas_call(functools.partial(middle_kernel, n, in_width), in_specs=[a...  159 us
    dot_general x3, matrix products, dot(): return lax.dot_general(a, b, dims, preferred_element_type=F32)  59.7 us
    pallas_call x1, Pallas kernels, cross_products(): pl.pallas_call(functools.partial(cross_kernel, heads_tile), grid=(d // ti...  46.5 us
    ppermute x3, waiting for transfers between devices, exchange(): lax.ppermute(part(z - k), 'mp', [(i, i - k) for i in range(k, n)])  36.4 us
    pallas_call x1, Pallas kernels, attend_back(): pl.pallas_call(functools.partial(attend_back_kernel, t, heads), grid=(1,)...  33.8 us
    pallas_call x1, Pallas kernels, attend(): pl.pallas_call(functools.partial(attend_kernel, t, heads), grid=(1,), in_...  25.7 us
  transfers between devices with their start and end apart: 10, of which 2 were waited for; matrix products, arithmetic and copies ran while one was open for 15% of the time, Pallas kernels for 50%

profile of v3, /device:TPU:0, one launch (start us, length us, event | category | flops | bytes accessed | tf_op | source)
XLA Modules:
  0.0 862.7 jit_solution(14633058656410333731)
XLA Ops:
  15.4 4.1 copy.46
  20.1 3.7 fusion.19
  26.5 197.8 %opening.1 = (bf16[2048,2048]{1,0:T(8,128)(2,1)}, bf16[2048,1536]{1,0:T(8,128)(2,1)}, bf16[2048,2560]{1,0:T(8,128)(2,1)}, bf16[2048,2048]{1,0:T(8,128)(2,1)}, bf16[2048,2048]{1,0:T(8,128)(2,1)}) custom-call(bf16[512,2048]{1,0:T(8,128)(2,1)} %fusion.9.refs_0_, bf16[2048,1536]{1,0:T(8,128)(2,1)} %bitcast.97, bf16[2048,2048]{1,0:T(8,128)(2,1)} %up_ref.1, ...), custom_call_target="tpu_custom_call" | custom-call | flops 755914244096 | bytes 209715200 | tf_op jit(solution)/shard_map/opening/pallas_call | solution.py:241
  225.7 25.7 %attend.1 = (bf16[2048,2560]{1,0:T(8,128)(2,1)}, f32[2,2048]{1,0:T(2,128)}) custom-call(s32[4]{0:T(128)} %and_select_fusion.low_ref, bf16[2048,1536]{1,0:T(8,128)(2,1)} %get-tuple-element.33.qkv_ref, s32[1,2048]{1,0:T(1,128)} %bitcast.101, bf16[2048,2560]{1,0:T(8,128)(2,1)} %get-tuple-element.34.held_ref), custom_call_target="tpu_custom_call", output_to_operand_aliasing={{0}: (3, {})} | custom-call | flops 4294967296 | bytes 6291456 | tf_op jit(solution)/shard_map/attend/pallas_call | solution.py:608
  251.4 3.2 slice.69.refs_0_
  256.2 158.6 %middle.1 = (bf16[2048,2048]{1,0:T(8,128)(2,1)}, bf16[2048,512]{1,0:T(8,128)(2,1)}, bf16[2048,3584]{1,0:T(8,128)(2,1)}, bf16[2560,2048]{1,0:T(8,128)(2,1)}, bf16...) custom-call(bf16[512,2048]{1,0:T(8,128)(2,1)} %bitcast.95, bf16[2048,2048]{1,0:T(8,128)(2,1)} %get-tuple-element.36.refs_1_, ...), custom_call_target="tpu_custom_call" | custom-call | flops 687194767360 | bytes 209715200 | tf_op jit(solution)/shard_map/middle/pallas_call | solution.py:448
  414.8 33.8 %attend_back.1.back_ref = bf16[2048,3584]{1,0:T(8,128)(2,1)} custom-call(s32[8]{0:T(128)} %convert_reduce_fusion.2.high_ref, bf16[2048,1536]{1,0:T(8,128)(2,1)} %get-tuple-element.33.qkv_ref, bf16[2048,512]{1,0:T(8,128)(2,1)} %get-tuple-element.40.grad_ref, bf16[2048,2560]{1,0:T(8,128)(2,1)} %get-tuple-element.35.refs_2_.out_ref, ...), custom_call_target="tpu_custom_call", output_to_operand_aliasing={{}: (8, {})} | custom-call | flops 10737418240 | bytes 12582912 | tf_op jit(solution)/shard_map/attend_back/pallas_call | solution.py:703
  448.5 19.6 %fusion.1 = f32[2048,2048]{1,0:T(8,128)} fusion(bf16[2048,1536]{1,0:T(8,128)(2,1)} %bitcast.98, bf16[2048,3584]{1,0:T(8,128)(2,1)} %attend_back.1.back_ref), kind=kOutput, calls=%fused_computation.5 | convolution fusion | flops 12884901888 | bytes 29360128 | tf_op jit(solution)/shard_map/dot_general | solution.py:26
  470.8 3.2 constant_dynamic-slice_fusion
  482.0 46.5 %cross.1 = (bf16[2048,3584]{1,0:T(8,128)(2,1)}, f32[2048,128]{1,0:T(8,128)}, f32[8,3584]{1,0:T(8,128)}) custom-call(bf16[2048,2048]{1,0:T(8,128)(2,1)} %get-tuple-element.44.x_ref, bf16[2048,3584]{1,0:T(8,128)(2,1)} %attend_back.1.back_ref, bf16[2048,1536]{1,0:T(8,128)(2,1)} %bitcast.99, bf16[2048,2048]{1,0:T(8,128)(2,1)} %up_ref.1), custom_call_target="tpu_custom_call" | custom-call | flops 30064771072 | bytes 52428800 | tf_op jit(solution)/shard_map/cross/pallas_call | solution.py:526
  530.1 25.7 %add_convert_fusion.refs_0_ = bf16[2048,2048]{1,0:T(8,128)(2,1)} fusion(f32[2048,2048]{1,0:T(8,128)} %fusion.1, bf16[2048,2048]{1,0:T(8,128)(2,1)} %up_ref.1, bf16[2048,3584]{1,0:T(8,128)(2,1)} %attend_back.1.back_ref, f32[2048]{0:T(1024)S(1)} %copy-done.8, f32[2048]{0:T(1024)S(1)} %copy-done.12), kind=kOutput, calls=%fused_computation.1 | convolution fusion | flops 17196646400 | bytes 41959424 | tf_op jit(solution)/shard_map/dot_general | solution.py:26
  565.7 3.6 collective-permute-done.3
  569.4 32.8 %collective-permute-done.4 = bf16[512,512]{1,0:T(8,128)(2,1)S(1)} collective-permute-done((bf16[512,512]{1,0:T(8,128)(2,1)S(1)}, bf16[512,512]{1,0:T(8,128)(2,1)S(1)}, u32[]{:S(2)}, u32[]{:S(2)}) %collective-permute-start.4) | collective-permute-done | bytes 524320 | tf_op jit(solution)/shard_map/ppermute | solution.py:982
  603.8 4.6 copy.43
  608.4 14.4 %multiply_reduce_fusion = (f32[]{:T(128)}, bf16[1,512,2048]{2,1,0:T(8,128)(2,1)}, f32[]{:T(128)}) fusion(bf16[512,2048]{1,0:T(8,128)(2,1)} %collective-permute-done.7, bf16[512,2048]{1,0:T(8,128)(2,1)} %collective-permute-done.6, f32[2048]{0:T(1024)S(1)} %copy-done.24, bf16[2048,2048]{1,0:T(8,128)(2,1)} %get-tuple-element.36.refs_1_, s32[]{:T(128)S(6)} %select_n.43, ...), kind=kOutput, calls=%fused_computation.25 | convolution fusion | flops 4310695936 | bytes 20987916 | tf_op jit(solution)/shard_map/dot_general | solution.py:26
  625.5 164.4 %closing_sums.1 = (f32[512,2048]{1,0:T(8,128)}, bf16[2048,3584]{1,0:T(8,128)(2,1)}, f32[16,2048]{1,0:T(8,128)}) custom-call(bf16[2048,2048]{1,0:T(8,128)(2,1)} %add_convert_fusion.refs_0_, bf16[2048,3584]{1,0:T(8,128)(2,1)} %get-tuple-element.45.refs_1_, f32[16,2048]{1,0:T(8,128)} %concatenate.11.refs_2_), custom_call_target="tpu_custom_call" | custom-call | tf_op jit(solution)/shard_map/closing_sums/pallas_call | solution.py:949
  789.9 5.9 slice.81
  795.8 13.5 %reshape.104 = bf16[2048,2,768]{2,1,0:T(2,128)(2,1)} reshape(bf16[2048,1536]{1,0:T(8,128)(2,1)} %slice.81) | data formatting | bytes 12582912 | tf_op jit(solution)/shard_map/reshape | solution.py:1083
  812.1 3.4 fusion.20
  816.7 2.7 fusion.17
  819.5 9.5 %multiply_add_fusion.1 = f32[2048,2,768]{2,1,0:T(2,128)} fusion(bf16[2048,2,768]{2,1,0:T(2,128)(2,1)S(1)} %bitcast.94, f32[2048]{0:T(1024)S(1)} %copy-done.12, f32[2,768]{1,0:T(2,128)S(1)} %mul.194, f32[2048]{0:T(1024)S(1)} %copy-done.14), kind=kLoop, calls=%fused_computation.2 | loop fusion | flops 12582912 | bytes 18896896 | tf_op jit(solution)/shard_map/add | solution.py:1085
  829.0 10.3 %multiply_add_fusion = f32[2048,2048]{1,0:T(8,128)} fusion(f32[2048]{0:T(1024)S(1)} %bitcast.111, f32[2048]{0:T(1024)S(1)} %copy-done.10, f32[2048]{0:T(1024)S(1)} %copy-done.8, bf16[2048,3584]{1,0:T(8,128)(2,1)} %get-tuple-element.50), kind=kLoop, calls=%fused_computation | loop fusion | flops 16777216 | bytes 25190400 | tf_op jit(solution)/shard_map/add | solution.py:1088
  839.3 11.7 %slice_convert_fusion = f32[2048,2048]{1,0:T(8,128)} fusion(bf16[2560,2048]{1,0:T(8,128)(2,1)} %all-reduce.4.cloned.1.call-done), kind=kLoop, calls=%fused_computation.3 | loop fusion | flops 4194304 | bytes 25165824 | tf_op jit(solution)/shard_map/convert_element_type | solution.py:1103
  851.0 4.1 slice_convert_fusion.1
  (124 shorter events, 45.2 us)
Async XLA Ops:
  7.2 249.0 %all-gather.2.cloned.1.call-start = ((), (), s32[]{:S(2)}) async-start(), calls=%async_computation | async-start | bytes 8650752 | tf_op jit(solution)/shard_map/all_gather | solution.py:1013
  15.4 8.4 copy-start.7
  15.4 8.4 copy-start.9
  15.4 8.4 copy-start.11
  15.4 8.4 copy-start.13
  448.5 390.8 %all-reduce.4.cloned.1.call-start = ((), (), s32[]{:S(2)}) async-start(), calls=%async_computation.1 | async-start | bytes 20971520 | tf_op jit(solution)/shard_map/psum | solution.py:1057
  468.2 140.2 %collective-permute-start.6 = (bf16[512,2048]{1,0:T(8,128)(2,1)}, bf16[512,2048]{1,0:T(8,128)(2,1)}, u32[]{:S(2)}, u32[]{:S(2)}) collective-permute-start(bf16[512,2048]{1,0:T(8,128)(2,1)} %get-tuple-element.38.refs_1_), channel_id=1, source_target_pairs={{0,1},{1,2},{2,3},{4,5},{5,6},{6,7},{8,9},{9,10},{10,11},{12,13},{... | collective-permute-start | bytes 6291464 | tf_op jit(solution)/shard_map/ppermute | solution.py:972
  474.0 83.5 %collective-permute-start = (bf16[512,512]{1,0:T(8,128)(2,1)}, bf16[512,512]{1,0:T(8,128)(2,1)}, u32[]{:S(2)}, u32[]{:S(2)}) collective-permute-start(bf16[512,512]{1,0:T(8,128)(2,1)} %get-tuple-element.61), channel_id=1, source_target_pairs={{0,3},{4,7},{8,11},{12,15},{16,19},{20,23},{24,27},{28,31}} | collective-permute-start | bytes 1572872 | tf_op jit(solution)/shard_map/ppermute | solution.py:981
  476.1 83.8 %collective-permute-start.1 = (bf16[512,512]{1,0:T(8,128)(2,1)}, bf16[512,512]{1,0:T(8,128)(2,1)}, u32[]{:S(2)}, u32[]{:S(2)}) collective-permute-start(bf16[512,512]{1,0:T(8,128)(2,1)} %get-tuple-element.60), channel_id=1, source_target_pairs={{0,2},{1,3},{4,6},{5,7},{8,10},{9,11},{12,14},{13,15},{16,18},{17,... | collective-permute-start | bytes 1572872 | tf_op jit(solution)/shard_map/ppermute | solution.py:981
  478.6 83.6 %collective-permute-start.2 = (bf16[512,512]{1,0:T(8,128)(2,1)S(1)}, bf16[512,512]{1,0:T(8,128)(2,1)}, u32[]{:S(2)}, u32[]{:S(2)}) collective-permute-start(bf16[512,512]{1,0:T(8,128)(2,1)S(1)} %get-tuple-element.59), channel_id=1, source_target_pairs={{0,1},{1,2},{2,3},{4,5},{5,6},{6,7},{8,9},{9,10},{10,11},{12,13},{... | collective-permute-start | bytes 1572872 | tf_op jit(solution)/shard_map/ppermute | solution.py:981
  480.7 127.6 %collective-permute-start.7 = (bf16[512,2048]{1,0:T(8,128)(2,1)}, bf16[512,2048]{1,0:T(8,128)(2,1)}, u32[]{:S(2)}, u32[]{:S(2)}) collective-permute-start(bf16[512,2048]{1,0:T(8,128)(2,1)} %get-tuple-element.39), channel_id=1, source_target_pairs={{1,0},{2,1},{3,2},{5,4},{6,5},{7,6},{9,8},{10,9},{11,10},{13,12},{... | collective-permute-start | bytes 6291464 | tf_op jit(solution)/shard_map/ppermute | solution.py:973
  482.0 48.1 %copy-start.8 = (f32[2048]{0:T(1024)S(1)}, f32[2048]{0:T(1024)}, u32[]{:S(2)}) copy-start(f32[2048]{0:T(1024)} %param.20) | copy-start | bytes 24580
  482.0 48.1 %copy-start.12 = (f32[2048]{0:T(1024)S(1)}, f32[2048]{0:T(1024)}, u32[]{:S(2)}) copy-start(f32[2048]{0:T(1024)} %param.18) | copy-start | bytes 24580
  557.5 11.8 %collective-permute-start.3 = (bf16[512,512]{1,0:T(8,128)(2,1)S(1)}, bf16[512,512]{1,0:T(8,128)(2,1)S(1)}, u32[]{:S(2)}, u32[]{:S(2)}) collective-permute-start(bf16[512,512]{1,0:T(8,128)(2,1)S(1)} %get-tuple-element.58), channel_id=1, source_target_pairs={{1,0},{2,1},{3,2},{5,4},{6,5},{7,6},{9,8},{10,9},{11,10},{13,12},{... | collective-permute-start | bytes 1572872 | tf_op jit(solution)/shard_map/ppermute | solution.py:982
  559.9 42.3 %collective-permute-start.4 = (bf16[512,512]{1,0:T(8,128)(2,1)S(1)}, bf16[512,512]{1,0:T(8,128)(2,1)S(1)}, u32[]{:S(2)}, u32[]{:S(2)}) collective-permute-start(bf16[512,512]{1,0:T(8,128)(2,1)S(1)} %get-tuple-element.57), channel_id=1, source_target_pairs={{2,0},{3,1},{6,4},{7,5},{10,8},{11,9},{14,12},{15,13},{18,16},{19,... | collective-permute-start | bytes 1572872 | tf_op jit(solution)/shard_map/ppermute | solution.py:982
  562.2 40.0 %collective-permute-start.5 = (bf16[512,512]{1,0:T(8,128)(2,1)S(1)}, bf16[512,512]{1,0:T(8,128)(2,1)S(1)}, u32[]{:S(2)}, u32[]{:S(2)}) collective-permute-start(bf16[512,512]{1,0:T(8,128)(2,1)S(1)} %get-tuple-element.56), channel_id=1, source_target_pairs={{3,0},{7,4},{11,8},{15,12},{19,16},{23,20},{27,24},{31,28}} | collective-permute-start | bytes 1572872 | tf_op jit(solution)/shard_map/ppermute | solution.py:982
  608.4 15.8 %copy-start.20 = (f32[2048]{0:T(1024)S(1)}, f32[2048]{0:T(1024)}, u32[]{:S(2)}) copy-start(f32[2048]{0:T(1024)} %convert_reduce_fusion) | copy-start | bytes 24580
  795.8 16.2 %copy-start.16 = (f32[512]{0:T(512)S(1)}, f32[512]{0:T(512)}, u32[]{:S(2)}) copy-start(f32[512]{0:T(512)} %copy-done.15) | copy-start | bytes 6148
  795.8 16.2 %copy-start.19 = (f32[512]{0:T(512)S(1)}, f32[512]{0:T(512)}, u32[]{:S(2)}) copy-start(f32[512]{0:T(512)} %copy-done.18) | copy-start | bytes 6148
  810.2 9.2 %copy-start.22 = (f32[2,768]{1,0:T(2,128)}, f32[2,768]{1,0:T(2,128)S(1)}, u32[]{:S(2)}) copy-start(f32[2,768]{1,0:T(2,128)S(1)} %mul.194) | copy-start | bytes 18436
  812.0 17.0 %copy-start.17 = (f32[1,2048]{1,0:T(1,128)}, f32[1,2048]{1,0:T(1,128)S(1)}, u32[]{:S(2)}) copy-start(f32[1,2048]{1,0:T(1,128)S(1)} %get-tuple-element.64) | copy-start | bytes 24580
  812.0 43.1 %copy-start.21 = (f32[1,2048]{1,0:T(1,128)}, f32[1,2048]{1,0:T(1,128)S(1)}, u32[]{:S(2)}) copy-start(f32[1,2048]{1,0:T(1,128)S(1)} %get-tuple-element.65) | copy-start | bytes 24580
  812.1 7.4 slice-start
  819.5 9.6 %copy-start.10 = (f32[2048]{0:T(1024)S(1)}, f32[2048]{0:T(1024)}, u32[]{:S(2)}) copy-start(f32[2048]{0:T(1024)} %param.21) | copy-start | bytes 24580
  (14 other events, 68.1 us)
Sparse Core Ops, SparseCore 0:
  11.5 102.5 all-gather.1
  468.3 151.6 all-reduce.3

commit v4 on v3

--- a/solution.py
+++ b/solution.py
@@ -739,13 +739,15 @@
 
 def closing_kernel(n, groups, *refs):
     bits, mp_bits = groups.bit_length() - 1, n.bit_length() - 1
-    part_ref, cross_ref, small_ref, norm_ref, summed_ref, small_out = refs[:6]
-    come = {1: refs[6], -1: refs[7]}
-    keep, core_in = refs[8:10]
-    stage_in = [refs[10 : 9 + bits], refs[9 + bits : 8 + 2 * bits]]
-    small_in, small_sum, send, recv, load = refs[8 + 2 * bits :]
+    back_ref, cross_ref, small_ref, in_ref, up_ref, vec_ref, norm_ref, summed_ref, small_out = refs[:9]
+    part = refs[9]
+    come = {1: refs[10], -1: refs[11]}
+    keep, core_in, chunk, in_tiles, up_tiles = refs[12:17]
+    stage_in = [refs[17 : 16 + bits], refs[16 + bits : 15 + 2 * bits]]
+    small_in, small_sum, send, recv, load, fetch = refs[15 + 2 * bits :]
     z, group = lax.axis_index("mp"), lax.axis_index("dp")
-    t = norm_ref.shape[0]
+    t, d = norm_ref.shape
+    in_width = in_ref.shape[1]
     half = keep.shape[0]
     quarter = half // 2
     ids = pl.DeviceIdType.MESH
@@ -767,135 +769,20 @@
     barrier = pltpu.get_barrier_semaphore()
     for peer in [dp_peer(b) for b in range(bits)] + [mp_peer(b) for b in range(mp_bits)]:
         pl.semaphore_signal(barrier, inc=1, device_id=peer, device_id_type=ids)
-
-    @pl.when(z + 1 < n)
-    def _():
-        pl.semaphore_signal(barrier, inc=1, device_id={"mp": z + 1}, device_id_type=ids)
-
-    @pl.when(z >= 1)
-    def _():
-        pl.semaphore_signal(barrier, inc=1, device_id={"mp": z - 1}, device_id_type=ids)
+    for way in (1, -1):
+
+        @pl.when((z + way >= 0) & (z + way < n))
+        def _():
+            pl.semaphore_signal(barrier, inc=1, device_id={"mp": z + way}, device_id_type=ids)
 
     ends = jnp.where(z == 0, 1, 0) + jnp.where(z == n - 1, 1, 0)
     pl.semaphore_wait(barrier, bits + mp_bits + 2 - ends)
 
-    small_peers = [dp_peer(b) for b in range(bits)] + [mp_peer(b) for b in range(mp_bits)]
-    small_copies = []
-
-    def small_step(i):
-        if i == 0:
-            small_sum[0] = small_ref[...]
-        else:
-            small_copies[i - 1].wait_recv()
-            if i - 1 < bits:
-                total = small_sum[i - 1] + small_in[i - 1]
-            else:
-                total = small_sum[i - 1]
-                small_sum[i, 8:, :] = total[8:]
-                total = total[:8] + small_in[i - 1, :8, :]
-            small_sum[i, : total.shape[0], :] = total
-        if i < len(small_peers):
-            small_copies.append(remote(small_sum.at[i], small_in.at[i], small_peers[i]))
-            small_copies[i].start()
-        else:
-            small_out[...] = small_sum[i]
-
-    hops = {}
-
-    def rows_at(distance):
-        return pl.multiple_of(jnp.clip(z + distance, 0, n - 1) * t, t)
-
-    def line_step(k):
-        for way in (1, -1):
-            buffer = come[way].at[k]
-            here = (z + k < n) if way == 1 else (z >= k)
-            first = (z == 0) if way == 1 else (z == n - 1)
-            if k < n - 1:
-
-                @pl.when(here & jnp.logical_not(first))
-                def _():
-                    hops[k + 1, way][0].wait_recv()
-                    add_rows(buffer, 0, part_ref, rows_at(way * k), t) if k > 0 else None
-
-            if k > 0:
-
-                @pl.when(here & first)
-                def _():
-                    buffer[...] = part_ref[pl.ds(rows_at(way * k), t), :]
-
-                hops[k, way] = (remote(buffer, come[way].at[k - 1], {"mp": z + way}), here)
-
-                @pl.when(here)
-                def _():
-                    hops[k, way][0].start()
-
-        if k == 0:
-            step = 32
-
-            def body(i, unused):
-                rows = pl.ds(pl.multiple_of(i * step, step), step)
-                total = part_ref[pl.ds(pl.multiple_of(z * t + i * step, step), step), :].astype(F32)
-                for way in (1, -1):
-                    first = (z == 0) if way == 1 else (z == n - 1)
-                    total = total + jnp.where(first, 0.0, come[way][0, rows, :].astype(F32))
-                norm_ref[rows, :] = total
-                return unused
-
-            lax.fori_loop(0, t // step, body, 0)
-
     mine, other = bit_of(0) * half, (1 - bit_of(0)) * half
-    path = [list(range(1, bits)), list(range(bits - 1, 0, -1))]
-    base = [0, quarter]
-    size = quarter
-    regions = [[], []]
-    current = [None, None]
-
-    def first_halving():
-        own.wait()
-        for p in (0, 1):
-            core[p].wait_recv()
-            add_rows(keep, p * quarter, core_in, p * quarter, quarter)
-            halve(p, 0)
-
-    def halve(p, s):
-        b = path[p][s]
-        part = quarter // 2 ** (s + 1)
-        regions[p].append((base[p], 2 * part))
-        away = pl.multiple_of(base[p] + (1 - bit_of(b)) * part, 32)
-        current[p] = remote(keep.at[pl.ds(away, part)], stage_in[p][s], dp_peer(b))
-        current[p].start()
-        started.append(current[p])
-        base[p] = base[p] + bit_of(b) * part
-
-    def next_halving(s):
-        for p in (0, 1):
-            current[p].wait_recv()
-            add_rows(keep, base[p], stage_in[p][s - 1], 0, quarter // 2**s)
-            if s < bits - 1:
-                halve(p, s)
-            else:
-                count = quarter // 2**s
-                place = pl.ds(pl.multiple_of(base[p], 32), count)
-                target = summed_ref.at[pl.ds(pl.multiple_of(mine + base[p], 32), count)]
-                local = pltpu.make_async_copy(keep.at[place], target, load.at[1 + p])
-                local.start()
-                current[p] = remote(keep.at[place], target, dp_peer(path[p][s - 1]))
-                current[p].start()
-                started.append(current[p])
-                locals_.append(local)
-
-    def doubling(s):
-        for p in (0, 1):
-            current[p].wait_recv()
-            if s == bits - 2:
-                locals_[p].wait()
-            at, count = regions[p][s]
-            rows = summed_ref.at[pl.ds(pl.multiple_of(mine + at, 32), count)]
-            current[p] = remote(rows, rows, dp_peer(path[p][s - 1] if s > 0 else 0))
-            current[p].start()
-            started.append(current[p])
-
-    started, locals_ = [], []
+
+    def summed_rows(at, count):
+        return summed_ref.at[pl.ds(pl.multiple_of(mine + at, 32), count)]
+
     core = [
         remote(
             cross_ref.at[pl.ds(pl.multiple_of(other + p * quarter, 32), quarter)],
@@ -905,82 +792,262 @@
         for p in (0, 1)
     ]
     own = pltpu.make_async_copy(cross_ref.at[pl.ds(pl.multiple_of(mine, 32), half)], keep, load.at[0])
+    plans = []
+    for p, path in enumerate((list(range(1, bits)), list(range(bits - 1, 0, -1)))):
+        at, count = p * quarter, quarter
+        halvings, regions = [], []
+        for s, b in enumerate(path):
+            regions.append((at, count))
+            count //= 2
+            away = keep.at[pl.ds(pl.multiple_of(at + (1 - bit_of(b)) * count, 32), count)]
+            at = at + bit_of(b) * count
+            halvings.append((remote(away, stage_in[p][s], dp_peer(b)), at, count))
+        place = keep.at[pl.ds(pl.multiple_of(at, 32), count)]
+        local = pltpu.make_async_copy(place, summed_rows(at, count), load.at[1 + p])
+        doublings = [remote(place, summed_rows(at, count), dp_peer(path[-1]))]
+        for s in range(bits - 2, -1, -1):
+            rows = summed_rows(*regions[s])
+            doublings.append(remote(rows, rows, dp_peer(path[s - 1] if s > 0 else 0)))
+        plans.append((halvings, local, doublings))
+
+    def first_halving():
+        own.wait()
+        for p, (halvings, _, _) in enumerate(plans):
+            core[p].wait_recv()
+            add_rows(keep, p * quarter, core_in, p * quarter, quarter)
+            halvings[0][0].start()
+
+    def next_halving(s):
+        for p, (halvings, local, doublings) in enumerate(plans):
+            copy, at, count = halvings[s - 1]
+            copy.wait_recv()
+            add_rows(keep, at, stage_in[p][s - 1], 0, count)
+            if s < bits - 1:
+                halvings[s][0].start()
+            else:
+                local.start()
+                doublings[0].start()
+
+    def doubling(s):
+        for _, local, doublings in plans:
+            doublings[s - 1].wait_recv()
+            if s == 1:
+                local.wait()
+            doublings[s].start()
+
+    small_peers = [dp_peer(b) for b in range(bits)] + [mp_peer(b) for b in range(mp_bits)]
+    small_copies = [remote(small_sum.at[i], small_in.at[i], peer) for i, peer in enumerate(small_peers)]
+
+    def small_step(i):
+        if i == 0:
+            small_sum[0] = small_ref[...]
+        else:
+            small_copies[i - 1].wait_recv()
+            if i - 1 < bits:
+                small_sum[i] = small_sum[i - 1] + small_in[i - 1]
+            else:
+                small_sum[i, 8:, :] = small_sum[i - 1, 8:, :]
+                small_sum[i, :8, :] = small_sum[i - 1, :8, :] + small_in[i - 1, :8, :]
+        if i < len(small_peers):
+            small_copies[i].start()
+        else:
+            small_out[...] = small_sum[i]
+
+    def part_rows(position):
+        return pl.ds(pl.multiple_of(jnp.clip(position, 0, n - 1) * t, t), t)
+
+    hops = {}
+    for k in range(1, n):
+        for way in (1, -1):
+            here = (z + k < n) if way == 1 else (z >= k)
+            first = (z == 0) if way == 1 else (z == n - 1)
+            target, device = come[way].at[k - 1], {"mp": z + way}
+            at = next(sems)
+            bare, passed = (
+                pltpu.make_async_remote_copy(source, target, send.at[at], recv.at[at], device, ids)
+                for source in (part.at[part_rows(z + way * k)], come[way].at[min(k, n - 2)])
+            )
+            hops[k, way] = (here & first, here & jnp.logical_not(first), here, bare, passed)
+
+    def line_step(k):
+        for way in (1, -1):
+            first, later, _, bare, passed = hops[k, way]
+            pl.when(first)(bare.start)
+            if k < n - 1:
+
+                @pl.when(later)
+                def _():
+                    hops[k + 1, way][3].wait_recv()
+                    begin = pl.multiple_of(jnp.clip(z + way * k, 0, n - 1) * t, t)
+                    add_rows(come[way].at[k], 0, part, begin, t)
+                    passed.start()
+
+    def line_end():
+        for way, first in ((1, z == 0), (-1, z == n - 1)):
+            pl.when(jnp.logical_not(first))(hops[1, way][3].wait_recv)
+        step = 32
+
+        def body(i, unused):
+            rows = pl.ds(pl.multiple_of(i * step, step), step)
+            total = part[pl.ds(pl.multiple_of(z * t + i * step, step), step), :].astype(F32)
+            for way, first in ((1, z == 0), (-1, z == n - 1)):
+                total = total + jnp.where(first, 0.0, come[way][0, rows, :].astype(F32))
+            norm_ref[rows, :] = total
+            return unused
+
+        lax.fori_loop(0, t // step, body, 0)
+
+    tile = in_tiles.shape[1]
+    tiles = d // tile
+
+    def fetches(j, slot):
+        rows = pl.ds(pl.multiple_of(j * tile, tile), tile)
+        return (
+            pltpu.make_async_copy(in_ref.at[rows], in_tiles.at[slot], fetch.at[slot]),
+            pltpu.make_async_copy(up_ref.at[rows], up_tiles.at[slot], fetch.at[2 + slot]),
+        )
+
+    def product(position):
+        rows = part_rows(position)
+        copy = pltpu.make_async_copy(back_ref.at[rows], chunk, load.at[3])
+        copy.start()
+        copy.wait()
+
+        def one_tile(j, unused):
+            slot = lax.rem(j, 2)
+            for copy in fetches(j, slot):
+                copy.wait()
+            for copy in fetches(lax.rem(j + 1, tiles), 1 - slot):
+                copy.start()
+            cols = pl.ds(pl.multiple_of(j * tile, tile), tile)
+            total = dot(chunk[:, :in_width], in_tiles[slot], NT) * vec_ref[0:1, cols]
+            total = total + dot(chunk[:, in_width:], up_tiles[slot], NT) * vec_ref[2:3, cols]
+            part[rows, cols] = total.astype(BF16)
+            return unused
+
+        lax.fori_loop(0, tiles, one_tile, 0)
+
     for copy in core:
         copy.start()
     own.start()
-    line_step(n - 1)
+    for copy in fetches(0, 0):
+        copy.start()
     small_step(0)
 
-    sums = [first_halving]
-    sums += [functools.partial(next_halving, s) for s in range(1, bits)]
-    sums += [functools.partial(doubling, s) for s in range(bits - 2, -1, -1)]
-    lines = list(range(n - 2, -1, -1))
-    smalls = list(range(1, bits + mp_bits + 1))
+    def one_product(i, unused):
+        distance = (n - 1 - i // 2) * (1 - 2 * lax.rem(i, 2))
+        position = z + distance
+
+        @pl.when(i == 2)
+        def _():
+            line_step(n - 1)
+            first_halving()
+
+        @pl.when((position >= 0) & (position < n))
+        def _():
+            product(position)
+
+        return unused
+
+    lax.fori_loop(0, 2 * (n - 1) + 1, one_product, 0)
+    for copy in fetches(0, 0):
+        copy.wait()
+    sums = [functools.partial(next_halving, s) for s in range(1, bits)]
+    sums += [functools.partial(doubling, s) for s in range(1, bits)]
+    lines = [functools.partial(line_step, k) for k in range(n - 2, 0, -1)] + [line_end]
+    smalls = [functools.partial(small_step, i) for i in range(1, bits + mp_bits + 1)]
+    lines.pop(0)()
     for at, step in enumerate(sums):
         step()
-        if at in (0, bits - 1) or at >= bits:
-            if lines:
-                line_step(lines.pop(0))
+        if at >= bits - 2 and lines:
+            lines.pop(0)()
         if smalls:
-            small_step(smalls.pop(0))
-    for k in lines:
-        line_step(k)
-    for i in smalls:
-        small_step(i)
-    for p in (0, 1):
-        current[p].wait_recv()
-    for copy in core + started + small_copies:
+            smalls.pop(0)()
+    for step in lines + smalls:
+        step()
+    for _, _, doublings in plans:
+        doublings[-1].wait_recv()
+    sent = core + small_copies
+    for halvings, _, doublings in plans:
+        sent = sent + [copy for copy, _, _ in halvings] + doublings
+    for copy in sent:
         copy.wait_send()
-    for copy, here in hops.values():
-
-        @pl.when(here)
-        def _():
-            copy.wait_send()
-
-
-def closing_sums(n, groups, part, cross, small):
-    rows, d = part.shape
-    width = cross.shape[1]
-    t, half = rows // n, d // 2
+    for _, _, here, bare, _ in hops.values():
+        pl.when(here)(bare.wait_send)
+
+
+def closing_sums(n, groups, back, cross, small, flat_in, up_weight, vectors):
+    rows, width = back.shape
+    d = cross.shape[0]
+    t, half, tile = rows // n, d // 2, 256
     bits, mp_bits = groups.bit_length() - 1, n.bit_length() - 1
     stages = [pltpu.VMEM((half // 2 // 2**s, width), BF16) for s in range(1, bits)]
-    copies = 2 + 2 * (bits - 1) + 2 + 2 * (bits - 1) + 2 * (n - 1) + bits + mp_bits
-    whole = pl.BlockSpec(memory_space=pltpu.VMEM)
+    copies = 2 + 4 * (bits - 1) + 2 + 2 * (n - 1) + bits + mp_bits
+    whole, anywhere = pl.BlockSpec(memory_space=pltpu.VMEM), pl.BlockSpec(memory_space=pl.ANY)
     return pl.pallas_call(
         functools.partial(closing_kernel, n, groups),
-        in_specs=[whole, pl.BlockSpec(memory_space=pl.ANY), whole],
-        out_specs=[whole, pl.BlockSpec(memory_space=pl.ANY), whole],
+        in_specs=[anywhere, anywhere, whole, anywhere, anywhere, whole],
+        out_specs=[whole, anywhere, whole],
         out_shape=[
             jax.ShapeDtypeStruct((t, d), F32),
             jax.ShapeDtypeStruct((d, width), BF16),
             jax.ShapeDtypeStruct(small.shape, F32),
         ],
-        scratch_shapes=[pltpu.VMEM((n, t, d), BF16)] * 2
+        scratch_shapes=[pltpu.VMEM((rows, d), BF16)]
+        + [pltpu.VMEM((n - 1, t, d), BF16)] * 2
         + [pltpu.VMEM((half, width), BF16)] * 2
+        + [pltpu.VMEM((t, width), BF16)]
+        + [pltpu.VMEM((2, tile, flat_in.shape[1]), BF16), pltpu.VMEM((2, tile, up_weight.shape[1]), BF16)]
         + stages * 2
         + [pltpu.VMEM((bits + mp_bits,) + small.shape, F32), pltpu.VMEM((bits + mp_bits + 1,) + small.shape, F32)]
         + [pltpu.SemaphoreType.DMA((copies,))] * 2
-        + [pltpu.SemaphoreType.DMA((3,))],
+        + [pltpu.SemaphoreType.DMA((4,))] * 2,
         compiler_params=pltpu.CompilerParams(
-            vmem_limit_bytes=VMEM_LIMIT, collective_id=0, has_side_effects=True
+            vmem_limit_bytes=60 * 1024 * 1024, collective_id=0, has_side_effects=True
         ),
         name="closing_sums",
-    )(part, cross, small)
+    )(back, cross, small, flat_in, up_weight, vectors)
+
+
+def finish_kernel(heads, summed_ref, total_ref, vec_ref, in_ref, up_ref):
+    in_width = heads * 3 * HD
+    for h in range(heads):
+        cols = slice(h * 3 * HD, (h + 1) * 3 * HD)
+        wide = summed_ref[:, cols].astype(F32)
+        in_ref[:, h, :] = wide * vec_ref[:, 0:1] + vec_ref[:, 1:2] * total_ref[0:1, cols]
+    wide = summed_ref[:, in_width:].astype(F32)
+    up_ref[...] = wide * vec_ref[:, 2:3] + vec_ref[:, 3:4] * total_ref[0:1, in_width:]
+
+
+def finish(heads, summed, totals, vectors):
+    d, width = summed.shape
+    in_width = heads * 3 * HD
+    block = 256
+    return pl.pallas_call(
+        functools.partial(finish_kernel, heads),
+        grid=(d // block,),
+        in_specs=[
+            pl.BlockSpec((block, width), lambda i: (i, 0)),
+            pl.BlockSpec((8, width), lambda i: (0, 0)),
+            pl.BlockSpec((block, 8), lambda i: (i, 0)),
+        ],
+        out_specs=[
+            pl.BlockSpec((block, heads, 3 * HD), lambda i: (i, 0, 0)),
+            pl.BlockSpec((block, width - in_width), lambda i: (i, 0)),
+        ],
+        out_shape=[
+            jax.ShapeDtypeStruct((d, heads, 3 * HD), F32),
+            jax.ShapeDtypeStruct((d, width - in_width), F32),
+        ],
+        compiler_params=params(),
+        name="finish",
+    )(summed, totals, vectors)
 
 
 def last_hop(to_right, to_left, n):
     right = lax.ppermute(to_right, "mp", [(i, i + 1) for i in range(n - 1)])
     left = lax.ppermute(to_left, "mp", [(i, i - 1) for i in range(1, n)])
     return right.astype(F32) + left.astype(F32)
-
-
-def exchange(part, own, z, n):
-    came = [None] * (2 * n - 1)
-    came[n - 1] = own
-    for k in range(1, n):
-        came[n - 1 - k] = lax.ppermute(part(z + k), "mp", [(i, i + k) for i in range(n - k)])
-        came[n - 1 + k] = lax.ppermute(part(z - k), "mp", [(i, i - k) for i in range(k, n)])
-    return lax.dynamic_slice_in_dim(jnp.stack(came), n - 1 - z, n, axis=0)
 
 
 def document_starts(row_lengths, length):
@@ -1010,9 +1077,7 @@
 
     flat_in = lax.optimization_barrier(in_weight.reshape(d, in_width))
     share = out_weight.shape[0] // groups
-    out_full = lax.all_gather(
-        lax.dynamic_slice_in_dim(out_weight, group * share, share, axis=0), ("mp", "dp"), axis=0, tiled=True
-    )
+    out_share = lax.dynamic_slice_in_dim(out_weight, group * share, share, axis=0)
 
     starts = document_starts(seq_lengths[0], length)
     first_of_block = starts[::t]
@@ -1032,9 +1097,11 @@
         n, normed.astype(BF16), flat_in, up_weight, down_weight, vectors, in_bias.reshape(1, in_width),
         up_bias[None, :], cosine, sine,
     )
+    out_part = lax.all_gather(after(out_share, slope), "mp", axis=0, tiled=True)
+    out_full = lax.all_gather(out_part, "dp", axis=0, tiled=True)
     joint, logs = attend(t, low, qkv, start_row, joint)
     unused, heads_grad, back, out_down_grad, to_right, to_left = middle(
-        n, in_width, own_grad, down_part, joint, slope, out_weight, down_weight, out_full
+        n, in_width, own_grad, down_part, joint, slope, out_weight, down_weight, out_part
     )
 
     def rows_for(array):
@@ -1043,21 +1110,18 @@
 
         return part
 
-    heads_out = after(joint[:, :heads_width], to_right)
-    heads_mine = exchange(rows_for(heads_out), rows_for(heads_out)(z), z, n)
-    heads_mine = heads_mine.transpose(1, 0, 2).reshape(t, n * heads_width)
+    back = attend_back(
+        t, high, qkv, heads_grad, joint, logs, start_row, cosine, sine, back, out_full
+    )
+    heads_out = after(joint[:, :heads_width], back)
+    heads_mine = lax.all_to_all(heads_out.reshape(n, t, heads_width), "mp", 0, 0)
+    heads_mine = heads_mine.reshape(n, t, groups, share).transpose(1, 2, 0, 3).reshape(t, n * heads_width)
     attn_branch = dot(heads_mine, out_full) + out_bias
     mlp_branch = last_hop(to_right, to_left, n) + rows_for(down_part)(z).astype(F32) + down_bias
     block_out = (own_tokens + attn_branch + mlp_branch).astype(BF16)
     squares = jnp.stack([jnp.sum(attn_branch * attn_branch), jnp.sum(mlp_branch * mlp_branch)])
 
-    back = attend_back(
-        t, high, qkv, heads_grad, joint, logs, start_row, cosine, sine, back, out_down_grad
-    )
-    out_down_grad = lax.psum(out_down_grad, "dp")
-    norm_part = (
-        dot(back[:, :in_width], flat_in, NT) * attn_gain + dot(back[:, in_width:], up_weight, NT) * mlp_gain
-    ).astype(BF16)
+    out_down_grad = lax.psum(after(out_down_grad, out_full), "dp")
     cross, row_sums, total = cross_products(heads_width, x_rows, back, flat_in, up_weight)
     total = total[0]
     attn_sums = row_sums[:, 0:2].T
@@ -1075,17 +1139,13 @@
             jnp.zeros((6, d), F32),
         ]
     )
-    norm_grad, cross, small = closing_sums(n, groups, norm_part, cross, small)
+    norm_grad, cross, small = closing_sums(n, groups, back, cross, small, flat_in, up_weight, vectors)
     mean_grad = jnp.mean(norm_grad, axis=-1, keepdims=True)
     mean_normed = jnp.mean(norm_grad * normed, axis=-1, keepdims=True)
     tokens_grad = (own_grad.astype(F32) + spread * (norm_grad - mean_grad - normed * mean_normed)).astype(BF16)
     in_total, up_total = small[8, :in_width], small[9, :hidden]
-    in_cross = lax.optimization_barrier(cross[:, :in_width].reshape(d, local_heads, 3 * HD))
-    grad_in_weight = (
-        in_cross.astype(F32) * attn_gain[:, None, None]
-        + attn_shift[:, None, None] * in_total.reshape(local_heads, 3 * HD)[None]
-    )
-    grad_up_weight = cross[:, in_width:].astype(F32) * mlp_gain[:, None] + mlp_shift[:, None] * up_total[None, :]
+    totals = jnp.broadcast_to(jnp.concatenate([in_total, up_total])[None], (8, in_width + hidden))
+    grad_in_weight, grad_up_weight = finish(local_heads, cross, totals, vectors.T)
     element_count = float(groups * n * t * d)
     return (
         block_out[None],

time: 878 us -> 771 us (0.88)
  matrix products: 59.7 us -> 12.6 us
  waiting for transfers between devices: 36.5 us -> 1.15 us
  Pallas kernels: 627 us -> 658 us
  local copies, waits for them, and re-layouts: 52.9 us -> 28.1 us
  other arithmetic: 57.7 us -> 37.4 us
    pallas_call x1 -> x2, Pallas kernels: 164 us -> 230 us  [the longest x1 212 us: closing_sums(): pl.pallas_call(functools.partial(closing_kernel, n, groups), in_specs=[an...]
    dot_general x3 -> x1, matrix products: 59.7 us -> 12.6 us  [dot(): return lax.dot_general(a, b, dims, preferred_element_type=F32)]
    ppermute x6 -> x0, waiting for transfers between devices: 36.4 us -> none  [the longest x3 36.4 us: exchange(): lax.ppermute(part(z - k), 'mp', [(i, i - k) for i in range(k, n)])]
    pallas_call x1, Pallas kernels: 198 us -> 161 us  [opening(): pl.pallas_call(functools.partial(opening_kernel, n, heads), in_specs=[any...]
    add x2 -> x0, other arithmetic: 19.8 us -> none  [the longest x1 10.3 us: per_device(): cross[:, in_width:].astype(F32) * mlp_gain[:, None]]
    ppermute x6 -> x0, starting transfers between devices: 10.6 us -> none  [the longest x3 6.73 us: exchange(): lax.ppermute(part(z + k), 'mp', [(i, i + k) for i in range(n - k)])]
    reshape x1, local copies, waits for them, and re-layouts: 13.5 us -> 4.13 us  [per_device(): heads_out.reshape(n, t, heads_width)]
  transfers between devices with their start and end apart: 10 -> 6, of which waited for: 2 -> 1; matrix products, arithmetic and copies ran while one was open for 15% -> 5% of each run, Pallas kernels for 50% -> 65%
where the time goes in v4:
time: 771 us; the launch traced here: 763 us
  Pallas kernels  658 us (85%)
  other arithmetic  37.4 us (5%)
  local copies, waits for them, and re-layouts  28.1 us (4%)
  between operations  14.3 us (2%)
  matrix products  12.6 us (2%)
  starting transfers between devices  11.5 us (1%)
    pallas_call x1, Pallas kernels, closing_sums(): pl.pallas_call(functools.partial(closing_kernel, n, groups), in_specs=[an...  212 us
    pallas_call x1, Pallas kernels, middle(): pl.pallas_call(functools.partial(middle_kernel, n, in_width), in_specs=[a...  167 us
    pallas_call x1, Pallas kernels, opening(): pl.pallas_call(functools.partial(opening_kernel, n, heads), in_specs=[any...  161 us
    pallas_call x1, Pallas kernels, cross_products(): pl.pallas_call(functools.partial(cross_kernel, heads_tile), grid=(d // ti...  45.8 us
    pallas_call x1, Pallas kernels, attend_back(): pl.pallas_call(functools.partial(attend_back_kernel, t, heads), grid=(1,)...  30.6 us
    pallas_call x1, Pallas kernels, attend(): pl.pallas_call(functools.partial(attend_kernel, t, heads), grid=(1,), in_...  22.6 us
    pallas_call x1, Pallas kernels, finish(): pl.pallas_call(functools.partial(finish_kernel, heads), grid=(d // block,...  17.6 us
  transfers between devices with their start and end apart: 6, of which 1 were waited for; matrix products, arithmetic and copies ran while one was open for 5% of the time, Pallas kernels for 65%

profile of v4, /device:TPU:0, one launch (start us, length us, event | category | flops | bytes accessed | tf_op | source)
XLA Modules:
  0.0 762.9 jit_solution(5978872774594411781)
XLA Ops:
  9.0 2.1 convert_reduce_fusion.1
  11.1 2.6 fusion.10
  13.7 1.9 fusion.6.refs_0_
  15.7 4.1 copy.70
  20.3 3.7 fusion.16
  26.5 1.9 maximum_maximum_fusion
  28.4 161.5 %opening.1 = (bf16[2048,2048]{1,0:T(8,128)(2,1)}, bf16[2048,1536]{1,0:T(8,128)(2,1)}, bf16[2048,2560]{1,0:T(8,128)(2,1)}, bf16[2048,2048]{1,0:T(8,128)(2,1)}, bf16[2048,2048]{1,0:T(8,128)(2,1)}) custom-call(bf16[512,2048]{1,0:T(8,128)(2,1)} %fusion.6.refs_0_, bf16[2048,1536]{1,0:T(8,128)(2,1)} %bitcast.80, bf16[2048,2048]{1,0:T(8,128)(2,1)} %refs_4_.3, ...), custom_call_target="tpu_custom_call" | custom-call | flops 755914244096 | bytes 209715200 | tf_op jit(solution)/shard_map/opening/pallas_call | solution.py:241
  193.0 22.6 %attend.1 = (bf16[2048,2560]{1,0:T(8,128)(2,1)}, f32[2,2048]{1,0:T(2,128)}) custom-call(s32[4]{0:T(128)} %and_select_fusion.low_ref, bf16[2048,1536]{1,0:T(8,128)(2,1)} %get-tuple-element.35.qkv_ref, s32[1,2048]{1,0:T(1,128)} %bitcast.88, bf16[2048,2560]{1,0:T(8,128)(2,1)} %get-tuple-element.36.held_ref), custom_call_target="tpu_custom_call", output_to_operand_aliasing={{0}: (3, {})} | custom-call | flops 4294967296 | bytes 6291456 | tf_op jit(solution)/shard_map/attend/pallas_call | solution.py:608
  215.6 3.2 slice.57.refs_0_
  220.4 167.2 %middle.1 = (bf16[2048,2048]{1,0:T(8,128)(2,1)}, bf16[2048,512]{1,0:T(8,128)(2,1)}, bf16[2048,3584]{1,0:T(8,128)(2,1)}, bf16[2560,2048]{1,0:T(8,128)(2,1)}, bf16...) custom-call(bf16[512,2048]{1,0:T(8,128)(2,1)} %bitcast.84, bf16[2048,2048]{1,0:T(8,128)(2,1)} %get-tuple-element.38.refs_1_, ...), custom_call_target="tpu_custom_call" | custom-call | flops 687194767360 | bytes 209715200 | tf_op jit(solution)/shard_map/middle/pallas_call | solution.py:448
  387.6 2.6 collective-permute-start
  391.5 30.6 %attend_back.1.refs_1_.back_ref.refs_0_ = bf16[2048,3584]{1,0:T(8,128)(2,1)} custom-call(s32[8]{0:T(128)} %convert_reduce_fusion.2.high_ref, bf16[2048,1536]{1,0:T(8,128)(2,1)} %get-tuple-element.35.qkv_ref, bf16[2048,512]{1,0:T(8,128)(2,1)} %get-tuple-element.40.grad_ref, ...), custom_call_target="tpu_custom_call", output_to_operand_aliasing={{}: (8, {})} | custom-call | flops 10737418240 | bytes 12582912 | tf_op jit(solution)/shard_map/attend_back/pallas_call | solution.py:703
  422.2 4.1 copy.65
  426.3 6.9 all-to-all-start
  433.9 45.8 %cross.1 = (bf16[2048,3584]{1,0:T(8,128)(2,1)}, f32[2048,128]{1,0:T(8,128)}, f32[8,3584]{1,0:T(8,128)}) custom-call(bf16[2048,2048]{1,0:T(8,128)(2,1)} %get-tuple-element.45.x_ref, bf16[2048,3584]{1,0:T(8,128)(2,1)} %attend_back.1.refs_1_.back_ref.refs_0_, bf16[2048,1536]{1,0:T(8,128)(2,1)} %bitcast.81, bf16[2048,2048]{1,0:T(8,128)(2,1)} %refs_4_.3), custom_call_target="tpu_custom_call" | custom-call | flops 30064771072 | bytes 52428800 | tf_op jit(solution)/shard_map/cross/pallas_call | solution.py:526
  479.8 1.7 copy.67
  483.8 1.7 copy.66
  485.6 12.6 %multiply_reduce_fusion = (f32[]{:T(128)}, bf16[1,512,2048]{2,1,0:T(8,128)(2,1)}, f32[]{:T(128)}) fusion(bf16[512,2048]{1,0:T(8,128)(2,1)} %collective-permute-done.1, bf16[512,2048]{1,0:T(8,128)(2,1)} %collective-permute-done, f32[2048]{0:T(1024)S(1)} %copy-done.20, bf16[2048,2048]{1,0:T(8,128)(2,1)} %get-tuple-element.38.refs_1_, s32[]{:T(128)S(6)} %select_n.18, ...), kind=kOutput, calls=%fused_computation.19 | convolution fusion | flops 4310695936 | bytes 20987916 | tf_op jit(solution)/shard_map/dot_general | solution.py:26
  501.0 212.4 %closing_sums.1 = (f32[512,2048]{1,0:T(8,128)}, bf16[2048,3584]{1,0:T(8,128)(2,1)}, f32[16,2048]{1,0:T(8,128)}) custom-call(bf16[2048,3584]{1,0:T(8,128)(2,1)} %attend_back.1.refs_1_.back_ref.refs_0_, bf16[2048,3584]{1,0:T(8,128)(2,1)} %get-tuple-element.46.refs_1_, f32[16,2048]{1,0:T(8,128)} %concatenate.14.refs_2_, bf16[2048,1536]{1,0:T(8,128)(2,1)} %bitcast.82, ...), custom_call_target="tpu_custom_call" | custom-call | tf_op jit(solution)/shard_map/closing_sums/pallas_call | solution.py:987
  713.4 1.7 fusion.18
  717.2 17.6 %finish.1 = (f32[2048,2,768]{2,1,0:T(2,128)}, f32[2048,2048]{1,0:T(8,128)}) custom-call(bf16[2048,3584]{1,0:T(8,128)(2,1)} %get-tuple-element.51.summed_ref, f32[8,3584]{1,0:T(8,128)} %broadcast_in_dim.75.total_ref, f32[2048,8]{1,0:T(8,128)} %bitcast.86), custom_call_target="tpu_custom_call" | custom-call | tf_op jit(solution)/shard_map/finish/pallas_call | solution.py:1026
  737.1 2.7 fusion.14
  739.7 11.7 %slice_convert_fusion = f32[2048,2048]{1,0:T(8,128)} fusion(bf16[2560,2048]{1,0:T(8,128)(2,1)} %all-reduce.4.cloned.1.call-done), kind=kLoop, calls=%fused_computation | loop fusion | flops 4194304 | bytes 25165824 | tf_op jit(solution)/shard_map/convert_element_type | solution.py:1163
  751.4 4.1 slice_convert_fusion.1
  (96 shorter events, 21.4 us)
Async XLA Ops:
  7.2 6.6 copy-start
  7.2 213.2 %all-gather.3.cloned.1.call-start = ((), (), s32[]{:S(2)}) async-start(), calls=%async_computation.1 | async-start | bytes 1310720 | tf_op jit(solution)/shard_map/all_gather | solution.py:1100
  9.0 6.6 copy-start.5
  11.1 8.6 %copy-start.8 = (f32[512]{0:T(512)}, f32[512]{0:T(512)S(1)}, u32[]{:S(2)}) copy-start(f32[512]{0:T(512)S(1)} %broadcast_multiply_fusion.2) | copy-start | bytes 6148
  13.7 6.0 copy-start.10
  15.6 4.1 copy-start.19
  15.6 10.1 %copy-start.13 = (f32[2048]{0:T(1024)S(1)}, f32[2048]{0:T(1024)}, u32[]{:S(2)}) copy-start(f32[2048]{0:T(1024)} %param.18) | copy-start | bytes 24580
  15.6 10.1 %copy-start.14 = (f32[2048]{0:T(1024)S(1)}, f32[2048]{0:T(1024)}, u32[]{:S(2)}) copy-start(f32[2048]{0:T(1024)} %param.19) | copy-start | bytes 24580
  15.6 10.1 %copy-start.15 = (f32[2048]{0:T(1024)S(1)}, f32[2048]{0:T(1024)}, u32[]{:S(2)}) copy-start(f32[2048]{0:T(1024)} %param.20) | copy-start | bytes 24580
  15.6 10.1 %copy-start.16 = (f32[2048]{0:T(1024)S(1)}, f32[2048]{0:T(1024)}, u32[]{:S(2)}) copy-start(f32[2048]{0:T(1024)} %param.21) | copy-start | bytes 24580
  189.9 201.6 %all-gather.5.cloned.1.call-start = ((), (), s32[]{:S(2)}) async-start(), calls=%async_computation.2 | async-start | bytes 9437184 | tf_op jit(solution)/shard_map/all_gather | solution.py:1101
  387.6 97.9 %collective-permute-start = (bf16[512,2048]{1,0:T(8,128)(2,1)}, bf16[512,2048]{1,0:T(8,128)(2,1)}, u32[]{:S(2)}, u32[]{:S(2)}) collective-permute-start(bf16[512,2048]{1,0:T(8,128)(2,1)} %get-tuple-element.43), channel_id=1, source_target_pairs={{0,1},{1,2},{2,3},{4,5},{5,6},{6,7},{8,9},{9,10},{10,11},{12,13},{... | collective-permute-start | bytes 6291464 | tf_op jit(solution)/shard_map/ppermute | solution.py:1048
  390.2 95.3 %collective-permute-start.1 = (bf16[512,2048]{1,0:T(8,128)(2,1)}, bf16[512,2048]{1,0:T(8,128)(2,1)}, u32[]{:S(2)}, u32[]{:S(2)}) collective-permute-start(bf16[512,2048]{1,0:T(8,128)(2,1)} %get-tuple-element.44), channel_id=1, source_target_pairs={{1,0},{2,1},{3,2},{5,4},{6,5},{7,6},{9,8},{10,9},{11,10},{13,12},{... | collective-permute-start | bytes 6291464 | tf_op jit(solution)/shard_map/ppermute | solution.py:1049
  426.3 57.5 %all-to-all-start = ((bf16[4,512,512]{1,2,0:T(8,128)(2,1)}), bf16[4,512,512]{1,2,0:T(8,128)(2,1)}, u32[]{:S(2)}, u32[]{:S(2)}) async-start(bf16[4,512,512]{1,2,0:T(8,128)(2,1)} %copy.65), calls=%async_computation | async-start | bytes 4194304 | tf_op jit(solution)/shard_map/all_to_all | solution.py:1117
  433.2 306.5 %all-reduce.4.cloned.1.call-start = ((), (), s32[]{:S(2)}) async-start(), calls=%async_computation.3 | async-start | bytes 20971520 | tf_op jit(solution)/shard_map/psum | solution.py:1124
  479.7 5.8 copy-start.1
  479.7 5.8 copy-start.20
  479.7 5.8 copy-start.21
  485.6 14.0 %copy-start.12 = (f32[2048]{0:T(1024)S(1)}, f32[2048]{0:T(1024)}, u32[]{:S(2)}) copy-start(f32[2048]{0:T(1024)} %convert_reduce_fusion) | copy-start | bytes 24580
  715.1 19.7 %copy-start.18 = (f32[1,2048]{1,0:T(1,128)}, f32[1,2048]{1,0:T(1,128)S(1)}, u32[]{:S(2)}) copy-start(f32[1,2048]{1,0:T(1,128)S(1)} %get-tuple-element.63) | copy-start | bytes 24580
  715.1 40.5 %copy-start.17 = (f32[1,2048]{1,0:T(1,128)}, f32[1,2048]{1,0:T(1,128)S(1)}, u32[]{:S(2)}) copy-start(f32[1,2048]{1,0:T(1,128)S(1)} %get-tuple-element.62) | copy-start | bytes 24580
  717.2 17.6 %copy-start.2 = (f32[512,2048]{1,0:T(8,128)S(1)}, f32[512,2048]{1,0:T(8,128)}, u32[]{:S(2)}) copy-start(f32[512,2048]{1,0:T(8,128)} %get-tuple-element.49) | copy-start | bytes 12582916
  717.2 17.6 %copy-start.9 = (f32[512]{0:T(512)S(1)}, f32[512]{0:T(512)}, u32[]{:S(2)}) copy-start(f32[512]{0:T(512)} %copy-done.8) | copy-start | bytes 6148
  717.2 17.6 %copy-start.11 = (f32[512]{0:T(512)S(1)}, f32[512]{0:T(512)}, u32[]{:S(2)}) copy-start(f32[512]{0:T(512)} %copy-done.10) | copy-start | bytes 6148
  (4 other events, 8.0 us)
Sparse Core Ops, SparseCore 0:
  190.1 27.8 all-gather.2
  220.5 56.3 all-gather.4
  437.5 204.1 all-reduce.3

commit v5 on v4

--- a/solution.py
+++ b/solution.py
@@ -481,7 +481,7 @@
     )(g, down_part, joint, slope, out_weight, down_weight, earlier)
 
 
-def cross_kernel(heads_tile, x_ref, back_ref, in_ref, up_ref, cross_ref, sums_ref, total_ref, xt_ref):
+def cross_kernel(heads_tile, x_ref, back_ref, in_ref, up_ref, earlier_ref, cross_ref, sums_ref, total_ref, xt_ref):
     width, in_width = back_ref.shape[1], in_ref.shape[1]
     tile = heads_tile
 
@@ -518,7 +518,7 @@
     sums_ref[...] = out
 
 
-def cross_products(heads_tile, x_rows, back, flat_in, up_weight):
+def cross_products(heads_tile, x_rows, back, flat_in, up_weight, earlier):
     rows, d = x_rows.shape
     width = back.shape[1]
     tile = 512
@@ -531,6 +531,7 @@
             pl.BlockSpec((rows, width), lambda i: (0, 0), pipeline_mode=once),
             pl.BlockSpec((tile, flat_in.shape[1]), lambda i: (i, 0)),
             pl.BlockSpec((tile, up_weight.shape[1]), lambda i: (i, 0)),
+            pl.BlockSpec(memory_space=pl.ANY),
         ],
         out_specs=[
             pl.BlockSpec((tile, width), lambda i: (i, 0)),
@@ -548,7 +549,7 @@
             flops=2 * rows * d * width, bytes_accessed=2 * (rows * d + rows * width + 2 * d * width), transcendentals=0
         ),
         name="cross",
-    )(x_rows, back, flat_in, up_weight)
+    )(x_rows, back, flat_in, up_weight, earlier)
 
 
 def allowed(j, i, t, start):
@@ -739,6 +740,7 @@
 
 def closing_kernel(n, groups, *refs):
     bits, mp_bits = groups.bit_length() - 1, n.bit_length() - 1
+    refs = refs[:6] + refs[7:]
     back_ref, cross_ref, small_ref, in_ref, up_ref, vec_ref, norm_ref, summed_ref, small_out = refs[:9]
     part = refs[9]
     come = {1: refs[10], -1: refs[11]}
@@ -976,7 +978,7 @@
         pl.when(here)(bare.wait_send)
 
 
-def closing_sums(n, groups, back, cross, small, flat_in, up_weight, vectors):
+def closing_sums(n, groups, back, cross, small, flat_in, up_weight, vectors, earlier):
     rows, width = back.shape
     d = cross.shape[0]
     t, half, tile = rows // n, d // 2, 256
@@ -986,7 +988,7 @@
     whole, anywhere = pl.BlockSpec(memory_space=pltpu.VMEM), pl.BlockSpec(memory_space=pl.ANY)
     return pl.pallas_call(
         functools.partial(closing_kernel, n, groups),
-        in_specs=[anywhere, anywhere, whole, anywhere, anywhere, whole],
+        in_specs=[anywhere, anywhere, whole, anywhere, anywhere, whole, anywhere],
         out_specs=[whole, anywhere, whole],
         out_shape=[
             jax.ShapeDtypeStruct((t, d), F32),
@@ -1006,10 +1008,10 @@
             vmem_limit_bytes=60 * 1024 * 1024, collective_id=0, has_side_effects=True
         ),
         name="closing_sums",
-    )(back, cross, small, flat_in, up_weight, vectors)
-
-
-def finish_kernel(heads, summed_ref, total_ref, vec_ref, in_ref, up_ref):
+    )(back, cross, small, flat_in, up_weight, vectors, earlier)
+
+
+def finish_kernel(heads, summed_ref, total_ref, vec_ref, out_low, down_low, in_ref, up_ref, out_ref, down_ref):
     in_width = heads * 3 * HD
     for h in range(heads):
         cols = slice(h * 3 * HD, (h + 1) * 3 * HD)
@@ -1017,12 +1019,18 @@
         in_ref[:, h, :] = wide * vec_ref[:, 0:1] + vec_ref[:, 1:2] * total_ref[0:1, cols]
     wide = summed_ref[:, in_width:].astype(F32)
     up_ref[...] = wide * vec_ref[:, 2:3] + vec_ref[:, 3:4] * total_ref[0:1, in_width:]
-
-
-def finish(heads, summed, totals, vectors):
+    out_ref[...] = out_low[...].astype(F32)
+    down_ref[...] = down_low[...].astype(F32)
+
+
+def finish(heads, summed, totals, vectors, out_down):
     d, width = summed.shape
-    in_width = heads * 3 * HD
+    in_width, heads_width = heads * 3 * HD, heads * HD
     block = 256
+    steps = d // block
+    hidden = width - in_width
+    out_rows, down_rows = heads_width // steps, hidden // steps
+    first = heads_width // down_rows
     return pl.pallas_call(
         functools.partial(finish_kernel, heads),
         grid=(d // block,),
@@ -1030,24 +1038,30 @@
             pl.BlockSpec((block, width), lambda i: (i, 0)),
             pl.BlockSpec((8, width), lambda i: (0, 0)),
             pl.BlockSpec((block, 8), lambda i: (i, 0)),
+            pl.BlockSpec((out_rows, d), lambda i: (i, 0)),
+            pl.BlockSpec((down_rows, d), lambda i: (first + i, 0)),
         ],
         out_specs=[
             pl.BlockSpec((block, heads, 3 * HD), lambda i: (i, 0, 0)),
-            pl.BlockSpec((block, width - in_width), lambda i: (i, 0)),
+            pl.BlockSpec((block, hidden), lambda i: (i, 0)),
+            pl.BlockSpec((out_rows, d), lambda i: (i, 0)),
+            pl.BlockSpec((down_rows, d), lambda i: (i, 0)),
         ],
         out_shape=[
             jax.ShapeDtypeStruct((d, heads, 3 * HD), F32),
-            jax.ShapeDtypeStruct((d, width - in_width), F32),
+            jax.ShapeDtypeStruct((d, hidden), F32),
+            jax.ShapeDtypeStruct((heads_width, d), F32),
+            jax.ShapeDtypeStruct((hidden, d), F32),
         ],
         compiler_params=params(),
         name="finish",
-    )(summed, totals, vectors)
+    )(summed, totals, vectors, out_down, out_down)
 
 
 def last_hop(to_right, to_left, n):
     right = lax.ppermute(to_right, "mp", [(i, i + 1) for i in range(n - 1)])
     left = lax.ppermute(to_left, "mp", [(i, i - 1) for i in range(1, n)])
-    return right.astype(F32) + left.astype(F32)
+    return right, left
 
 
 def document_starts(row_lengths, length):
@@ -1113,16 +1127,19 @@
     back = attend_back(
         t, high, qkv, heads_grad, joint, logs, start_row, cosine, sine, back, out_full
     )
-    heads_out = after(joint[:, :heads_width], back)
-    heads_mine = lax.all_to_all(heads_out.reshape(n, t, heads_width), "mp", 0, 0)
-    heads_mine = heads_mine.reshape(n, t, groups, share).transpose(1, 2, 0, 3).reshape(t, n * heads_width)
+    from_left, from_right = last_hop(to_right, to_left, n)
+    heads_out = after(joint[:, :heads_width], back, from_left, from_right)
+    heads_here = lax.all_to_all(heads_out.reshape(n, t, heads_width), "mp", 0, 0)
+    heads_mine = heads_here.reshape(n, t, groups, share).transpose(1, 2, 0, 3).reshape(t, n * heads_width)
     attn_branch = dot(heads_mine, out_full) + out_bias
-    mlp_branch = last_hop(to_right, to_left, n) + rows_for(down_part)(z).astype(F32) + down_bias
+    mlp_branch = from_left.astype(F32) + from_right.astype(F32) + rows_for(down_part)(z).astype(F32) + down_bias
     block_out = (own_tokens + attn_branch + mlp_branch).astype(BF16)
     squares = jnp.stack([jnp.sum(attn_branch * attn_branch), jnp.sum(mlp_branch * mlp_branch)])
 
-    out_down_grad = lax.psum(after(out_down_grad, out_full), "dp")
-    cross, row_sums, total = cross_products(heads_width, x_rows, back, flat_in, up_weight)
+    grad_share = lax.psum_scatter(after(out_down_grad, out_full), "dp", scatter_dimension=0, tiled=True)
+    cross, row_sums, total = cross_products(heads_width, x_rows, back, flat_in, up_weight, heads_out)
+    grad_share = after(grad_share, row_sums, heads_here)
+    out_down_grad = lax.all_gather(grad_share, "dp", axis=0, tiled=True)
     total = total[0]
     attn_sums = row_sums[:, 0:2].T
     mlp_sums = row_sums[:, 2:4].T
@@ -1139,13 +1156,15 @@
             jnp.zeros((6, d), F32),
         ]
     )
-    norm_grad, cross, small = closing_sums(n, groups, back, cross, small, flat_in, up_weight, vectors)
+    norm_grad, cross, small = closing_sums(n, groups, back, cross, small, flat_in, up_weight, vectors, grad_share)
     mean_grad = jnp.mean(norm_grad, axis=-1, keepdims=True)
     mean_normed = jnp.mean(norm_grad * normed, axis=-1, keepdims=True)
     tokens_grad = (own_grad.astype(F32) + spread * (norm_grad - mean_grad - normed * mean_normed)).astype(BF16)
     in_total, up_total = small[8, :in_width], small[9, :hidden]
     totals = jnp.broadcast_to(jnp.concatenate([in_total, up_total])[None], (8, in_width + hidden))
-    grad_in_weight, grad_up_weight = finish(local_heads, cross, totals, vectors.T)
+    grad_in_weight, grad_up_weight, grad_out_weight, grad_down_weight = finish(
+        local_heads, cross, totals, vectors.T, out_down_grad
+    )
     element_count = float(groups * n * t * d)
     return (
         block_out[None],
@@ -1156,11 +1175,11 @@
         small[3],
         grad_in_weight,
         in_total.reshape(local_heads, 3 * HD),
-        out_down_grad[:heads_width].astype(F32),
+        grad_out_weight,
         small[4],
         grad_up_weight,
         up_total,
-        out_down_grad[heads_width:].astype(F32),
+        grad_down_weight,
         small[4],
         jnp.sqrt(small[5, :2] / element_count),
     )

time: 771 us -> 749 us (0.971)
  Pallas kernels: 658 us -> 641 us
  other arithmetic: 37.4 us -> 25 us
  waiting for transfers between devices: 1.15 us -> 13.1 us
    pallas_call x1, Pallas kernels: 212 us -> 185 us  [closing_sums(): pl.pallas_call(functools.partial(closing_kernel, n, groups), in_specs=[an...]
    convert_element_type x2 -> x0, other arithmetic: 15.8 us -> none  [the longest x1 11.7 us: per_device(): out_down_grad[heads_width:].astype(F32)]
    pallas_call x1, Pallas kernels: 17.6 us -> 27.3 us  [finish(): pl.pallas_call(functools.partial(finish_kernel, heads), grid=(d // block,...]
  transfers between devices with their start and end apart: 6 -> 7, of which waited for: 1 -> 3; matrix products, arithmetic and copies ran while one was open for 5% -> 6% of each run, Pallas kernels for 65% -> 61%
where the time goes in v5:
time: 749 us; the launch traced here: 741 us
  Pallas kernels  641 us (86%)
  local copies, waits for them, and re-layouts  29 us (4%)
  other arithmetic  25 us (3%)
  between operations  14.3 us (2%)
  waiting for transfers between devices  13.1 us (2%)
  matrix products  11.8 us (2%)
    pallas_call x1, Pallas kernels, closing_sums(): pl.pallas_call(functools.partial(closing_kernel, n, groups), in_specs=[an...  185 us
    pallas_call x1, Pallas kernels, middle(): pl.pallas_call(functools.partial(middle_kernel, n, in_width), in_specs=[a...  165 us
    pallas_call x1, Pallas kernels, opening(): pl.pallas_call(functools.partial(opening_kernel, n, heads), in_specs=[any...  161 us
    pallas_call x1, Pallas kernels, cross_products(): pl.pallas_call(functools.partial(cross_kernel, heads_tile), grid=(d // ti...  46 us
    pallas_call x1, Pallas kernels, attend_back(): pl.pallas_call(functools.partial(attend_back_kernel, t, heads), grid=(1,)...  33.6 us
    pallas_call x1, Pallas kernels, finish(): pl.pallas_call(functools.partial(finish_kernel, heads), grid=(d // block,...  27.3 us
    pallas_call x1, Pallas kernels, attend(): pl.pallas_call(functools.partial(attend_kernel, t, heads), grid=(1,), in_...  22.6 us
  transfers between devices with their start and end apart: 7, of which 3 were waited for; matrix products, arithmetic and copies ran while one was open for 6% of the time, Pallas kernels for 61%

profile of v5, /device:TPU:0, one launch (start us, length us, event | category | flops | bytes accessed | tf_op | source)
XLA Modules:
  0.0 741.1 jit_solution(3454571728937595267)
XLA Ops:
  9.0 2.1 convert_reduce_fusion.1
  11.1 2.6 fusion.10
  13.7 1.9 fusion.6.refs_0_
  15.7 4.1 copy.71
  20.3 3.7 fusion.16
  26.5 1.9 maximum_maximum_fusion
  28.4 161.4 %opening.1 = (bf16[2048,2048]{1,0:T(8,128)(2,1)}, bf16[2048,1536]{1,0:T(8,128)(2,1)}, bf16[2048,2560]{1,0:T(8,128)(2,1)}, bf16[2048,2048]{1,0:T(8,128)(2,1)}, bf16[2048,2048]{1,0:T(8,128)(2,1)}) custom-call(bf16[512,2048]{1,0:T(8,128)(2,1)} %fusion.6.refs_0_, bf16[2048,1536]{1,0:T(8,128)(2,1)} %bitcast.80, bf16[2048,2048]{1,0:T(8,128)(2,1)} %refs_4_.3, ...), custom_call_target="tpu_custom_call" | custom-call | flops 755914244096 | bytes 209715200 | tf_op jit(solution)/shard_map/opening/pallas_call | solution.py:241
  191.2 22.6 %attend.1 = (bf16[2048,2560]{1,0:T(8,128)(2,1)}, f32[2,2048]{1,0:T(2,128)}) custom-call(s32[4]{0:T(128)} %and_select_fusion.low_ref, bf16[2048,1536]{1,0:T(8,128)(2,1)} %get-tuple-element.37.qkv_ref, s32[1,2048]{1,0:T(1,128)} %bitcast.89, bf16[2048,2560]{1,0:T(8,128)(2,1)} %get-tuple-element.38.held_ref), custom_call_target="tpu_custom_call", output_to_operand_aliasing={{0}: (3, {})} | custom-call | flops 4294967296 | bytes 6291456 | tf_op jit(solution)/shard_map/attend/pallas_call | solution.py:609
  213.8 4.1 all-gather.4.cloned.1.call-done.refs_6_
  218.0 164.9 %middle.1 = (bf16[2048,2048]{1,0:T(8,128)(2,1)}, bf16[2048,512]{1,0:T(8,128)(2,1)}, bf16[2048,3584]{1,0:T(8,128)(2,1)}, bf16[2560,2048]{1,0:T(8,128)(2,1)}, bf16...) custom-call(bf16[512,2048]{1,0:T(8,128)(2,1)} %bitcast.85, bf16[2048,2048]{1,0:T(8,128)(2,1)} %get-tuple-element.40.refs_1_, ...), custom_call_target="tpu_custom_call" | custom-call | flops 687194767360 | bytes 209715200 | tf_op jit(solution)/shard_map/middle/pallas_call | solution.py:448
  385.8 3.0 slice.51.refs_0_
  389.4 33.6 %attend_back.1.refs_1_.back_ref.refs_0_ = bf16[2048,3584]{1,0:T(8,128)(2,1)} custom-call(s32[8]{0:T(128)} %convert_reduce_fusion.2.high_ref, bf16[2048,1536]{1,0:T(8,128)(2,1)} %get-tuple-element.37.qkv_ref, bf16[2048,512]{1,0:T(8,128)(2,1)} %get-tuple-element.42.grad_ref, ...), custom_call_target="tpu_custom_call", output_to_operand_aliasing={{}: (8, {})} | custom-call | flops 10737418240 | bytes 12582912 | tf_op jit(solution)/shard_map/attend_back/pallas_call | solution.py:704
  423.0 4.6 collective-permute-done.refs_2_
  427.6 4.2 collective-permute-done.1.refs_3_
  431.9 3.6 all-to-all-start
  436.0 46.0 %cross.1 = (bf16[2048,3584]{1,0:T(8,128)(2,1)}, f32[2048,128]{1,0:T(8,128)}, f32[8,3584]{1,0:T(8,128)}) custom-call(bf16[2048,2048]{1,0:T(8,128)(2,1)} %get-tuple-element.47.x_ref, bf16[2048,3584]{1,0:T(8,128)(2,1)} %attend_back.1.refs_1_.back_ref.refs_0_, bf16[2048,1536]{1,0:T(8,128)(2,1)} %bitcast.81, bf16[2048,2048]{1,0:T(8,128)(2,1)} %refs_4_.3, ...), custom_call_target="tpu_custom_call" | custom-call | flops 30064771072 | bytes 52428800 | tf_op jit(solution)/shard_map/cross/pallas_call | solution.py:526
  484.7 2.0 convert_reduce_fusion
  488.7 4.3 copy.66
  493.1 2.1 copy.67
  495.7 11.8 %multiply_reduce_fusion = (f32[]{:T(128)}, bf16[1,512,2048]{2,1,0:T(8,128)(2,1)}, f32[]{:T(128)}) fusion(bf16[512,2048]{1,0:T(8,128)(2,1)} %collective-permute-done.1.refs_3_, bf16[512,2048]{1,0:T(8,128)(2,1)S(1)} %copy-done.8, f32[2048]{0:T(1024)S(1)} %copy-done.22, bf16[2048,2048]{1,0:T(8,128)(2,1)} %get-tuple-element.40.refs_1_, s32[]{:T(128)S(6)} %select_n.18, ...), kind=kOutput, calls=%fused_computation.18 | convolution fusion | flops 4310695936 | bytes 20987916 | tf_op jit(solution)/shard_map/dot_general | solution.py:26
  510.3 185.1 %closing_sums.1 = (f32[512,2048]{1,0:T(8,128)}, bf16[2048,3584]{1,0:T(8,128)(2,1)}, f32[16,2048]{1,0:T(8,128)}) custom-call(bf16[2048,3584]{1,0:T(8,128)(2,1)} %attend_back.1.refs_1_.back_ref.refs_0_, bf16[2048,3584]{1,0:T(8,128)(2,1)} %get-tuple-element.48.refs_1_, f32[16,2048]{1,0:T(8,128)} %concatenate.14.refs_2_, bf16[2048,1536]{1,0:T(8,128)(2,1)} %bitcast.82, ...), custom_call_target="tpu_custom_call" | custom-call | tf_op jit(solution)/shard_map/closing_sums/pallas_call | solution.py:989
  698.6 3.3 fusion.17
  703.1 2.7 fusion.14
  706.5 27.3 %finish.1 = (f32[2048,2,768]{2,1,0:T(2,128)}, f32[2048,2048]{1,0:T(8,128)}, f32[512,2048]{1,0:T(8,128)}, f32[2048,2048]{1,0:T(8,128)}) custom-call(bf16[2048,3584]{1,0:T(8,128)(2,1)} %get-tuple-element.54.summed_ref, f32[8,3584]{1,0:T(8,128)} %broadcast_in_dim.75.total_ref, f32[2048,8]{1,0:T(8,128)} %bitcast.87, ...), custom_call_target="tpu_custom_call" | custom-call | tf_op jit(solution)/shard_map/finish/pallas_call | solution.py:1034
  (106 shorter events, 23.6 us)
Async XLA Ops:
  7.2 6.6 copy-start
  7.2 210.8 %all-gather.4.cloned.1.call-start = ((), (), s32[]{:S(2)}) async-start(), calls=%async_computation.2 | async-start | bytes 1310720 | tf_op jit(solution)/shard_map/all_gather | solution.py:1114
  9.0 6.6 copy-start.5
  11.1 8.6 %copy-start.11 = (f32[512]{0:T(512)}, f32[512]{0:T(512)S(1)}, u32[]{:S(2)}) copy-start(f32[512]{0:T(512)S(1)} %broadcast_multiply_fusion.2) | copy-start | bytes 6148
  13.7 6.0 copy-start.13
  15.6 10.1 %copy-start.15 = (f32[2048]{0:T(1024)S(1)}, f32[2048]{0:T(1024)}, u32[]{:S(2)}) copy-start(f32[2048]{0:T(1024)} %param.18) | copy-start | bytes 24580
  15.6 10.1 %copy-start.16 = (f32[2048]{0:T(1024)S(1)}, f32[2048]{0:T(1024)}, u32[]{:S(2)}) copy-start(f32[2048]{0:T(1024)} %param.19) | copy-start | bytes 24580
  15.6 10.1 %copy-start.17 = (f32[2048]{0:T(1024)S(1)}, f32[2048]{0:T(1024)}, u32[]{:S(2)}) copy-start(f32[2048]{0:T(1024)} %param.20) | copy-start | bytes 24580
  15.6 10.1 %copy-start.18 = (f32[2048]{0:T(1024)S(1)}, f32[2048]{0:T(1024)}, u32[]{:S(2)}) copy-start(f32[2048]{0:T(1024)} %param.21) | copy-start | bytes 24580
  189.8 193.1 %all-gather.6.cloned.1.call-start = ((), (), s32[]{:S(2)}) async-start(), calls=%async_computation.3 | async-start | bytes 9437184 | tf_op jit(solution)/shard_map/all_gather | solution.py:1115
  190.7 23.2 %copy-start.24 = (s32[4]{0:T(128)}, s32[4]{0:T(128)S(1)}, u32[]{:S(2)}) copy-start(s32[4]{0:T(128)S(1)} %slice.50) | copy-start | bytes 52
  218.0 264.1 %reduce-scatter.2.cloned.1.call-start = ((), (), s32[]{:S(2)}) async-start(), calls=%async_computation.4 | async-start | bytes 11796480 | tf_op jit(solution)/shard_map/reduce_scatter | solution.py:1139
  383.0 5.8 copy-start.25
  383.0 44.6 %collective-permute-start = (bf16[512,2048]{1,0:T(8,128)(2,1)}, bf16[512,2048]{1,0:T(8,128)(2,1)S(1)}, u32[]{:S(2)}, u32[]{:S(2)}) collective-permute-start(bf16[512,2048]{1,0:T(8,128)(2,1)} %get-tuple-element.45), channel_id=1, source_target_pairs={{0,1},{1,2},{2,3},{4,5},{5,6},{6,7},{8,9},{9,10},{10,11},{12,13},{... | collective-permute-start | bytes 6291464 | tf_op jit(solution)/shard_map/ppermute | solution.py:1062
  384.5 47.4 %collective-permute-start.1 = (bf16[512,2048]{1,0:T(8,128)(2,1)}, bf16[512,2048]{1,0:T(8,128)(2,1)}, u32[]{:S(2)}, u32[]{:S(2)}) collective-permute-start(bf16[512,2048]{1,0:T(8,128)(2,1)} %get-tuple-element.46), channel_id=1, source_target_pairs={{1,0},{2,1},{3,2},{5,4},{6,5},{7,6},{9,8},{10,9},{11,10},{13,12},{... | collective-permute-start | bytes 6291464 | tf_op jit(solution)/shard_map/ppermute | solution.py:1063
  431.9 50.1 %all-to-all-start = ((bf16[4,512,512]{2,1,0:T(8,128)(2,1)}), bf16[4,512,512]{2,1,0:T(8,128)(2,1)S(1)}, u32[]{:S(2)}, u32[]{:S(2)}) async-start(bf16[4,512,512]{2,1,0:T(8,128)(2,1)} %bitcast.83), calls=%async_computation | async-start | bytes 4194304 | tf_op jit(solution)/shard_map/all_to_all | solution.py:1132
  435.5 270.3 %all-gather.8.cloned.1.call-start = ((), (), s32[]{:S(2)}) async-start(), calls=%async_computation.5 | async-start | bytes 11796480 | tf_op jit(solution)/shard_map/all_gather | solution.py:1142
  488.7 6.5 copy-start.1
  488.7 6.5 copy-start.22
  488.7 6.5 copy-start.23
  510.3 188.3 %copy-start.12 = (f32[512]{0:T(512)S(1)}, f32[512]{0:T(512)}, u32[]{:S(2)}) copy-start(f32[512]{0:T(512)} %copy-done.11) | copy-start | bytes 6148
  510.3 188.3 %copy-start.14 = (f32[512]{0:T(512)S(1)}, f32[512]{0:T(512)}, u32[]{:S(2)}) copy-start(f32[512]{0:T(512)} %copy-done.13) | copy-start | bytes 6148
  697.1 8.7 %copy-start.20 = (f32[1,2048]{1,0:T(1,128)}, f32[1,2048]{1,0:T(1,128)S(1)}, u32[]{:S(2)}) copy-start(f32[1,2048]{1,0:T(1,128)S(1)} %get-tuple-element.67) | copy-start | bytes 24580
  697.1 36.6 %copy-start.19 = (f32[1,2048]{1,0:T(1,128)}, f32[1,2048]{1,0:T(1,128)S(1)}, u32[]{:S(2)}) copy-start(f32[1,2048]{1,0:T(1,128)S(1)} %get-tuple-element.66) | copy-start | bytes 24580
  (9 other events, 26.8 us)
Sparse Core Ops, SparseCore 0:
  190.0 27.9 all-gather.3
  219.8 53.8 all-gather.5
  383.1 80.6 reduce-scatter.1
  483.5 76.9 all-gather.7

commit v6 on v5

--- a/solution.py
+++ b/solution.py
@@ -10,7 +10,6 @@
 
 HD = 256
 ROT = 64
-KBLOCK = 256
 NORM_EPS = 1e-05
 NEG_FILL = -1000000000.0
 VMEM_LIMIT = 56 * 1024 * 1024
@@ -552,15 +551,19 @@
     )(x_rows, back, flat_in, up_weight, earlier)
 
 
+def key_block(t):
+    return min(512, t)
+
+
 def allowed(j, i, t, start):
-    key = j * KBLOCK + lax.broadcasted_iota(jnp.int32, (KBLOCK, t), 0)
+    key = j * key_block(t) + lax.broadcasted_iota(jnp.int32, (key_block(t), t), 0)
     query = i * t + lax.broadcasted_iota(jnp.int32, (1, t), 1)
     return (key >= start) & (key <= query)
 
 
 def attend_kernel(t, heads, low_ref, qkv_ref, start_ref, held_ref, out_ref, log_ref, vt_ref, acc_ref):
     blocks = qkv_ref.shape[0] // t
-    per = t // KBLOCK
+    per = t // key_block(t)
 
     for h in range(heads):
         for c in range(blocks):
@@ -573,26 +576,26 @@
         start = start_ref[:, where]
         acc_ref[...] = jnp.zeros_like(acc_ref)
 
-        def key_block(j, carried):
-            place = pl.multiple_of(j * KBLOCK, KBLOCK)
+        def keys_step(j, carried):
+            place = pl.multiple_of(j * key_block(t), key_block(t))
             mask = allowed(j, i, t, start)
             new = []
             for h in range(heads):
                 top, total = carried[h]
                 query = qkv_ref[pl.ds(row, t), 3 * h * HD : (3 * h + 1) * HD]
-                key = qkv_ref[pl.ds(place, KBLOCK), (3 * h + 1) * HD : (3 * h + 2) * HD]
+                key = qkv_ref[pl.ds(place, key_block(t)), (3 * h + 1) * HD : (3 * h + 2) * HD]
                 s = jnp.where(mask, dot(key, query, NT), NEG_FILL)
                 higher = jnp.maximum(top, jnp.max(s, axis=0, keepdims=True))
                 p = jnp.exp(s - higher)
                 shrink = jnp.exp(top - higher)
                 total = total * shrink + jnp.sum(p, axis=0, keepdims=True)
-                vt = vt_ref[h, :, pl.ds(place, KBLOCK)]
+                vt = vt_ref[h, :, pl.ds(place, key_block(t))]
                 acc_ref[h] = acc_ref[h] * shrink + dot(vt, p.astype(BF16))
                 new.append((higher, total))
             return tuple(new)
 
         first = (jnp.full((1, t), 2 * NEG_FILL, F32), jnp.zeros((1, t), F32))
-        carried = lax.fori_loop(low_ref[i], (i + 1) * per, key_block, (first,) * heads)
+        carried = lax.fori_loop(low_ref[i], (i + 1) * per, keys_step, (first,) * heads)
         for h in range(heads):
             top, total = carried[h]
             log_ref[h : h + 1, where] = top + jnp.log(total)
@@ -633,7 +636,7 @@
 ):
     rows = qkv_ref.shape[0]
     blocks = rows // t
-    per = t // KBLOCK
+    per = t // key_block(t)
     query_grad[...] = jnp.zeros_like(query_grad)
 
     def prepare(i, unused):
@@ -650,8 +653,8 @@
         cosine, sine = cos_ref[pl.ds(place, count), :], sin_ref[pl.ds(place, count), :]
         return turn(grad[:, :128], cosine, -sine)
 
-    def key_block(j, unused):
-        place = pl.multiple_of(j * KBLOCK, KBLOCK)
+    def keys_step(j, unused):
+        place = pl.multiple_of(j * key_block(t), key_block(t))
         key_grad[...] = jnp.zeros_like(key_grad)
         value_grad[...] = jnp.zeros_like(value_grad)
 
@@ -661,8 +664,8 @@
             mask = allowed(j, i, t, start_ref[:, where])
             for h in range(heads):
                 query = qkv_ref[pl.ds(row, t), 3 * h * HD : (3 * h + 1) * HD]
-                key = qkv_ref[pl.ds(place, KBLOCK), (3 * h + 1) * HD : (3 * h + 2) * HD]
-                value = qkv_ref[pl.ds(place, KBLOCK), (3 * h + 2) * HD : (3 * h + 3) * HD]
+                key = qkv_ref[pl.ds(place, key_block(t)), (3 * h + 1) * HD : (3 * h + 2) * HD]
+                value = qkv_ref[pl.ds(place, key_block(t)), (3 * h + 2) * HD : (3 * h + 3) * HD]
                 grad = grad_ref[pl.ds(row, t), h * HD : (h + 1) * HD]
                 s = dot(key, query, NT) - log_ref[h : h + 1, where]
                 p = jnp.exp(jnp.where(mask, s, NEG_FILL))
@@ -677,12 +680,12 @@
         for h in range(heads):
             base = 3 * h * HD
             grad = key_grad[h]
-            proj_ref[pl.ds(place, KBLOCK), base + HD : base + HD + 128] = turned_back(grad, place, KBLOCK).astype(BF16)
-            proj_ref[pl.ds(place, KBLOCK), base + HD + 128 : base + 2 * HD] = grad[:, 128:].astype(BF16)
-            proj_ref[pl.ds(place, KBLOCK), base + 2 * HD : base + 3 * HD] = value_grad[h].astype(BF16)
+            proj_ref[pl.ds(place, key_block(t)), base + HD : base + HD + 128] = turned_back(grad, place, key_block(t)).astype(BF16)
+            proj_ref[pl.ds(place, key_block(t)), base + HD + 128 : base + 2 * HD] = grad[:, 128:].astype(BF16)
+            proj_ref[pl.ds(place, key_block(t)), base + 2 * HD : base + 3 * HD] = value_grad[h].astype(BF16)
         return unused
 
-    lax.fori_loop(0, rows // KBLOCK, key_block, 0)
+    lax.fori_loop(0, rows // key_block(t), keys_step, 0)
 
     def finish(c, unused):
         place = pl.multiple_of(c * t, t)
@@ -712,8 +715,8 @@
         scratch_shapes=[
             pltpu.VMEM((rows, heads * HD), F32),
             pltpu.VMEM((heads, rows), F32),
-            pltpu.VMEM((heads, KBLOCK, HD), F32),
-            pltpu.VMEM((heads, KBLOCK, HD), F32),
+            pltpu.VMEM((heads, key_block(t), HD), F32),
+            pltpu.VMEM((heads, key_block(t), HD), F32),
         ],
         input_output_aliases={8: 0},
         compiler_params=params(),
@@ -1095,8 +1098,8 @@
 
     starts = document_starts(seq_lengths[0], length)
     first_of_block = starts[::t]
-    low = first_of_block // KBLOCK
-    last_key = (jnp.arange(length // KBLOCK, dtype=jnp.int32) + 1) * KBLOCK - 1
+    low = first_of_block // key_block(t)
+    last_key = (jnp.arange(length // key_block(t), dtype=jnp.int32) + 1) * key_block(t) - 1
     high = jnp.sum((first_of_block[None, :] <= last_key[:, None]).astype(jnp.int32), axis=1)
     offsets = jnp.arange(length, dtype=jnp.int32) - starts
     inverse = 10000.0 ** (-jnp.arange(0, ROT, 2).astype(F32) / ROT)

time: 749 us -> 749 us (level)
  no operation moved by 1% of the time
where the time goes in v6:
time: 749 us; the launch traced here: 741 us
  Pallas kernels  638 us (85%)
  local copies, waits for them, and re-layouts  29 us (4%)
  other arithmetic  25.1 us (3%)
  waiting for transfers between devices  15.4 us (2%)
  between operations  14.3 us (2%)
  matrix products  11.8 us (2%)
    pallas_call x1, Pallas kernels, closing_sums(): pl.pallas_call(functools.partial(closing_kernel, n, groups), in_specs=[an...  185 us
    pallas_call x1, Pallas kernels, middle(): pl.pallas_call(functools.partial(middle_kernel, n, in_width), in_specs=[a...  165 us
    pallas_call x1, Pallas kernels, opening(): pl.pallas_call(functools.partial(opening_kernel, n, heads), in_specs=[any...  161 us
    pallas_call x1, Pallas kernels, cross_products(): pl.pallas_call(functools.partial(cross_kernel, heads_tile), grid=(d // ti...  46 us
    pallas_call x1, Pallas kernels, attend_back(): pl.pallas_call(functools.partial(attend_back_kernel, t, heads), grid=(1,)...  32.7 us
    pallas_call x1, Pallas kernels, finish(): pl.pallas_call(functools.partial(finish_kernel, heads), grid=(d // block,...  27.3 us
    pallas_call x1, Pallas kernels, attend(): pl.pallas_call(functools.partial(attend_kernel, t, heads), grid=(1,), in_...  21 us
  transfers between devices with their start and end apart: 7, of which 3 were waited for; matrix products, arithmetic and copies ran while one was open for 6% of the time, Pallas kernels for 61%

profile of v6, /device:TPU:0, one launch (start us, length us, event | category | flops | bytes accessed | tf_op | source)
XLA Modules:
  0.0 741.1 jit_solution(15048942622222998518)
XLA Ops:
  9.0 2.1 convert_reduce_fusion.1
  11.1 2.6 fusion.10
  13.7 1.9 fusion.6.refs_0_
  15.7 4.1 copy.71
  20.3 3.7 fusion.16
  26.5 1.9 maximum_maximum_fusion
  28.4 161.4 %opening.1 = (bf16[2048,2048]{1,0:T(8,128)(2,1)}, bf16[2048,1536]{1,0:T(8,128)(2,1)}, bf16[2048,2560]{1,0:T(8,128)(2,1)}, bf16[2048,2048]{1,0:T(8,128)(2,1)}, bf16[2048,2048]{1,0:T(8,128)(2,1)}) custom-call(bf16[512,2048]{1,0:T(8,128)(2,1)} %fusion.6.refs_0_, bf16[2048,1536]{1,0:T(8,128)(2,1)} %bitcast.80, bf16[2048,2048]{1,0:T(8,128)(2,1)} %refs_4_.3, ...), custom_call_target="tpu_custom_call" | custom-call | flops 755914244096 | bytes 209715200 | tf_op jit(solution)/shard_map/opening/pallas_call | solution.py:240
  191.4 21.0 %attend.1 = (bf16[2048,2560]{1,0:T(8,128)(2,1)}, f32[2,2048]{1,0:T(2,128)}) custom-call(s32[4]{0:T(128)} %and_select_fusion.low_ref, bf16[2048,1536]{1,0:T(8,128)(2,1)} %get-tuple-element.37.qkv_ref, s32[1,2048]{1,0:T(1,128)} %bitcast.89, bf16[2048,2560]{1,0:T(8,128)(2,1)} %get-tuple-element.38.held_ref), custom_call_target="tpu_custom_call", output_to_operand_aliasing={{0}: (3, {})} | custom-call | flops 4294967296 | bytes 6291456 | tf_op jit(solution)/shard_map/attend/pallas_call | solution.py:612
  212.4 5.6 all-gather.4.cloned.1.call-done.refs_6_
  218.0 164.9 %middle.1 = (bf16[2048,2048]{1,0:T(8,128)(2,1)}, bf16[2048,512]{1,0:T(8,128)(2,1)}, bf16[2048,3584]{1,0:T(8,128)(2,1)}, bf16[2560,2048]{1,0:T(8,128)(2,1)}, bf16...) custom-call(bf16[512,2048]{1,0:T(8,128)(2,1)} %bitcast.85, bf16[2048,2048]{1,0:T(8,128)(2,1)} %get-tuple-element.40.refs_1_, ...), custom_call_target="tpu_custom_call" | custom-call | flops 687194767360 | bytes 209715200 | tf_op jit(solution)/shard_map/middle/pallas_call | solution.py:447
  385.8 3.0 slice.51.refs_0_
  389.5 32.7 %attend_back.1.refs_1_.back_ref.refs_0_ = bf16[2048,3584]{1,0:T(8,128)(2,1)} custom-call(s32[4]{0:T(128)} %convert_reduce_fusion.2.high_ref, bf16[2048,1536]{1,0:T(8,128)(2,1)} %get-tuple-element.37.qkv_ref, bf16[2048,512]{1,0:T(8,128)(2,1)} %get-tuple-element.42.grad_ref, ...), custom_call_target="tpu_custom_call", output_to_operand_aliasing={{}: (8, {})} | custom-call | flops 10737418240 | bytes 12582912 | tf_op jit(solution)/shard_map/attend_back/pallas_call | solution.py:707
  422.2 5.5 collective-permute-done.refs_2_
  427.6 4.2 collective-permute-done.1.refs_3_
  431.9 3.6 all-to-all-start
  436.0 46.0 %cross.1 = (bf16[2048,3584]{1,0:T(8,128)(2,1)}, f32[2048,128]{1,0:T(8,128)}, f32[8,3584]{1,0:T(8,128)}) custom-call(bf16[2048,2048]{1,0:T(8,128)(2,1)} %get-tuple-element.47.x_ref, bf16[2048,3584]{1,0:T(8,128)(2,1)} %attend_back.1.refs_1_.back_ref.refs_0_, bf16[2048,1536]{1,0:T(8,128)(2,1)} %bitcast.81, bf16[2048,2048]{1,0:T(8,128)(2,1)} %refs_4_.3, ...), custom_call_target="tpu_custom_call" | custom-call | flops 30064771072 | bytes 52428800 | tf_op jit(solution)/shard_map/cross/pallas_call | solution.py:525
  484.7 2.0 convert_reduce_fusion
  488.7 4.3 copy.66
  493.1 2.1 copy.67
  495.7 11.8 %multiply_reduce_fusion = (f32[]{:T(128)}, bf16[1,512,2048]{2,1,0:T(8,128)(2,1)}, f32[]{:T(128)}) fusion(bf16[512,2048]{1,0:T(8,128)(2,1)} %collective-permute-done.1.refs_3_, bf16[512,2048]{1,0:T(8,128)(2,1)S(1)} %copy-done.8, f32[2048]{0:T(1024)S(1)} %copy-done.22, bf16[2048,2048]{1,0:T(8,128)(2,1)} %get-tuple-element.40.refs_1_, s32[]{:T(128)S(6)} %select_n.18, ...), kind=kOutput, calls=%fused_computation.18 | convolution fusion | flops 4310695936 | bytes 20987916 | tf_op jit(solution)/shard_map/dot_general | solution.py:25
  510.3 185.1 %closing_sums.1 = (f32[512,2048]{1,0:T(8,128)}, bf16[2048,3584]{1,0:T(8,128)(2,1)}, f32[16,2048]{1,0:T(8,128)}) custom-call(bf16[2048,3584]{1,0:T(8,128)(2,1)} %attend_back.1.refs_1_.back_ref.refs_0_, bf16[2048,3584]{1,0:T(8,128)(2,1)} %get-tuple-element.48.refs_1_, f32[16,2048]{1,0:T(8,128)} %concatenate.14.refs_2_, bf16[2048,1536]{1,0:T(8,128)(2,1)} %bitcast.82, ...), custom_call_target="tpu_custom_call" | custom-call | tf_op jit(solution)/shard_map/closing_sums/pallas_call | solution.py:992
  698.6 3.3 fusion.17
  703.1 2.7 fusion.14
  706.5 27.3 %finish.1 = (f32[2048,2,768]{2,1,0:T(2,128)}, f32[2048,2048]{1,0:T(8,128)}, f32[512,2048]{1,0:T(8,128)}, f32[2048,2048]{1,0:T(8,128)}) custom-call(bf16[2048,3584]{1,0:T(8,128)(2,1)} %get-tuple-element.54.summed_ref, f32[8,3584]{1,0:T(8,128)} %broadcast_in_dim.75.total_ref, f32[2048,8]{1,0:T(8,128)} %bitcast.87, ...), custom_call_target="tpu_custom_call" | custom-call | tf_op jit(solution)/shard_map/finish/pallas_call | solution.py:1037
  (106 shorter events, 23.9 us)
Async XLA Ops:
  7.2 6.6 copy-start
  7.2 210.8 %all-gather.4.cloned.1.call-start = ((), (), s32[]{:S(2)}) async-start(), calls=%async_computation.2 | async-start | bytes 1310720 | tf_op jit(solution)/shard_map/all_gather | solution.py:1117
  9.0 6.6 copy-start.5
  11.1 8.6 %copy-start.11 = (f32[512]{0:T(512)}, f32[512]{0:T(512)S(1)}, u32[]{:S(2)}) copy-start(f32[512]{0:T(512)S(1)} %broadcast_multiply_fusion.2) | copy-start | bytes 6148
  13.7 6.0 copy-start.13
  15.6 10.1 %copy-start.15 = (f32[2048]{0:T(1024)S(1)}, f32[2048]{0:T(1024)}, u32[]{:S(2)}) copy-start(f32[2048]{0:T(1024)} %param.18) | copy-start | bytes 24580
  15.6 10.1 %copy-start.16 = (f32[2048]{0:T(1024)S(1)}, f32[2048]{0:T(1024)}, u32[]{:S(2)}) copy-start(f32[2048]{0:T(1024)} %param.19) | copy-start | bytes 24580
  15.6 10.1 %copy-start.17 = (f32[2048]{0:T(1024)S(1)}, f32[2048]{0:T(1024)}, u32[]{:S(2)}) copy-start(f32[2048]{0:T(1024)} %param.20) | copy-start | bytes 24580
  15.6 10.1 %copy-start.18 = (f32[2048]{0:T(1024)S(1)}, f32[2048]{0:T(1024)}, u32[]{:S(2)}) copy-start(f32[2048]{0:T(1024)} %param.21) | copy-start | bytes 24580
  189.8 193.1 %all-gather.6.cloned.1.call-start = ((), (), s32[]{:S(2)}) async-start(), calls=%async_computation.3 | async-start | bytes 9437184 | tf_op jit(solution)/shard_map/all_gather | solution.py:1118
  190.9 21.5 %copy-start.24 = (s32[4]{0:T(128)}, s32[4]{0:T(128)S(1)}, u32[]{:S(2)}) copy-start(s32[4]{0:T(128)S(1)} %slice.50) | copy-start | bytes 52
  218.0 264.1 %reduce-scatter.2.cloned.1.call-start = ((), (), s32[]{:S(2)}) async-start(), calls=%async_computation.4 | async-start | bytes 11796480 | tf_op jit(solution)/shard_map/reduce_scatter | solution.py:1142
  383.0 5.8 copy-start.25
  383.0 44.6 %collective-permute-start = (bf16[512,2048]{1,0:T(8,128)(2,1)}, bf16[512,2048]{1,0:T(8,128)(2,1)S(1)}, u32[]{:S(2)}, u32[]{:S(2)}) collective-permute-start(bf16[512,2048]{1,0:T(8,128)(2,1)} %get-tuple-element.45), channel_id=1, source_target_pairs={{0,1},{1,2},{2,3},{4,5},{5,6},{6,7},{8,9},{9,10},{10,11},{12,13},{... | collective-permute-start | bytes 6291464 | tf_op jit(solution)/shard_map/ppermute | solution.py:1065
  384.5 47.4 %collective-permute-start.1 = (bf16[512,2048]{1,0:T(8,128)(2,1)}, bf16[512,2048]{1,0:T(8,128)(2,1)}, u32[]{:S(2)}, u32[]{:S(2)}) collective-permute-start(bf16[512,2048]{1,0:T(8,128)(2,1)} %get-tuple-element.46), channel_id=1, source_target_pairs={{1,0},{2,1},{3,2},{5,4},{6,5},{7,6},{9,8},{10,9},{11,10},{13,12},{... | collective-permute-start | bytes 6291464 | tf_op jit(solution)/shard_map/ppermute | solution.py:1066
  431.9 50.1 %all-to-all-start = ((bf16[4,512,512]{2,1,0:T(8,128)(2,1)}), bf16[4,512,512]{2,1,0:T(8,128)(2,1)S(1)}, u32[]{:S(2)}, u32[]{:S(2)}) async-start(bf16[4,512,512]{2,1,0:T(8,128)(2,1)} %bitcast.83), calls=%async_computation | async-start | bytes 4194304 | tf_op jit(solution)/shard_map/all_to_all | solution.py:1135
  435.5 270.3 %all-gather.8.cloned.1.call-start = ((), (), s32[]{:S(2)}) async-start(), calls=%async_computation.5 | async-start | bytes 11796480 | tf_op jit(solution)/shard_map/all_gather | solution.py:1145
  488.7 6.5 copy-start.1
  488.7 6.5 copy-start.22
  488.7 6.5 copy-start.23
  510.3 188.3 %copy-start.12 = (f32[512]{0:T(512)S(1)}, f32[512]{0:T(512)}, u32[]{:S(2)}) copy-start(f32[512]{0:T(512)} %copy-done.11) | copy-start | bytes 6148
  510.3 188.3 %copy-start.14 = (f32[512]{0:T(512)S(1)}, f32[512]{0:T(512)}, u32[]{:S(2)}) copy-start(f32[512]{0:T(512)} %copy-done.13) | copy-start | bytes 6148
  697.1 8.7 %copy-start.20 = (f32[1,2048]{1,0:T(1,128)}, f32[1,2048]{1,0:T(1,128)S(1)}, u32[]{:S(2)}) copy-start(f32[1,2048]{1,0:T(1,128)S(1)} %get-tuple-element.67) | copy-start | bytes 24580
  697.1 36.6 %copy-start.19 = (f32[1,2048]{1,0:T(1,128)}, f32[1,2048]{1,0:T(1,128)S(1)}, u32[]{:S(2)}) copy-start(f32[1,2048]{1,0:T(1,128)S(1)} %get-tuple-element.66) | copy-start | bytes 24580
  (9 other events, 26.8 us)
Sparse Core Ops, SparseCore 0:
  190.0 27.9 all-gather.3
  219.8 53.8 all-gather.5
  383.1 80.5 reduce-scatter.1
  483.5 76.9 all-gather.7
